TPU v7x, 32 devices: a whole 2x2x4 slice. The times are simulated.
32 devices in a mesh: expert: 4 (over y, core), tensor: 2 (over x), dp: 4 (over z).
Axes of the slice: x: 2, y: 2, z: 4, core: 2. Of those that a mesh axis runs over, the one named last changes fastest.
Arguments:
- tokens: bfloat16 [2048, 4096], P(('expert', 'dp'), 'tensor'), may hold values from -6 to 6
- routes: int32 [2048, 2], P(('expert', 'dp')), may hold values from 0 to 3, all different within a row; in each aligned block of 128 rows (0 to 127, 128 to 255, ...) at most 80 rows name the same one
- gate_prob: float32 [2048, 2], P(('expert', 'dp')), may hold values from 0.05 to 1
- token_count: int32 [16], P(('expert', 'dp')), may hold values from 1 to 128, 1536 in all
- gate_weight: bfloat16 [4, 4096, 1536], P(None, ('expert', 'dp'), 'tensor'), may hold values from -0.09375 to 0.09375
- up_weight: bfloat16 [4, 4096, 1536], P(None, ('expert', 'dp'), 'tensor'), may hold values from -0.09375 to 0.09375
- down_weight: bfloat16 [4, 4096, 1536], P(None, ('expert', 'dp'), 'tensor'), may hold values from -0.15625 to 0.15625
Outputs:
- mixed: bfloat16 [2048, 4096], P(('expert', 'dp'), 'tensor')
Inputs may be any that keep to these rules, and one draw needn't show every extreme that they name: `routes`: each row names 2 different experts; among the rows of one group (aligned blocks of 128 rows) no expert is named by more than 80 rows. `token_count`: rows of a group at or past its count are padding.
All inputs are finite; a program needn't handle non-finite values.
Results may differ from a plain program's by a relative error of at most 0.012.
Values may be sent and summed in bfloat16 or wider, within the bound.
No kernel may reach another device: no remote copies, remote signals or barrier semaphores. Data moves between devices by JAX's collectives and lax.ppermute only.
A program may use at most 64 MiB of HBM per device.

v0:
```python
import jax
import jax.numpy as jnp
from jax import lax
from jax.sharding import PartitionSpec as P


def shards(tokens, routes, gate_prob, token_count, gate_weight, up_weight, down_weight):
    experts = gate_weight.shape[0]
    stored_rows = gate_weight.shape[1]
    hidden_share = gate_weight.shape[2]
    tok_rows, top_slots = routes.shape
    capacity = min(tok_rows, tok_rows * top_slots * 5 // (4 * experts))
    expert_count = lax.axis_size("expert")
    replica_count = lax.axis_size("dp")
    model_width = stored_rows * expert_count * replica_count
    arrived_rows = (
        lax.all_to_all(gate_weight, "expert", split_axis=0, concat_axis=1, tiled=True),
        lax.all_to_all(up_weight, "expert", split_axis=0, concat_axis=1, tiled=True),
        lax.all_to_all(down_weight, "expert", split_axis=0, concat_axis=1, tiled=True),
    )

    def split_blocks(weight):
        return weight.reshape(1, expert_count, 1, stored_rows, hidden_share)

    assembled = (
        lax.all_gather(split_blocks(arrived_rows[0]), "dp", axis=2, tiled=True),
        lax.all_gather(split_blocks(arrived_rows[1]), "dp", axis=2, tiled=True),
        lax.all_gather(split_blocks(arrived_rows[2]), "dp", axis=2, tiled=True),
    )
    w_gate = assembled[0].reshape(model_width, hidden_share)
    w_up = assembled[1].reshape(model_width, hidden_share)
    w_down = assembled[2].reshape(model_width, hidden_share)
    positions = jnp.arange(tok_rows)
    live_rows = positions < token_count[0]
    live_pair = jnp.repeat(live_rows, top_slots)
    route_flat = routes.reshape(-1)
    expert_ids = jnp.arange(experts)
    one_hot = ((route_flat[:, None] == expert_ids[None, :]) & live_pair[:, None]).astype(jnp.int32)
    pair_rank = jnp.sum((jnp.cumsum(one_hot, axis=0) - one_hot) * one_hot, axis=1)
    slot_of_pair = jnp.where(live_pair, route_flat * capacity + pair_rank, -1)
    slot_ids = jnp.arange(experts * capacity)
    assign_pair = (slot_ids[:, None] == slot_of_pair[None, :]).astype(jnp.bfloat16)
    assign_slots = assign_pair.reshape(experts * capacity, tok_rows, top_slots)
    assign_bf16 = jnp.sum(assign_slots.astype(jnp.float32), axis=2).astype(jnp.bfloat16)
    outgoing = jnp.dot(assign_bf16, tokens, preferred_element_type=jnp.float32).astype(jnp.bfloat16)
    incoming = lax.all_to_all(
        outgoing.reshape(experts, capacity, tokens.shape[1]),
        "expert",
        split_axis=0,
        concat_axis=0,
        tiled=True,
    )
    feature_piece = lax.all_gather(incoming, "tensor", axis=2, tiled=True)
    piece_width = feature_piece.shape[2]
    flat_piece = feature_piece.reshape(-1, piece_width)
    gate_proj = jnp.dot(flat_piece, w_gate, preferred_element_type=jnp.float32)
    up_proj = jnp.dot(flat_piece, w_up, preferred_element_type=jnp.float32)
    hidden = (jax.nn.silu(gate_proj) * up_proj).astype(jnp.bfloat16)
    partial_value = lax.dot_general(
        hidden, w_down, (((1,), (1,)), ((), ())), preferred_element_type=jnp.float32
    )
    expert_out = lax.psum_scatter(
        partial_value.astype(jnp.bfloat16), "tensor", scatter_dimension=1, tiled=True
    )
    returned = lax.all_to_all(
        expert_out.reshape(experts, capacity, -1), "expert", split_axis=0, concat_axis=0, tiled=True
    )
    returned_rows = returned.reshape(experts * capacity, -1)
    picked = jnp.einsum(
        "cts,cd->std", assign_slots, returned_rows, preferred_element_type=jnp.float32
    )
    slot_weights = gate_prob.T
    mixed = jnp.sum(slot_weights[:, :, None] * picked, axis=0)
    return mixed.astype(jnp.bfloat16)


def solution(mesh):
    in_specs = (
        P(("expert", "dp"), "tensor"),
        P(("expert", "dp"), None),
        P(("expert", "dp"), None),
        P(("expert", "dp")),
        P(None, ("expert", "dp"), "tensor"),
        P(None, ("expert", "dp"), "tensor"),
        P(None, ("expert", "dp"), "tensor"),
    )
    out_specs = P(("expert", "dp"), "tensor")
    return jax.shard_map(shards, mesh=mesh, in_specs=in_specs, out_specs=out_specs, check_vma=False)
```

profile of v0, /device:TPU:0, one launch (start us, length us, event | category | flops | bytes accessed | tf_op | source)
XLA Modules:
  0.0 497.5 jit_solution(904599229625638113)
XLA Ops:
  6.5 0.8 copy.35
  7.4 0.1 eq.66
  7.5 0.1 eq.62
  8.4 0.1 broadcast_in_dim.17
  8.6 1.2 reduce-window.6
  10.3 0.1 and.16
  10.5 0.1 reduce_sum.33
  10.7 0.7 add_select_fusion
  11.5 0.5 convolution_convert_fusion.1
  12.0 21.4 %all_to_all.37 = bf16[4,80,2048]{2,1,0:T(8,128)(2,1)} all-to-all(bf16[4,80,2048]{2,1,0:T(8,128)(2,1)S(1)} %bitcast.49), channel_id=1, replica_groups=mesh['expert'=4,'tensor'=2,'dp'=4] {'expert'}, dimensions={0} | all-to-all | bytes 2621440 | tf_op jit(solution)/shard_map/all_to_all | solution.py:46
  33.5 23.3 %all_to_all.38 = bf16[4,256,768]{2,1,0:T(8,128)(2,1)} all-to-all(bf16[4,256,768]{2,1,0:T(8,128)(2,1)S(1)} %copy-done.1), channel_id=1, replica_groups=mesh['expert'=4,'tensor'=2,'dp'=4] {'expert'}, dimensions={0} | all-to-all | bytes 3145728 | tf_op jit(solution)/shard_map/all_to_all | solution.py:17
  56.8 1.3 copy-done.2
  58.1 23.3 %all_to_all.39 = bf16[4,256,768]{2,1,0:T(8,128)(2,1)} all-to-all(bf16[4,256,768]{2,1,0:T(8,128)(2,1)S(1)} %copy-done.2), channel_id=1, replica_groups=mesh['expert'=4,'tensor'=2,'dp'=4] {'expert'}, dimensions={0} | all-to-all | bytes 3145728 | tf_op jit(solution)/shard_map/all_to_all | solution.py:18
  81.5 1.5 copy-done.3
  83.0 23.3 %all_to_all.40 = bf16[4,256,768]{2,1,0:T(8,128)(2,1)} all-to-all(bf16[4,256,768]{2,1,0:T(8,128)(2,1)S(1)} %copy-done.3), channel_id=1, replica_groups=mesh['expert'=4,'tensor'=2,'dp'=4] {'expert'}, dimensions={0} | all-to-all | bytes 3145728 | tf_op jit(solution)/shard_map/all_to_all | solution.py:19
  106.4 83.9 %all-gather.10.cloned.1.call-done = bf16[4,1024,768]{2,1,0:T(8,128)(2,1)} async-done(((bf16[4,256,768]{2,1,0:T(8,128)(2,1)}), bf16[4,1024,768]{2,1,0:T(8,128)(2,1)}) %all-gather.10.cloned.1.call-update) | async-done | bytes 6291472 | tf_op jit(solution)/shard_map/all_gather | solution.py:26
  190.3 7.0 %fusion.14 = f32[320,768]{1,0:T(8,128)} fusion(bf16[320,4096]{1,0:T(8,128)(2,1)} %bitcast.56, bf16[4096,768]{1,0:T(8,128)(2,1)} %bitcast.53), kind=kOutput, calls=%fused_computation.26 | convolution fusion | flops 2013265920 | bytes 9895936 | tf_op jit(solution)/shard_map/dot_general | solution.py:56
  197.3 108.2 %all-gather.12.cloned.1.call-done = bf16[4,1024,768]{2,1,0:T(8,128)(2,1)} async-done(((bf16[4,256,768]{2,1,0:T(8,128)(2,1)}), bf16[4,1024,768]{2,1,0:T(8,128)(2,1)}) %all-gather.12.cloned.1.call-update) | async-done | bytes 6291472 | tf_op jit(solution)/shard_map/all_gather | solution.py:27
  305.4 115.0 %all-gather.14.cloned.1.call-done = bf16[4,1024,768]{2,1,0:T(8,128)(2,1)} async-done(((bf16[4,256,768]{2,1,0:T(8,128)(2,1)}), bf16[4,1024,768]{2,1,0:T(8,128)(2,1)}) %all-gather.14.cloned.1.call-update) | async-done | bytes 6291472 | tf_op jit(solution)/shard_map/all_gather | solution.py:28
  420.4 12.0 %convolution_convert_fusion = bf16[320,4096]{1,0:T(8,128)(2,1)} fusion(bf16[4096,768]{1,0:T(8,128)(2,1)} %bitcast.55, bf16[320,4096]{1,0:T(8,128)(2,1)S(1)} %bitcast.57, bf16[4096,768]{1,0:T(8,128)(2,1)} %bitcast.54, f32[320,768]{1,0:T(8,128)} %fusion.14), kind=kOutput, calls=%fused_computation | convolution fusion | flops 4029317120 | bytes 18808832 | tf_op jit(solution)/shard_map/dot_general | solution.py:59
  432.5 35.9 %reduce-scatter.2.cloned.1.call-done = bf16[320,2048]{1,0:T(8,128)(2,1)} async-done(((bf16[320,4096]{1,0:T(8,128)(2,1)}), bf16[320,2048]{1,0:T(8,128)(2,1)}) %reduce-scatter.2.cloned.1.call-update) | async-done | bytes 1310736 | tf_op jit(solution)/shard_map/reduce_scatter | solution.py:62
  468.4 20.8 %all_to_all.41 = bf16[4,80,2048]{2,1,0:T(8,128)(2,1)S(1)} all-to-all(bf16[4,80,2048]{2,1,0:T(8,128)(2,1)} %bitcast.50), channel_id=1, replica_groups=mesh['expert'=4,'tensor'=2,'dp'=4] {'expert'}, dimensions={0} | all-to-all | bytes 2621440 | tf_op jit(solution)/shard_map/all_to_all | solution.py:65
  489.2 0.8 fusion.1
  489.9 1.0 copy.41
  (35 shorter events, 1.0 us)
Async XLA Ops:
  6.5 4.9 copy-start
  6.5 99.8 %all-gather.8.cloned.1.call-start = ((), (), s32[]{:S(2)}) async-start(), calls=%async_computation.6 | async-start | bytes 3932160 | tf_op jit(solution)/shard_map/all_gather | solution.py:53
  11.5 22.0 %copy-start.1 = (bf16[4,256,768]{2,1,0:T(8,128)(2,1)S(1)}, bf16[4,256,768]{2,1,0:T(8,128)(2,1)}, u32[]{:S(2)}) copy-start(bf16[4,256,768]{2,1,0:T(8,128)(2,1)} %param.11) | copy-start | bytes 4718596
  33.4 156.9 %all-gather.10.cloned.1.call-start = ((), (), s32[]{:S(2)}) async-start(), calls=%async_computation.8 | async-start | bytes 7864320 | tf_op jit(solution)/shard_map/all_gather | solution.py:26
  56.7 1.4 copy-start.2
  56.8 248.7 %all-gather.12.cloned.1.call-start = ((), (), s32[]{:S(2)}) async-start(), calls=%async_computation.9 | async-start | bytes 7864320 | tf_op jit(solution)/shard_map/all_gather | solution.py:27
  81.4 1.6 copy-start.3
  81.4 339.0 %all-gather.14.cloned.1.call-start = ((), (), s32[]{:S(2)}) async-start(), calls=%async_computation.10 | async-start | bytes 7864320 | tf_op jit(solution)/shard_map/all_gather | solution.py:28
  106.3 362.1 %reduce-scatter.2.cloned.1.call-start = ((), (), s32[]{:S(2)}) async-start(), calls=%async_computation.7 | async-start | bytes 3932160 | tf_op jit(solution)/shard_map/reduce_scatter | solution.py:62
  190.3 230.1 %copy-start.4 = (bf16[4,80,4096]{2,1,0:T(8,128)(2,1)S(1)}, bf16[4,80,4096]{2,1,0:T(8,128)(2,1)}, u32[]{:S(2)}) copy-start(bf16[4,80,4096]{2,1,0:T(8,128)(2,1)} %all-gather.8.cloned.1.call-done) | copy-start | bytes 7864324
  432.5 56.7 %copy-start.5 = (f32[128,2]{0,1:T(2,128)S(1)}, f32[128,2]{0,1:T(2,128)}, u32[]{:S(2)}) copy-start(f32[128,2]{0,1:T(2,128)} %param.9) | copy-start | bytes 3076
Sparse Core Ops, SparseCore 0:
  33.5 39.7 all-gather.7
  74.9 115.3 all-gather.9
  191.9 113.5 all-gather.11
  306.9 113.5 all-gather.13
  432.6 35.7 reduce-scatter.1
where the time goes:
time: 498 us; the launch traced here: 497 us
  waiting for transfers between devices  343 us (69%)
  blocking collectives  112 us (22%)
  matrix products  20.2 us (4%)
  between operations  13.9 us (3%)
  local copies, waits for them, and re-layouts  5.94 us (1%)
    all_gather x1, waiting for transfers between devices, shards(): lax.all_gather(split_blocks(arrived_rows[2]), 'dp', axis=2, tiled=True)  115 us
    all_gather x1, waiting for transfers between devices, shards(): lax.all_gather(split_blocks(arrived_rows[1]), 'dp', axis=2, tiled=True)  108 us
    all_gather x1, waiting for transfers between devices, shards(): lax.all_gather(split_blocks(arrived_rows[0]), 'dp', axis=2, tiled=True)  83.9 us
    reduce_scatter x1, waiting for transfers between devices, shards(): lax.psum_scatter(partial_value.astype(jnp.bfloat16), 'tensor', scatter_di...  35.9 us
    all_to_all x1, blocking collectives, shards(): lax.all_to_all(up_weight, 'expert', split_axis=0, concat_axis=1, tiled=True)  23.3 us
    all_to_all x1, blocking collectives, shards(): lax.all_to_all(gate_weight, 'expert', split_axis=0, concat_axis=1, tiled=...  23.3 us
    all_to_all x1, blocking collectives, shards(): lax.all_to_all(down_weight, 'expert', split_axis=0, concat_axis=1, tiled=...  23.3 us
    all_to_all x1, blocking collectives, shards(): lax.all_to_all(outgoing.reshape(experts, capacity, tokens.shape[1]), 'exp...  21.4 us
  transfers between devices with their start and end apart: 5, of which 4 were waited for; matrix products, arithmetic and copies ran while one was open for 1% of the time, Pallas kernels for 0%

commit v1 on v0

v1 whole, which is shorter than its diff:
```python
import functools

import jax
import jax.numpy as jnp
from jax import lax
from jax.experimental import pallas as pl
from jax.experimental.pallas import tpu as pltpu
from jax.sharding import PartitionSpec as P

BF = jnp.bfloat16
F32 = jnp.float32
VMEM_BYTES = 48 * 1024 * 1024


def gathered_plan(tokens, routes, gate_prob, token_count, gate_weight, up_weight, down_weight):
    experts = gate_weight.shape[0]
    stored_rows = gate_weight.shape[1]
    hidden_share = gate_weight.shape[2]
    tok_rows, top_slots = routes.shape
    capacity = min(tok_rows, tok_rows * top_slots * 5 // (4 * experts))
    expert_count = lax.axis_size("expert")
    replica_count = lax.axis_size("dp")
    model_width = stored_rows * expert_count * replica_count

    def relay(weight):
        arrived = lax.all_to_all(weight, "expert", split_axis=0, concat_axis=1, tiled=True)
        blocks = arrived.reshape(1, expert_count, 1, stored_rows, hidden_share)
        return lax.all_gather(blocks, "dp", axis=2, tiled=True).reshape(model_width, hidden_share)

    w_gate, w_up, w_down = relay(gate_weight), relay(up_weight), relay(down_weight)
    positions = jnp.arange(tok_rows)
    live_rows = positions < token_count[0]
    live_pair = jnp.repeat(live_rows, top_slots)
    route_flat = routes.reshape(-1)
    expert_ids = jnp.arange(experts)
    one_hot = ((route_flat[:, None] == expert_ids[None, :]) & live_pair[:, None]).astype(jnp.int32)
    pair_rank = jnp.sum((jnp.cumsum(one_hot, axis=0) - one_hot) * one_hot, axis=1)
    slot_of_pair = jnp.where(live_pair, route_flat * capacity + pair_rank, -1)
    slot_ids = jnp.arange(experts * capacity)
    assign_pair = (slot_ids[:, None] == slot_of_pair[None, :]).astype(BF)
    assign_slots = assign_pair.reshape(experts * capacity, tok_rows, top_slots)
    assign_bf16 = jnp.sum(assign_slots.astype(F32), axis=2).astype(BF)
    outgoing = jnp.dot(assign_bf16, tokens, preferred_element_type=F32).astype(BF)
    incoming = lax.all_to_all(
        outgoing.reshape(experts, capacity, tokens.shape[1]), "expert", split_axis=0, concat_axis=0, tiled=True
    )
    feature_piece = lax.all_gather(incoming, "tensor", axis=2, tiled=True)
    flat_piece = feature_piece.reshape(-1, feature_piece.shape[2])
    gate_proj = jnp.dot(flat_piece, w_gate, preferred_element_type=F32)
    up_proj = jnp.dot(flat_piece, w_up, preferred_element_type=F32)
    hidden = (jax.nn.silu(gate_proj) * up_proj).astype(BF)
    partial_value = lax.dot_general(hidden, w_down, (((1,), (1,)), ((), ())), preferred_element_type=F32)
    expert_out = lax.psum_scatter(partial_value.astype(BF), "tensor", scatter_dimension=1, tiled=True)
    returned = lax.all_to_all(
        expert_out.reshape(experts, capacity, -1), "expert", split_axis=0, concat_axis=0, tiled=True
    )
    returned_rows = returned.reshape(experts * capacity, -1)
    picked = jnp.einsum("cts,cd->std", assign_slots, returned_rows, preferred_element_type=F32)
    mixed = jnp.sum(gate_prob.T[:, :, None] * picked, axis=0)
    return mixed.astype(BF)


def group_of(where_ref, block, n_dp):
    z = lax.rem(where_ref[2] - block + n_dp, n_dp)
    return (where_ref[0] * 2 + where_ref[1]) * n_dp + z


def columns_of(where_ref, meta_ref, blocks, n_dp):
    parts = [meta_ref[group_of(where_ref, b, n_dp)] for b in blocks]
    return jnp.concatenate(parts, axis=0)


def send_order_kernel(where_ref, tokens_ref, *out_refs):
    n_dp = len(out_refs)
    width = tokens_ref.shape[1] // (2 * n_dp)
    core, z = where_ref[1], where_ref[2]
    for k, out in enumerate(out_refs):
        target = lax.rem(z + k, n_dp)
        for j in range(2):
            slot = (lax.rem(core + j, 2) * n_dp + target) * width
            out[:, j * width : (j + 1) * width] = tokens_ref[:, pl.ds(pl.multiple_of(slot, width), width)]


def place_kernel(where_ref, *refs):
    in_refs, out_ref = refs[:-1], refs[-1]
    n_dp = len(in_refs)
    width = out_ref.shape[1] // (2 * n_dp)
    core, z = where_ref[1], where_ref[2]
    for k, piece in enumerate(in_refs):
        source = lax.rem(z + k, n_dp)
        for j in range(2):
            slot = (lax.rem(core + j, 2) * n_dp + source) * width
            out_ref[:, pl.ds(pl.multiple_of(slot, width), width)] = piece[:, j * width : (j + 1) * width]


def gate_up_kernel(n_dp, where_ref, meta_ref, own_ref, far_ref, w0, w1, w2, w3, *out_refs):
    same = where_ref[3] == 1
    rows = own_ref.shape[1]
    experts, width = w0.shape[0], w0.shape[1]
    own = own_ref[...].reshape(n_dp * rows, 2 * width)
    far = far_ref[...].reshape(n_dp * rows, 2 * width)
    near_x = jnp.where(same, own, far)
    away_x = jnp.where(same, far, own)
    meta = columns_of(where_ref, meta_ref, range(n_dp), n_dp)
    slots = [None, None]
    for e in range(experts):
        part = jnp.dot(near_x[:, :width], w0[e], preferred_element_type=F32)
        part += jnp.dot(near_x[:, width:], w1[e], preferred_element_type=F32)
        part += jnp.dot(away_x[:, :width], w2[e], preferred_element_type=F32)
        part += jnp.dot(away_x[:, width:], w3[e], preferred_element_type=F32)
        for s in range(2):
            held = jnp.zeros_like(part) if e == 0 else slots[s]
            slots[s] = jnp.where(meta[:, s : s + 1] == float(e), part, held)
    for k, out in enumerate(out_refs):
        for s in range(2):
            out[s] = slots[s][k * rows : (k + 1) * rows].astype(BF)


def down_kernel(n_dp, where_ref, meta_ref, *refs):
    h_refs = refs[:n_dp]
    w_refs = refs[n_dp : n_dp + 4]
    near_out, away_out = refs[n_dp + 4 :]
    same = where_ref[3] == 1
    rows = h_refs[0].shape[1]
    experts, width = w_refs[0].shape[0], w_refs[0].shape[1]
    meta = columns_of(where_ref, meta_ref, range(n_dp), n_dp)
    h0 = jnp.concatenate([h[0] for h in h_refs], axis=0)
    h1 = jnp.concatenate([h[1] for h in h_refs], axis=0)
    total = [None] * 4
    for e in range(experts):
        first, second = meta[:, 0:1] == float(e), meta[:, 1:2] == float(e)
        h_e = jnp.where(first, h0, jnp.where(second, h1, jnp.zeros_like(h1)))
        scale = jnp.where(first, meta[:, 2:3], jnp.where(second, meta[:, 3:4], 0.0))
        for j in range(4):
            term = scale * lax.dot_general(h_e, w_refs[j][e], (((1,), (1,)), ((), ())), preferred_element_type=F32)
            total[j] = term if e == 0 else total[j] + term
    held = [t.astype(BF).reshape(n_dp, rows, width) for t in total]
    for j in range(2):
        cols = slice(j * width, (j + 1) * width)
        near_out[:, :, cols] = jnp.where(same, held[j], held[j + 2])
        away_out[:, :, cols] = jnp.where(same, held[j + 2], held[j])


SMEM = pl.BlockSpec(memory_space=pltpu.SMEM)
WHOLE = pl.BlockSpec(memory_space=pltpu.VMEM)
PARAMS = pltpu.CompilerParams(vmem_limit_bytes=VMEM_BYTES)


def stationary_plan(tokens, routes, gate_prob, token_count, gate_weight, up_weight, down_weight):
    experts, width, share = gate_weight.shape
    half = share // 2
    rows = tokens.shape[0]
    n_dp = lax.axis_size("dp")
    place = lax.axis_index("expert")
    y, core, x, z = place // 2, place % 2, lax.axis_index("tensor"), lax.axis_index("dp")
    same = (x == y).astype(jnp.int32)
    near = jnp.stack([y, core, z, same]).astype(jnp.int32)
    away = jnp.stack([1 - y, core, z, same]).astype(jnp.int32)

    def swap_y(v):
        return lax.ppermute(v, "expert", [(0, 2), (2, 0), (1, 3), (3, 1)])

    def swap_core(v):
        return lax.ppermute(v, "expert", [(0, 1), (1, 0), (2, 3), (3, 2)])

    def swap_x(v):
        return lax.ppermute(v, "tensor", [(0, 1), (1, 0)])

    def swap_xy(v):
        pairs = [(e * 2 + t, ((e + 2) % 4) * 2 + 1 - t) for e in range(4) for t in range(2)]
        return lax.ppermute(v, ("expert", "tensor"), pairs)

    def shift(v, k):
        return lax.ppermute(v, "dp", [(i, (i + k) % n_dp) for i in range(n_dp)])

    def cut(weight, which):
        return lax.dynamic_slice_in_dim(weight, which * half, half, axis=2)

    gu_send = jnp.concatenate([cut(gate_weight, 1 - y), cut(up_weight, 1 - y)], axis=2)
    gu_y = swap_y(gu_send)
    gu_keep = jnp.concatenate([cut(gate_weight, y), cut(up_weight, y)], axis=2)
    gu_core = swap_core(gu_keep)

    live = jnp.arange(rows)[:, None] < token_count[0]
    meta = jnp.concatenate([jnp.where(live, routes, -1).astype(F32), gate_prob], axis=1)
    metas = lax.all_gather(meta.T, ("expert", "dp"), axis=0).transpose(0, 2, 1)

    send = pl.pallas_call(
        send_order_kernel,
        out_shape=[jax.ShapeDtypeStruct((rows, 2 * width), BF)] * n_dp,
        in_specs=[SMEM, WHOLE],
        out_specs=[WHOLE] * n_dp,
        compiler_params=PARAMS,
    )(near, tokens)
    own = jnp.stack([send[0]] + [shift(send[k], k) for k in range(1, n_dp)])
    own_x = swap_x(own)
    own_y = swap_y(own)
    own_xy = swap_xy(own)
    gu_yc = swap_core(gu_y)

    down_send = cut(down_weight, 1 - y)
    down_send, _ = lax.optimization_barrier((down_send, gu_y))
    down_y = swap_y(down_send)
    down_keep = cut(down_weight, y)
    down_core = swap_core(down_keep)
    down_yc = swap_core(down_y)

    tile = 256
    steps = (2 * half) // tile

    def gate_up(where, mine, other):
        w_spec = pl.BlockSpec((experts, width, tile), lambda n: (0, 0, n))
        return pl.pallas_call(
            functools.partial(gate_up_kernel, n_dp),
            grid=(steps,),
            out_shape=[jax.ShapeDtypeStruct((2, rows, 2 * half), BF)] * n_dp,
            in_specs=[
                SMEM,
                pl.BlockSpec(metas.shape, lambda n: (0, 0, 0)),
                pl.BlockSpec(mine.shape, lambda n: (0, 0, 0)),
                pl.BlockSpec(other.shape, lambda n: (0, 0, 0)),
            ]
            + [w_spec] * 4,
            out_specs=[pl.BlockSpec((2, rows, tile), lambda n: (0, 0, n))] * n_dp,
            compiler_params=PARAMS,
        )(where, metas, mine, other, gu_keep, gu_core, gu_y, gu_yc)

    def ring_sum(parts):
        run = parts[1]
        for k in range(2, n_dp + 1):
            got = shift(run, 1).astype(F32)
            total = parts[k % n_dp].astype(F32) + got
            run = total if k == n_dp else total.astype(BF)
        return run

    def hidden_of(total):
        gate, up = total[..., :half], total[..., half:]
        return (jax.nn.silu(gate) * up).astype(BF)

    def down(where, hidden):
        return pl.pallas_call(
            functools.partial(down_kernel, n_dp),
            out_shape=[jax.ShapeDtypeStruct((n_dp, rows, 2 * width), BF)] * 2,
            in_specs=[SMEM] + [WHOLE] * (n_dp + 5),
            out_specs=[WHOLE] * 2,
            compiler_params=PARAMS,
        )(where, metas, *hidden, down_keep, down_core, down_y, down_yc)

    def gather_dp(v):
        return [v] + [shift(v, k) for k in range(1, n_dp)]

    parts_near = gate_up(near, own, own_x)
    parts_away = gate_up(away, own_y, own_xy)
    hidden_near = gather_dp(hidden_of(ring_sum(parts_near)))
    hidden_away = gather_dp(hidden_of(ring_sum(parts_away)))
    near_mine, near_x = down(near, hidden_near)
    away_y, away_xy = down(away, hidden_away)
    total = near_mine.astype(F32) + swap_x(near_x).astype(F32)
    total = total + swap_y(away_y).astype(F32) + swap_xy(away_xy).astype(F32)
    total = total.astype(BF)
    back = [total[0]] + [shift(total[k], -k) for k in range(1, n_dp)]
    return pl.pallas_call(
        place_kernel,
        out_shape=jax.ShapeDtypeStruct(tokens.shape, BF),
        in_specs=[SMEM] + [WHOLE] * n_dp,
        out_specs=WHOLE,
        compiler_params=PARAMS,
    )(near, *back)


def solution(mesh):
    in_specs = (
        P(("expert", "dp"), "tensor"),
        P(("expert", "dp"), None),
        P(("expert", "dp"), None),
        P(("expert", "dp")),
        P(None, ("expert", "dp"), "tensor"),
        P(None, ("expert", "dp"), "tensor"),
        P(None, ("expert", "dp"), "tensor"),
    )
    out_specs = P(("expert", "dp"), "tensor")
    plan = stationary_plan if mesh.shape["expert"] == 4 and mesh.shape["tensor"] == 2 else gathered_plan
    return jax.shard_map(plan, mesh=mesh, in_specs=in_specs, out_specs=out_specs, check_vma=False)
```

time: 498 us -> 219 us (0.44)
  waiting for transfers between devices: 343 us -> 128 us
  blocking collectives: 112 us -> 29.5 us
  starting transfers between devices: 0.17 us -> 36.3 us
  Pallas kernels: 0 us -> 20.4 us
  matrix products: 20.2 us -> 0 us
  between operations: 13.9 us -> 0.92 us
    all_gather x4 -> x0, waiting for transfers between devices: 307 us -> none  [the longest x1 115 us: shards(): lax.all_gather(split_blocks(arrived_rows[2]), 'dp', axis=2, tiled=True)]
    ppermute x0 -> x30, waiting for transfers between devices: none -> 128 us  [the longest x18 81 us: shift(): return lax.ppermute(v, 'dp', [(i, (i + k) % n_dp) for i in range(n_dp)])]
    all_to_all x5 -> x0, blocking collectives: 112 us -> none  [the longest x1 23.3 us: shards(): lax.all_to_all(up_weight, 'expert', split_axis=0, concat_axis=1, tiled=True)]
    ppermute x0 -> x30, starting transfers between devices: none -> 36.3 us  [the longest x18 22.7 us: shift(): return lax.ppermute(v, 'dp', [(i, (i + k) % n_dp) for i in range(n_dp)])]
    reduce_scatter x1 -> x0, waiting for transfers between devices: 35.9 us -> none  [shards(): lax.psum_scatter(partial_value.astype(jnp.bfloat16), 'tensor', scatter_di...]
    all_gather x0 -> x1, blocking collectives: none -> 29.5 us  [stationary_plan(): metas = lax.all_gather(meta.T, ('expert', 'dp'), axis=0).transpose(0, 2, 1)]
    pallas_call x0 -> x6, Pallas kernels: none -> 20.4 us  [the longest x2 11.6 us: gate_up(): pl.pallas_call(functools.partial(gate_up_kernel, n_dp), grid=(steps,), ou...]
    dot_general x4 -> x0, matrix products: 20.2 us -> none  [the longest x1 12 us: shards(): lax.dot_general(hidden, w_down, (((1,), (1,)), ((), ())), preferred_eleme...]
  transfers between devices with their start and end apart: 5 -> 30, of which waited for: 4 -> 17; matrix products, arithmetic and copies ran while one was open for 1% -> 1% of each run, Pallas kernels for 0% -> 9%
where the time goes in v1:
time: 219 us
  waiting for transfers between devices  128 us (58%)
  starting transfers between devices  36.3 us (17%)
  blocking collectives  29.5 us (13%)
  Pallas kernels  20.4 us (9%)
  local copies, waits for them, and re-layouts  2.79 us (1%)
    ppermute x18, waiting for transfers between devices, shift(): return lax.ppermute(v, 'dp', [(i, (i + k) % n_dp) for i in range(n_dp)])  81 us
    ppermute x4, waiting for transfers between devices, swap_y(): return lax.ppermute(v, 'expert', [(0, 2), (2, 0), (1, 3), (3, 1)])  45.4 us
    all_gather x1, blocking collectives, stationary_plan(): metas = lax.all_gather(meta.T, ('expert', 'dp'), axis=0).transpose(0, 2, 1)  29.5 us
    ppermute x18, starting transfers between devices, shift(): return lax.ppermute(v, 'dp', [(i, (i + k) % n_dp) for i in range(n_dp)])  22.7 us
    pallas_call x2, Pallas kernels, gate_up(): pl.pallas_call(functools.partial(gate_up_kernel, n_dp), grid=(steps,), ou...  11.6 us
    pallas_call x2, Pallas kernels, down(): pl.pallas_call(functools.partial(down_kernel, n_dp), out_shape=[jax.Shape...  6.75 us
    ppermute x4, starting transfers between devices, swap_y(): return lax.ppermute(v, 'expert', [(0, 2), (2, 0), (1, 3), (3, 1)])  6.17 us
    ppermute x2, starting transfers between devices, swap_xy(): return lax.ppermute(v, ('expert', 'tensor'), pairs)  4.7 us
  transfers between devices with their start and end apart: 30, of which 17 were waited for; matrix products, arithmetic and copies ran while one was open for 1% of the time, Pallas kernels for 9%

profile of v1, /device:TPU:0, one launch (start us, length us, event | category | flops | bytes accessed | tf_op | source)
XLA Modules:
  0.0 219.0 jit_solution(370402203475154904)
XLA Ops:
  0.0 2.2 constant_dynamic-slice_fusion.2
  2.3 3.0 %collective-permute-start.5 = (bf16[4,256,768]{2,1,0:T(8,128)(2,1)S(1)}, bf16[4,256,768]{2,1,0:T(8,128)(2,1)}, u32[]{:S(2)}, u32[]{:S(2)}) collective-permute-start(bf16[4,256,768]{2,1,0:T(8,128)(2,1)S(1)} %pad_maximum_fusion.1), channel_id=1, source_target_pairs={{0,16},{16,0},{8,24},{24,8},{1,17},{17,1},{9,25},{25,9},{2,18},{18... | collective-permute-start | bytes 4718600 | tf_op jit(solution)/shard_map/ppermute | solution.py:161
  5.6 34.3 %collective-permute-done.5.w2 = bf16[4,256,768]{2,1,0:T(8,128)(2,1)} collective-permute-done((bf16[4,256,768]{2,1,0:T(8,128)(2,1)S(1)}, bf16[4,256,768]{2,1,0:T(8,128)(2,1)}, u32[]{:S(2)}, u32[]{:S(2)}) %collective-permute-start.5) | collective-permute-done | bytes 1572896 | tf_op jit(solution)/shard_map/ppermute | solution.py:161
  40.6 3.9 %collective-permute-start.2 = (bf16[128,512]{1,0:T(8,128)(2,1)S(1)}, bf16[128,512]{1,0:T(8,128)(2,1)S(1)}, u32[]{:S(2)}, u32[]{:S(2)}) collective-permute-start(bf16[128,512]{1,0:T(8,128)(2,1)S(1)} %get-tuple-element.25), channel_id=1, source_target_pairs={{0,3},{1,0},{2,1},{3,2},{4,7},{5,4},{6,5},{7,6},{8,11},{9,8},{10,9... | collective-permute-start | bytes 393224 | tf_op jit(solution)/shard_map/ppermute | solution.py:174
  46.1 2.2 %collective-permute-done.2 = bf16[128,512]{1,0:T(8,128)(2,1)S(1)} collective-permute-done((bf16[128,512]{1,0:T(8,128)(2,1)S(1)}, bf16[128,512]{1,0:T(8,128)(2,1)S(1)}, u32[]{:S(2)}, u32[]{:S(2)}) %collective-permute-start.2) | collective-permute-done | bytes 131104 | tf_op jit(solution)/shard_map/ppermute | solution.py:174
  48.3 8.2 %collective-permute-done.1 = bf16[128,512]{1,0:T(8,128)(2,1)S(1)} collective-permute-done((bf16[128,512]{1,0:T(8,128)(2,1)S(1)}, bf16[128,512]{1,0:T(8,128)(2,1)S(1)}, u32[]{:S(2)}, u32[]{:S(2)}) %collective-permute-start.1) | collective-permute-done | bytes 131104 | tf_op jit(solution)/shard_map/ppermute | solution.py:174
  60.3 29.5 %all-gather.1 = f32[16,4,128]{2,1,0:T(4,128)S(1)} all-gather(f32[1,4,128]{2,1,0:T(4,128)S(1)} %maximum_bitcast_fusion), channel_id=2, replica_groups=mesh['expert'=4,'tensor'=2,'dp'=4] {'expert','dp'}, dimensions={0}, use_global_device_ids=true | all-gather | bytes 34816 | tf_op jit(solution)/shard_map/all_gather | solution.py:186
  90.3 5.9 %shard_map.76 = (bf16[2,128,768]{2,1,0:T(8,128)(2,1)S(1)}, bf16[2,128,768]{2,1,0:T(8,128)(2,1)S(1)}, bf16[2,128,768]{2,1,0:T(8,128)(2,1)S(1)}, bf16[2,128,768]{2,1,0:T(8,128)(2,1)S(1)}) custom-call(s32[4]{0:T(128)S(1)} %add_add_fusion.1.where_ref, f32[16,128,4]{2,1,0:T(8,128)S(1)} %bitcast.24, bf16[4,128,512]{2,1,0:T(8,128)(2,1)} %collective-permute-done.17.own_ref, ...), custom_call_target="tpu_custom_call" | custom-call | tf_op jit(solution)/shard_map/pallas_call | solution.py:213
  99.8 5.7 %shard_map.74 = (bf16[2,128,768]{2,1,0:T(8,128)(2,1)S(1)}, bf16[2,128,768]{2,1,0:T(8,128)(2,1)S(1)}, bf16[2,128,768]{2,1,0:T(8,128)(2,1)S(1)}, bf16[2,128,768]{2,1,0:T(8,128)(2,1)S(1)}) custom-call(s32[4]{0:T(128)S(1)} %add_add_fusion.where_ref, f32[16,128,4]{2,1,0:T(8,128)S(1)} %bitcast.25, bf16[4,128,512]{2,1,0:T(8,128)(2,1)S(1)} %pad_maximum_fusion.2.own_ref, ...), custom_call_target="tpu_custom_call" | custom-call | tf_op jit(solution)/shard_map/pallas_call | solution.py:213
  107.7 11.7 %collective-permute-done.7 = bf16[2,128,768]{2,1,0:T(8,128)(2,1)S(1)} collective-permute-done((bf16[2,128,768]{2,1,0:T(8,128)(2,1)S(1)}, bf16[2,128,768]{2,1,0:T(8,128)(2,1)S(1)}, u32[]{:S(2)}, u32[]{:S(2)}) %collective-permute-start.7) | collective-permute-done | bytes 393248 | tf_op jit(solution)/shard_map/ppermute | solution.py:174
  119.5 8.3 %collective-permute-done.20 = bf16[2,128,768]{2,1,0:T(8,128)(2,1)S(1)} collective-permute-done((bf16[2,128,768]{2,1,0:T(8,128)(2,1)S(1)}, bf16[2,128,768]{2,1,0:T(8,128)(2,1)S(1)}, u32[]{:S(2)}, u32[]{:S(2)}) %collective-permute-start.20) | collective-permute-done | bytes 393248 | tf_op jit(solution)/shard_map/ppermute | solution.py:174
  128.5 7.7 %collective-permute-done.8 = bf16[2,128,768]{2,1,0:T(8,128)(2,1)S(1)} collective-permute-done((bf16[2,128,768]{2,1,0:T(8,128)(2,1)S(1)}, bf16[2,128,768]{2,1,0:T(8,128)(2,1)S(1)}, u32[]{:S(2)}, u32[]{:S(2)}) %collective-permute-start.8) | collective-permute-done | bytes 393248 | tf_op jit(solution)/shard_map/ppermute | solution.py:174
  136.4 8.4 %collective-permute-done.21 = bf16[2,128,768]{2,1,0:T(8,128)(2,1)S(1)} collective-permute-done((bf16[2,128,768]{2,1,0:T(8,128)(2,1)S(1)}, bf16[2,128,768]{2,1,0:T(8,128)(2,1)S(1)}, u32[]{:S(2)}, u32[]{:S(2)}) %collective-permute-start.21) | collective-permute-done | bytes 393248 | tf_op jit(solution)/shard_map/ppermute | solution.py:174
  145.6 7.5 %collective-permute-done.9 = bf16[2,128,768]{2,1,0:T(8,128)(2,1)S(1)} collective-permute-done((bf16[2,128,768]{2,1,0:T(8,128)(2,1)S(1)}, bf16[2,128,768]{2,1,0:T(8,128)(2,1)S(1)}, u32[]{:S(2)}, u32[]{:S(2)}) %collective-permute-start.9) | collective-permute-done | bytes 393248 | tf_op jit(solution)/shard_map/ppermute | solution.py:174
  157.4 2.8 %collective-permute-start.12 = (bf16[2,128,384]{2,1,0:T(8,128)(2,1)S(1)}, bf16[2,128,384]{2,1,0:T(8,128)(2,1)S(1)}, u32[]{:S(2)}, u32[]{:S(2)}) collective-permute-start(bf16[2,128,384]{2,1,0:T(8,128)(2,1)S(1)} %fusion.1.refs_0_), channel_id=1, source_target_pairs={{0,3},{1,0},{2,1},{3,2},{4,7},{5,4},{6,5},{7,6},{8,11},{9,8},{10,9... | collective-permute-start | bytes 589832 | tf_op jit(solution)/shard_map/ppermute | solution.py:174
  160.1 5.4 %collective-permute-done.23.refs_2_ = bf16[2,128,384]{2,1,0:T(8,128)(2,1)S(1)} collective-permute-done((bf16[2,128,384]{2,1,0:T(8,128)(2,1)S(1)}, bf16[2,128,384]{2,1,0:T(8,128)(2,1)S(1)}, u32[]{:S(2)}, u32[]{:S(2)}) %collective-permute-start.23) | collective-permute-done | bytes 196640 | tf_op jit(solution)/shard_map/ppermute | solution.py:174
  165.6 3.4 %shard_map.77 = (bf16[4,128,512]{2,1,0:T(8,128)(2,1)S(1)}, bf16[4,128,512]{2,1,0:T(8,128)(2,1)S(1)}) custom-call(s32[4]{0:T(128)S(1)} %add_add_fusion.1.where_ref, f32[16,128,4]{2,1,0:T(8,128)S(1)} %bitcast.26, bf16[2,128,384]{2,1,0:T(8,128)(2,1)S(1)} %fusion.refs_0_, bf16[2,128,384]{2,1,0:T(8,128)(2,1)S(1)} %collective-permute-done.22.refs_1_, ...), custom_call_target="tpu_custom_call" | custom-call | tf_op jit(solution)/shard_map/pallas_call | solution.py:241
  169.0 3.3 %collective-permute-start.26 = (bf16[4,128,512]{2,1,0:T(8,128)(2,1)S(1)}, bf16[4,128,512]{2,1,0:T(8,128)(2,1)S(1)}, u32[]{:S(2)}, u32[]{:S(2)}) collective-permute-start(bf16[4,128,512]{2,1,0:T(8,128)(2,1)S(1)} %get-tuple-element.38), channel_id=1, source_target_pairs={{0,20},{4,16},{8,28},{12,24},{16,4},{20,0},{24,12},{28,8},{1,21},{... | collective-permute-start | bytes 1572872 | tf_op jit(solution)/shard_map/ppermute | solution.py:171
  172.2 6.0 %collective-permute-done.11.refs_2_ = bf16[2,128,384]{2,1,0:T(8,128)(2,1)S(1)} collective-permute-done((bf16[2,128,384]{2,1,0:T(8,128)(2,1)S(1)}, bf16[2,128,384]{2,1,0:T(8,128)(2,1)S(1)}, u32[]{:S(2)}, u32[]{:S(2)}) %collective-permute-start.11) | collective-permute-done | bytes 196640 | tf_op jit(solution)/shard_map/ppermute | solution.py:174
  178.2 3.4 %shard_map.75 = (bf16[4,128,512]{2,1,0:T(8,128)(2,1)S(1)}, bf16[4,128,512]{2,1,0:T(8,128)(2,1)S(1)}) custom-call(s32[4]{0:T(128)S(1)} %add_add_fusion.where_ref, f32[16,128,4]{2,1,0:T(8,128)S(1)} %bitcast.27, bf16[2,128,384]{2,1,0:T(8,128)(2,1)S(1)} %fusion.1.refs_0_, bf16[2,128,384]{2,1,0:T(8,128)(2,1)S(1)} %collective-permute-done.10.refs_1_, ...), custom_call_target="tpu_custom_call" | custom-call | tf_op jit(solution)/shard_map/pallas_call | solution.py:241
  183.8 11.1 %collective-permute-done.25 = bf16[4,128,512]{2,1,0:T(8,128)(2,1)S(1)} collective-permute-done((bf16[4,128,512]{2,1,0:T(8,128)(2,1)S(1)}, bf16[4,128,512]{2,1,0:T(8,128)(2,1)S(1)}, u32[]{:S(2)}, u32[]{:S(2)}) %collective-permute-start.25) | collective-permute-done | bytes 524320 | tf_op jit(solution)/shard_map/ppermute | solution.py:161
  195.7 5.6 %collective-permute-start.27 = (bf16[128,512]{1,0:T(8,128)(2,1)S(1)}, bf16[128,512]{1,0:T(8,128)(2,1)S(1)}, u32[]{:S(2)}, u32[]{:S(2)}) collective-permute-start(bf16[128,512]{1,0:T(8,128)(2,1)S(1)} %get-tuple-element.47), channel_id=1, source_target_pairs={{0,3},{1,0},{2,1},{3,2},{4,7},{5,4},{6,5},{7,6},{8,11},{9,8},{10,9... | collective-permute-start | bytes 393224 | tf_op jit(solution)/shard_map/ppermute | solution.py:174
  201.3 4.5 %collective-permute-start.28 = (bf16[128,512]{1,0:T(8,128)(2,1)S(1)}, bf16[128,512]{1,0:T(8,128)(2,1)S(1)}, u32[]{:S(2)}, u32[]{:S(2)}) collective-permute-start(bf16[128,512]{1,0:T(8,128)(2,1)S(1)} %get-tuple-element.46), channel_id=1, source_target_pairs={{0,2},{1,3},{2,0},{3,1},{4,6},{5,7},{6,4},{7,5},{8,10},{9,11},{10,... | collective-permute-start | bytes 393224 | tf_op jit(solution)/shard_map/ppermute | solution.py:174
  208.0 9.6 %collective-permute-done.28.refs_2_ = bf16[128,512]{1,0:T(8,128)(2,1)S(1)} collective-permute-done((bf16[128,512]{1,0:T(8,128)(2,1)S(1)}, bf16[128,512]{1,0:T(8,128)(2,1)S(1)}, u32[]{:S(2)}, u32[]{:S(2)}) %collective-permute-start.28) | collective-permute-done | bytes 131104 | tf_op jit(solution)/shard_map/ppermute | solution.py:174
  (72 shorter events, 24.7 us)
Async XLA Ops:
  2.3 37.5 %collective-permute-start.5 = (bf16[4,256,768]{2,1,0:T(8,128)(2,1)S(1)}, bf16[4,256,768]{2,1,0:T(8,128)(2,1)}, u32[]{:S(2)}, u32[]{:S(2)}) collective-permute-start(bf16[4,256,768]{2,1,0:T(8,128)(2,1)S(1)} %pad_maximum_fusion.1), channel_id=1, source_target_pairs={{0,16},{16,0},{8,24},{24,8},{1,17},{17,1},{9,25},{25,9},{2,18},{18... | collective-permute-start | bytes 4718600 | tf_op jit(solution)/shard_map/ppermute | solution.py:161
  5.5 84.7 %collective-permute-start.4 = (bf16[4,256,768]{2,1,0:T(8,128)(2,1)S(1)}, bf16[4,256,768]{2,1,0:T(8,128)(2,1)}, u32[]{:S(2)}, u32[]{:S(2)}) collective-permute-start(bf16[4,256,768]{2,1,0:T(8,128)(2,1)S(1)} %pad_maximum_fusion.w0), channel_id=1, source_target_pairs={{0,8},{8,0},{16,24},{24,16},{1,9},{9,1},{17,25},{25,17},{2,10},{10... | collective-permute-start | bytes 4718600 | tf_op jit(solution)/shard_map/ppermute | solution.py:164
  39.8 50.4 %collective-permute-start.6 = (bf16[4,256,768]{2,1,0:T(8,128)(2,1)}, bf16[4,256,768]{2,1,0:T(8,128)(2,1)}, u32[]{:S(2)}, u32[]{:S(2)}) collective-permute-start(bf16[4,256,768]{2,1,0:T(8,128)(2,1)} %collective-permute-done.5.w2), channel_id=1, source_target_pairs={{0,8},{8,0},{16,24},{24,16},{1,9},{9,1},{17,25},{25,17},{2,10},{10... | collective-permute-start | bytes 4718600 | tf_op jit(solution)/shard_map/ppermute | solution.py:164
  56.7 33.6 %collective-permute-start.17 = (bf16[4,128,512]{2,1,0:T(8,128)(2,1)S(1)}, bf16[4,128,512]{2,1,0:T(8,128)(2,1)}, u32[]{:S(2)}, u32[]{:S(2)}) collective-permute-start(bf16[4,128,512]{2,1,0:T(8,128)(2,1)S(1)} %pad_maximum_fusion.2.own_ref), channel_id=1, source_target_pairs={{0,16},{16,0},{8,24},{24,8},{1,17},{17,1},{9,25},{25,9},{2,18},{18... | collective-permute-start | bytes 1572872 | tf_op jit(solution)/shard_map/ppermute | solution.py:161
  58.2 32.0 %collective-permute-start.18 = (bf16[4,128,512]{2,1,0:T(8,128)(2,1)S(1)}, bf16[4,128,512]{2,1,0:T(8,128)(2,1)}, u32[]{:S(2)}, u32[]{:S(2)}) collective-permute-start(bf16[4,128,512]{2,1,0:T(8,128)(2,1)S(1)} %pad_maximum_fusion.2.own_ref), channel_id=1, source_target_pairs={{0,20},{4,16},{8,28},{12,24},{16,4},{20,0},{24,12},{28,8},{1,21},{... | collective-permute-start | bytes 1572872 | tf_op jit(solution)/shard_map/ppermute | solution.py:171
  59.7 40.1 %collective-permute-start.3 = (bf16[4,128,512]{2,1,0:T(8,128)(2,1)S(1)}, bf16[4,128,512]{2,1,0:T(8,128)(2,1)}, u32[]{:S(2)}, u32[]{:S(2)}) collective-permute-start(bf16[4,128,512]{2,1,0:T(8,128)(2,1)S(1)} %pad_maximum_fusion.2.own_ref), channel_id=1, source_target_pairs={{0,4},{4,0},{1,5},{5,1},{2,6},{6,2},{3,7},{7,3},{8,12},{12,8},{9,1... | collective-permute-start | bytes 1572872 | tf_op jit(solution)/shard_map/ppermute | solution.py:167
  98.3 29.8 %collective-permute-start.14 = (bf16[4,256,384]{2,1,0:T(8,128)(2,1)S(1)}, bf16[4,256,384]{2,1,0:T(8,128)(2,1)S(1)}, u32[]{:S(2)}, u32[]{:S(2)}) collective-permute-start(bf16[4,256,384]{2,1,0:T(8,128)(2,1)S(1)} %get-tuple-element.30), channel_id=1, source_target_pairs={{0,16},{16,0},{8,24},{24,8},{1,17},{17,1},{9,25},{25,9},{2,18},{18... | collective-permute-start | bytes 2359304 | tf_op jit(solution)/shard_map/ppermute | solution.py:161
  105.5 13.9 %collective-permute-start.7 = (bf16[2,128,768]{2,1,0:T(8,128)(2,1)S(1)}, bf16[2,128,768]{2,1,0:T(8,128)(2,1)S(1)}, u32[]{:S(2)}, u32[]{:S(2)}) collective-permute-start(bf16[2,128,768]{2,1,0:T(8,128)(2,1)S(1)} %get-tuple-element.29), channel_id=1, source_target_pairs={{0,1},{1,2},{2,3},{3,0},{4,5},{5,6},{6,7},{7,4},{8,9},{9,10},{10,1... | collective-permute-start | bytes 1179656 | tf_op jit(solution)/shard_map/ppermute | solution.py:174
  107.6 20.2 %collective-permute-start.20 = (bf16[2,128,768]{2,1,0:T(8,128)(2,1)S(1)}, bf16[2,128,768]{2,1,0:T(8,128)(2,1)S(1)}, u32[]{:S(2)}, u32[]{:S(2)}) collective-permute-start(bf16[2,128,768]{2,1,0:T(8,128)(2,1)S(1)} %add_convert_fusion.2), channel_id=1, source_target_pairs={{0,1},{1,2},{2,3},{3,0},{4,5},{5,6},{6,7},{7,4},{8,9},{9,10},{10,1... | collective-permute-start | bytes 1179656 | tf_op jit(solution)/shard_map/ppermute | solution.py:174
  119.5 16.8 %collective-permute-start.8 = (bf16[2,128,768]{2,1,0:T(8,128)(2,1)S(1)}, bf16[2,128,768]{2,1,0:T(8,128)(2,1)S(1)}, u32[]{:S(2)}, u32[]{:S(2)}) collective-permute-start(bf16[2,128,768]{2,1,0:T(8,128)(2,1)S(1)} %add_convert_fusion.4), channel_id=1, source_target_pairs={{0,1},{1,2},{2,3},{3,0},{4,5},{5,6},{6,7},{7,4},{8,9},{9,10},{10,1... | collective-permute-start | bytes 1179656 | tf_op jit(solution)/shard_map/ppermute | solution.py:174
  127.9 16.9 %collective-permute-start.21 = (bf16[2,128,768]{2,1,0:T(8,128)(2,1)S(1)}, bf16[2,128,768]{2,1,0:T(8,128)(2,1)S(1)}, u32[]{:S(2)}, u32[]{:S(2)}) collective-permute-start(bf16[2,128,768]{2,1,0:T(8,128)(2,1)S(1)} %add_convert_fusion.1), channel_id=1, source_target_pairs={{0,1},{1,2},{2,3},{3,0},{4,5},{5,6},{6,7},{7,4},{8,9},{9,10},{10,1... | collective-permute-start | bytes 1179656 | tf_op jit(solution)/shard_map/ppermute | solution.py:174
  128.0 25.6 %collective-permute-start.13 = (bf16[4,256,384]{2,1,0:T(8,128)(2,1)S(1)}, bf16[4,256,384]{2,1,0:T(8,128)(2,1)S(1)}, u32[]{:S(2)}, u32[]{:S(2)}) collective-permute-start(bf16[4,256,384]{2,1,0:T(8,128)(2,1)S(1)} %get-tuple-element.40.refs_4_), channel_id=1, source_target_pairs={{0,8},{8,0},{16,24},{24,16},{1,9},{9,1},{17,25},{25,17},{2,10},{10... | collective-permute-start | bytes 2359304 | tf_op jit(solution)/shard_map/ppermute | solution.py:164
  128.0 27.4 %collective-permute-start.15 = (bf16[4,256,384]{2,1,0:T(8,128)(2,1)S(1)}, bf16[4,256,384]{2,1,0:T(8,128)(2,1)S(1)}, u32[]{:S(2)}, u32[]{:S(2)}) collective-permute-start(bf16[4,256,384]{2,1,0:T(8,128)(2,1)S(1)} %collective-permute-done.14.refs_6_), channel_id=1, source_target_pairs={{0,8},{8,0},{16,24},{24,16},{1,9},{9,1},{17,25},{25,17},{2,10},{10... | collective-permute-start | bytes 2359304 | tf_op jit(solution)/shard_map/ppermute | solution.py:164
  136.3 16.9 %collective-permute-start.9 = (bf16[2,128,768]{2,1,0:T(8,128)(2,1)S(1)}, bf16[2,128,768]{2,1,0:T(8,128)(2,1)S(1)}, u32[]{:S(2)}, u32[]{:S(2)}) collective-permute-start(bf16[2,128,768]{2,1,0:T(8,128)(2,1)S(1)} %add_convert_fusion.3), channel_id=1, source_target_pairs={{0,1},{1,2},{2,3},{3,0},{4,5},{5,6},{6,7},{7,4},{8,9},{9,10},{10,1... | collective-permute-start | bytes 1179656 | tf_op jit(solution)/shard_map/ppermute | solution.py:174
  145.0 12.4 %collective-permute-start.22 = (bf16[2,128,384]{2,1,0:T(8,128)(2,1)S(1)}, bf16[2,128,384]{2,1,0:T(8,128)(2,1)S(1)}, u32[]{:S(2)}, u32[]{:S(2)}) collective-permute-start(bf16[2,128,384]{2,1,0:T(8,128)(2,1)S(1)} %fusion.refs_0_), channel_id=1, source_target_pairs={{0,1},{1,2},{2,3},{3,0},{4,5},{5,6},{6,7},{7,4},{8,9},{9,10},{10,1... | collective-permute-start | bytes 589832 | tf_op jit(solution)/shard_map/ppermute | solution.py:174
  145.0 20.6 %collective-permute-start.23 = (bf16[2,128,384]{2,1,0:T(8,128)(2,1)S(1)}, bf16[2,128,384]{2,1,0:T(8,128)(2,1)S(1)}, u32[]{:S(2)}, u32[]{:S(2)}) collective-permute-start(bf16[2,128,384]{2,1,0:T(8,128)(2,1)S(1)} %fusion.refs_0_), channel_id=1, source_target_pairs={{0,2},{1,3},{2,0},{3,1},{4,6},{5,7},{6,4},{7,5},{8,10},{9,11},{10,... | collective-permute-start | bytes 589832 | tf_op jit(solution)/shard_map/ppermute | solution.py:174
  153.2 12.4 %collective-permute-start.24 = (bf16[2,128,384]{2,1,0:T(8,128)(2,1)S(1)}, bf16[2,128,384]{2,1,0:T(8,128)(2,1)S(1)}, u32[]{:S(2)}, u32[]{:S(2)}) collective-permute-start(bf16[2,128,384]{2,1,0:T(8,128)(2,1)S(1)} %fusion.refs_0_), channel_id=1, source_target_pairs={{0,3},{1,0},{2,1},{3,2},{4,7},{5,4},{6,5},{7,6},{8,11},{9,8},{10,9... | collective-permute-start | bytes 589832 | tf_op jit(solution)/shard_map/ppermute | solution.py:174
  153.5 18.7 %collective-permute-start.10 = (bf16[2,128,384]{2,1,0:T(8,128)(2,1)S(1)}, bf16[2,128,384]{2,1,0:T(8,128)(2,1)S(1)}, u32[]{:S(2)}, u32[]{:S(2)}) collective-permute-start(bf16[2,128,384]{2,1,0:T(8,128)(2,1)S(1)} %fusion.1.refs_0_), channel_id=1, source_target_pairs={{0,1},{1,2},{2,3},{3,0},{4,5},{5,6},{6,7},{7,4},{8,9},{9,10},{10,1... | collective-permute-start | bytes 589832 | tf_op jit(solution)/shard_map/ppermute | solution.py:174
  155.5 22.7 %collective-permute-start.11 = (bf16[2,128,384]{2,1,0:T(8,128)(2,1)S(1)}, bf16[2,128,384]{2,1,0:T(8,128)(2,1)S(1)}, u32[]{:S(2)}, u32[]{:S(2)}) collective-permute-start(bf16[2,128,384]{2,1,0:T(8,128)(2,1)S(1)} %fusion.1.refs_0_), channel_id=1, source_target_pairs={{0,2},{1,3},{2,0},{3,1},{4,6},{5,7},{6,4},{7,5},{8,10},{9,11},{10,... | collective-permute-start | bytes 589832 | tf_op jit(solution)/shard_map/ppermute | solution.py:174
  157.4 20.8 %collective-permute-start.12 = (bf16[2,128,384]{2,1,0:T(8,128)(2,1)S(1)}, bf16[2,128,384]{2,1,0:T(8,128)(2,1)S(1)}, u32[]{:S(2)}, u32[]{:S(2)}) collective-permute-start(bf16[2,128,384]{2,1,0:T(8,128)(2,1)S(1)} %fusion.1.refs_0_), channel_id=1, source_target_pairs={{0,3},{1,0},{2,1},{3,2},{4,7},{5,4},{6,5},{7,6},{8,11},{9,8},{10,9... | collective-permute-start | bytes 589832 | tf_op jit(solution)/shard_map/ppermute | solution.py:174
  169.0 14.8 %collective-permute-start.26 = (bf16[4,128,512]{2,1,0:T(8,128)(2,1)S(1)}, bf16[4,128,512]{2,1,0:T(8,128)(2,1)S(1)}, u32[]{:S(2)}, u32[]{:S(2)}) collective-permute-start(bf16[4,128,512]{2,1,0:T(8,128)(2,1)S(1)} %get-tuple-element.38), channel_id=1, source_target_pairs={{0,20},{4,16},{8,28},{12,24},{16,4},{20,0},{24,12},{28,8},{1,21},{... | collective-permute-start | bytes 1572872 | tf_op jit(solution)/shard_map/ppermute | solution.py:171
  172.2 22.7 %collective-permute-start.25 = (bf16[4,128,512]{2,1,0:T(8,128)(2,1)S(1)}, bf16[4,128,512]{2,1,0:T(8,128)(2,1)S(1)}, u32[]{:S(2)}, u32[]{:S(2)}) collective-permute-start(bf16[4,128,512]{2,1,0:T(8,128)(2,1)S(1)} %get-tuple-element.37), channel_id=1, source_target_pairs={{0,16},{16,0},{8,24},{24,8},{1,17},{17,1},{9,25},{25,9},{2,18},{18... | collective-permute-start | bytes 1572872 | tf_op jit(solution)/shard_map/ppermute | solution.py:161
  181.6 13.8 %collective-permute-start.16 = (bf16[4,128,512]{2,1,0:T(8,128)(2,1)S(1)}, bf16[4,128,512]{2,1,0:T(8,128)(2,1)S(1)}, u32[]{:S(2)}, u32[]{:S(2)}) collective-permute-start(bf16[4,128,512]{2,1,0:T(8,128)(2,1)S(1)} %get-tuple-element.32), channel_id=1, source_target_pairs={{0,4},{4,0},{1,5},{5,1},{2,6},{6,2},{3,7},{7,3},{8,12},{12,8},{9,1... | collective-permute-start | bytes 1572872 | tf_op jit(solution)/shard_map/ppermute | solution.py:167
  201.3 16.2 %collective-permute-start.28 = (bf16[128,512]{1,0:T(8,128)(2,1)S(1)}, bf16[128,512]{1,0:T(8,128)(2,1)S(1)}, u32[]{:S(2)}, u32[]{:S(2)}) collective-permute-start(bf16[128,512]{1,0:T(8,128)(2,1)S(1)} %get-tuple-element.46), channel_id=1, source_target_pairs={{0,2},{1,3},{2,0},{3,1},{4,6},{5,7},{6,4},{7,5},{8,10},{9,11},{10,... | collective-permute-start | bytes 393224 | tf_op jit(solution)/shard_map/ppermute | solution.py:174
  (10 other events, 218.7 us)

commit v2 on v1

v2 whole, which is shorter than its diff:
```python
import functools

import jax
import jax.numpy as jnp
from jax import lax
from jax.experimental import pallas as pl
from jax.experimental.pallas import tpu as pltpu
from jax.sharding import PartitionSpec as P

BF = jnp.bfloat16
F32 = jnp.float32
VMEM_BYTES = 48 * 1024 * 1024


def gathered_plan(tokens, routes, gate_prob, token_count, gate_weight, up_weight, down_weight):
    experts = gate_weight.shape[0]
    stored_rows = gate_weight.shape[1]
    hidden_share = gate_weight.shape[2]
    tok_rows, top_slots = routes.shape
    capacity = min(tok_rows, tok_rows * top_slots * 5 // (4 * experts))
    expert_count = lax.axis_size("expert")
    replica_count = lax.axis_size("dp")
    model_width = stored_rows * expert_count * replica_count

    def relay(weight):
        arrived = lax.all_to_all(weight, "expert", split_axis=0, concat_axis=1, tiled=True)
        blocks = arrived.reshape(1, expert_count, 1, stored_rows, hidden_share)
        return lax.all_gather(blocks, "dp", axis=2, tiled=True).reshape(model_width, hidden_share)

    w_gate, w_up, w_down = relay(gate_weight), relay(up_weight), relay(down_weight)
    positions = jnp.arange(tok_rows)
    live_rows = positions < token_count[0]
    live_pair = jnp.repeat(live_rows, top_slots)
    route_flat = routes.reshape(-1)
    expert_ids = jnp.arange(experts)
    one_hot = ((route_flat[:, None] == expert_ids[None, :]) & live_pair[:, None]).astype(jnp.int32)
    pair_rank = jnp.sum((jnp.cumsum(one_hot, axis=0) - one_hot) * one_hot, axis=1)
    slot_of_pair = jnp.where(live_pair, route_flat * capacity + pair_rank, -1)
    slot_ids = jnp.arange(experts * capacity)
    assign_pair = (slot_ids[:, None] == slot_of_pair[None, :]).astype(BF)
    assign_slots = assign_pair.reshape(experts * capacity, tok_rows, top_slots)
    assign_bf16 = jnp.sum(assign_slots.astype(F32), axis=2).astype(BF)
    outgoing = jnp.dot(assign_bf16, tokens, preferred_element_type=F32).astype(BF)
    incoming = lax.all_to_all(
        outgoing.reshape(experts, capacity, tokens.shape[1]), "expert", split_axis=0, concat_axis=0, tiled=True
    )
    feature_piece = lax.all_gather(incoming, "tensor", axis=2, tiled=True)
    flat_piece = feature_piece.reshape(-1, feature_piece.shape[2])
    gate_proj = jnp.dot(flat_piece, w_gate, preferred_element_type=F32)
    up_proj = jnp.dot(flat_piece, w_up, preferred_element_type=F32)
    hidden = (jax.nn.silu(gate_proj) * up_proj).astype(BF)
    partial_value = lax.dot_general(hidden, w_down, (((1,), (1,)), ((), ())), preferred_element_type=F32)
    expert_out = lax.psum_scatter(partial_value.astype(BF), "tensor", scatter_dimension=1, tiled=True)
    returned = lax.all_to_all(
        expert_out.reshape(experts, capacity, -1), "expert", split_axis=0, concat_axis=0, tiled=True
    )
    returned_rows = returned.reshape(experts * capacity, -1)
    picked = jnp.einsum("cts,cd->std", assign_slots, returned_rows, preferred_element_type=F32)
    mixed = jnp.sum(gate_prob.T[:, :, None] * picked, axis=0)
    return mixed.astype(BF)


META_ROWS = 16
UNIT = 128


def split_in_three(value):
    high = value.astype(BF)
    rest = value - high.astype(F32)
    middle = rest.astype(BF)
    return high, middle, (rest - middle.astype(F32)).astype(BF)


def columns_of(token_refs, rows):
    held = jnp.concatenate([t[rows:, :rows].astype(F32).T for t in token_refs], axis=0)
    prob = [held[:, 2 + s : 3 + s] + held[:, 4 + s : 5 + s] + held[:, 6 + s : 7 + s] for s in range(2)]
    return held[:, 0:1], held[:, 1:2], prob[0], prob[1]


def send_order_kernel(where_ref, tokens_ref, route_ref, prob_ref, *out_refs):
    n_dp = len(out_refs)
    rows = tokens_ref.shape[0]
    width = tokens_ref.shape[1] // (2 * n_dp)
    core, z = where_ref[1], where_ref[2]
    meta = [route_ref[...].astype(BF), *split_in_three(prob_ref[...])]
    for k, out in enumerate(out_refs):
        target = lax.rem(z + k, n_dp)
        for j in range(2):
            slot = (lax.rem(core + j, 2) * n_dp + target) * width
            out[:rows, j * width : (j + 1) * width] = tokens_ref[:, pl.ds(pl.multiple_of(slot, width), width)]
        filler = jnp.zeros((META_ROWS - 8, rows), F32)
        block = jnp.concatenate([m.astype(F32) for m in meta] + [filler], axis=0).astype(BF)
        out[rows:, :] = jnp.zeros((META_ROWS, 2 * width), BF)
        out[rows:, :rows] = block


def place_kernel(where_ref, *refs):
    in_refs, out_ref = refs[:-1], refs[-1]
    n_dp = len(in_refs)
    width = out_ref.shape[1] // (2 * n_dp)
    core, z = where_ref[1], where_ref[2]
    for k, piece in enumerate(in_refs):
        source = lax.rem(z + k, n_dp)
        for j in range(2):
            slot = (lax.rem(core + j, 2) * n_dp + source) * width
            out_ref[:, pl.ds(pl.multiple_of(slot, width), width)] = piece[:, j * width : (j + 1) * width]


def gate_up_kernel(n_dp, where_ref, *refs):
    own_refs, far_refs = refs[:n_dp], refs[n_dp : 2 * n_dp]
    w_refs = refs[2 * n_dp : 2 * n_dp + 4]
    out_refs = refs[2 * n_dp + 4 :]
    same = where_ref[3] == 1
    rows = own_refs[0].shape[0] - META_ROWS
    blocks, experts, width, tile = w_refs[0].shape
    own = jnp.concatenate([r[:rows] for r in own_refs], axis=0)
    far = jnp.concatenate([r[:rows] for r in far_refs], axis=0)
    near_x = jnp.where(same, own, far)
    away_x = jnp.where(same, far, own)
    pieces = (near_x[:, :width], near_x[:, width:], away_x[:, :width], away_x[:, width:])
    route = columns_of(own_refs, rows)[:2]
    for b in range(blocks):
        slots = [None, None]
        for e in range(experts):
            part = sum(jnp.dot(p, w[b, e], preferred_element_type=F32) for p, w in zip(pieces, w_refs))
            for s in range(2):
                held = jnp.zeros_like(part) if e == 0 else slots[s]
                slots[s] = jnp.where(route[s] == float(e), part, held)
        for k, out in enumerate(out_refs):
            for s in range(2):
                out[s, :, b * tile : (b + 1) * tile] = slots[s][k * rows : (k + 1) * rows].astype(BF)


def hidden_kernel(n_spans, *refs):
    mine, got, out_ref = refs[:n_spans], refs[n_spans : 2 * n_spans], refs[-1]
    unit, at = UNIT, 0
    for a, b in zip(mine, got):
        for n in range(a.shape[-1] // (2 * unit)):
            gate_cols = slice(2 * n * unit, (2 * n + 1) * unit)
            up_cols = slice((2 * n + 1) * unit, (2 * n + 2) * unit)
            for s in range(2):
                gate = a[s, :, gate_cols].astype(F32) + b[s, :, gate_cols].astype(F32)
                up = a[s, :, up_cols].astype(F32) + b[s, :, up_cols].astype(F32)
                out_ref[s, :, at : at + unit] = (gate / (1.0 + jnp.exp(-gate)) * up).astype(BF)
            at += unit


def down_kernel(n_blocks, where_ref, *refs):
    token_refs, h_refs = refs[:n_blocks], refs[n_blocks : 2 * n_blocks]
    w_refs = refs[2 * n_blocks : 2 * n_blocks + 4]
    near_out, away_out = refs[2 * n_blocks + 4 :]
    same = where_ref[3] == 1
    rows = h_refs[0].shape[1]
    experts, width = w_refs[0].shape[0], w_refs[0].shape[1]
    route0, route1, prob0, prob1 = columns_of(token_refs, rows)
    h0 = jnp.concatenate([h[0] for h in h_refs], axis=0)
    h1 = jnp.concatenate([h[1] for h in h_refs], axis=0)
    total = [None] * 4
    for e in range(experts):
        first, second = route0 == float(e), route1 == float(e)
        h_e = jnp.where(first, h0, jnp.where(second, h1, jnp.zeros_like(h1)))
        scale = jnp.where(first, prob0, jnp.where(second, prob1, 0.0))
        for j in range(4):
            term = scale * lax.dot_general(h_e, w_refs[j][e], (((1,), (1,)), ((), ())), preferred_element_type=F32)
            total[j] = term if e == 0 else total[j] + term
    held = [t.astype(BF).reshape(n_blocks, rows, width) for t in total]
    for j in range(2):
        cols = slice(j * width, (j + 1) * width)
        near_out[:, :, cols] = jnp.where(same, held[j], held[j + 2])
        away_out[:, :, cols] = jnp.where(same, held[j + 2], held[j])


SMEM = pl.BlockSpec(memory_space=pltpu.SMEM)
WHOLE = pl.BlockSpec(memory_space=pltpu.VMEM)
PARAMS = pltpu.CompilerParams(vmem_limit_bytes=VMEM_BYTES)
LIGHT = pl.CostEstimate(flops=1, bytes_accessed=1, transcendentals=0)


def stationary_plan(tokens, routes, gate_prob, token_count, gate_weight, up_weight, down_weight):
    experts, width, share = gate_weight.shape
    half = share // 2
    rows = tokens.shape[0]
    n_dp = lax.axis_size("dp")
    place = lax.axis_index("expert")
    y, core, x, z = place // 2, place % 2, lax.axis_index("tensor"), lax.axis_index("dp")
    same = (x == y).astype(jnp.int32)
    where = jnp.stack([y, core, z, (x == y).astype(jnp.int32)]).astype(jnp.int32)

    def swap_y(v):
        return lax.ppermute(v, "expert", [(0, 2), (2, 0), (1, 3), (3, 1)])

    def swap_core(v):
        return lax.ppermute(v, "expert", [(0, 1), (1, 0), (2, 3), (3, 2)])

    def swap_x(v):
        return lax.ppermute(v, "tensor", [(0, 1), (1, 0)])

    def swap_xy(v):
        pairs = [(e * 2 + t, ((e + 2) % 4) * 2 + 1 - t) for e in range(4) for t in range(2)]
        return lax.ppermute(v, ("expert", "tensor"), pairs)

    def shift(v, k):
        return lax.ppermute(v, "dp", [(i, (i + k) % n_dp) for i in range(n_dp)])

    def cut(weight, which):
        return lax.dynamic_slice_in_dim(weight, which * half, half, axis=2)

    live = jnp.arange(rows)[None, :] < token_count[0]
    slots = jnp.where(live, routes.T, -1).astype(F32)

    send = pl.pallas_call(
        send_order_kernel,
        out_shape=[jax.ShapeDtypeStruct((rows + META_ROWS, 2 * width), BF)] * n_dp,
        in_specs=[SMEM] + [WHOLE] * 3,
        out_specs=[WHOLE] * n_dp,
        compiler_params=PARAMS,
        cost_estimate=LIGHT,
    )(where, tokens, slots, gate_prob.T)
    own = jnp.stack([send[0]] + [shift(send[k], k) for k in range(1, n_dp)])

    unit = UNIT

    def gate_up_blocks(which, first, count):
        def block(n):
            start = which * half + n * unit
            return jnp.concatenate(
                [lax.dynamic_slice_in_dim(w, start, unit, axis=2) for w in (gate_weight, up_weight)], axis=2
            )

        return jnp.stack([block(n) for n in range(first, first + count)])

    blocks = half // unit
    spans = [(0, 1), (1, blocks - 1)]
    gu_send = [gate_up_blocks(1 - y, *span) for span in spans]
    gu_send[0], _ = lax.optimization_barrier((gu_send[0], send[0]))
    gu_keep = [gate_up_blocks(y, *span) for span in spans]
    gu_core = [swap_core(v) for v in gu_keep]
    gu_y = [swap_y(gu_send[0])]
    own, gu_y[0], *gu_core = lax.optimization_barrier((own, gu_y[0], *gu_core))

    own_x, own_y = swap_x(own), swap_y(own)
    gu_yc = [swap_core(gu_y[0])]
    own_x, own_y, gu_yc[0], gu_send[1] = lax.optimization_barrier((own_x, own_y, gu_yc[0], gu_send[1]))
    own_xy = swap_x(own_y)
    gu_y.append(swap_y(gu_send[1]))

    def gate_up(span, mine, other):
        weights = (gu_keep[span], gu_core[span], gu_y[span], gu_yc[span])
        columns = weights[0].shape[0] * 2 * unit
        held = [pl.BlockSpec((None,) + mine.shape[1:], lambda n, k=k: (k, 0, 0)) for k in range(n_dp)]
        outs = pl.pallas_call(
            functools.partial(gate_up_kernel, n_dp),
            grid=(1,),
            out_shape=[jax.ShapeDtypeStruct((2, rows, columns), BF)] * n_dp,
            in_specs=[SMEM] + held * 2 + [WHOLE] * 4,
            out_specs=[WHOLE] * n_dp,
            compiler_params=PARAMS,
            cost_estimate=LIGHT,
        )(where, *[mine] * n_dp, *[other] * n_dp, *weights)
        return list(outs)

    def ring_step(parts, run, k):
        return (parts[k].astype(F32) + shift(run, 1).astype(F32)).astype(BF)

    def hidden_of(parts, gots):
        return pl.pallas_call(
            functools.partial(hidden_kernel, len(parts)),
            out_shape=jax.ShapeDtypeStruct((2, rows, half), BF),
            in_specs=[WHOLE] * (2 * len(parts)),
            out_specs=WHOLE,
            compiler_params=PARAMS,
            cost_estimate=LIGHT,
        )(*[p[0] for p in parts], *gots)

    near0 = gate_up(0, own, own_x)
    run_near0 = near0[1]
    for k in range(2, n_dp):
        run_near0 = ring_step(near0, run_near0, k)
    own_xy, run_near0 = lax.optimization_barrier((own_xy, run_near0))
    got_near0 = shift(run_near0, 1)
    away0 = gate_up(0, own_y, own_xy)
    run_away0 = ring_step(away0, away0[1], 2)
    gu_y[1], run_away0, got_near0 = lax.optimization_barrier((gu_y[1], run_away0, got_near0))
    gu_yc.append(swap_core(gu_y[1]))
    for k in range(3, n_dp):
        run_away0 = ring_step(away0, run_away0, k)
    got_away0 = shift(run_away0, 1)
    near1, away1 = gate_up(1, own, own_x), gate_up(1, own_y, own_xy)
    run_near1, run_away1 = near1[1], away1[1]
    for k in range(2, n_dp):
        run_away1 = ring_step(away1, run_away1, k)
        run_near1 = ring_step(near1, run_near1, k)
    hidden_away = hidden_of([away0, away1], [got_away0, shift(run_away1, 1)])
    hidden_near = hidden_of([near0, near1], [got_near0, shift(run_near1, 1)])

    down_send, _ = lax.optimization_barrier((cut(down_weight, 1 - y), gu_y[1]))
    down_y = swap_y(down_send)
    down_keep = cut(down_weight, y)
    down_core = swap_core(down_keep)
    down_yc = swap_core(down_y)

    def down(mine, hidden):
        held = [pl.BlockSpec((None,) + mine.shape[1:], lambda n, k=k: (k, 0, 0)) for k in range(n_dp)]
        return pl.pallas_call(
            functools.partial(down_kernel, n_dp),
            grid=(1,),
            out_shape=[jax.ShapeDtypeStruct((n_dp, rows, 2 * width), BF)] * 2,
            in_specs=[SMEM] + held + [WHOLE] * (n_dp + 4),
            out_specs=[WHOLE] * 2,
            compiler_params=PARAMS,
            cost_estimate=LIGHT,
        )(where, *[mine] * n_dp, *hidden, down_keep, down_core, down_y, down_yc)

    def gather_dp(v):
        return [v] + [shift(v, k) for k in range(1, n_dp)]

    hidden_away = gather_dp(hidden_away)
    hidden_near, *hidden_away = lax.optimization_barrier((hidden_near, *hidden_away))
    hidden_near = gather_dp(hidden_near)
    away_y, away_xy = down(own_y, hidden_away)
    near_mine, near_x = down(own, hidden_near)
    total = near_mine.astype(F32) + swap_y(away_y).astype(F32) + swap_xy(away_xy).astype(F32)
    total = (total + swap_x(near_x).astype(F32)).astype(BF)
    back = [total[0]] + [shift(total[k], -k) for k in range(1, n_dp)]
    return pl.pallas_call(
        place_kernel,
        out_shape=jax.ShapeDtypeStruct(tokens.shape, BF),
        in_specs=[SMEM] + [WHOLE] * n_dp,
        out_specs=WHOLE,
        compiler_params=PARAMS,
        cost_estimate=LIGHT,
    )(where, *back)


def solution(mesh):
    in_specs = (
        P(("expert", "dp"), "tensor"),
        P(("expert", "dp"), None),
        P(("expert", "dp"), None),
        P(("expert", "dp")),
        P(None, ("expert", "dp"), "tensor"),
        P(None, ("expert", "dp"), "tensor"),
        P(None, ("expert", "dp"), "tensor"),
    )
    out_specs = P(("expert", "dp"), "tensor")
    plan = stationary_plan if mesh.shape["expert"] == 4 and mesh.shape["tensor"] == 2 else gathered_plan
    return jax.shard_map(plan, mesh=mesh, in_specs=in_specs, out_specs=out_specs, check_vma=False)
```

time: 219 us -> 190 us (0.87)
  blocking collectives: 29.5 us -> 0 us
  waiting for transfers between devices: 128 us -> 125 us
  local copies, waits for them, and re-layouts: 2.79 us -> 5.35 us
    ppermute x4 -> x5, waiting for transfers between devices: 45.4 us -> 13.9 us  [swap_y(): return lax.ppermute(v, 'expert', [(0, 2), (2, 0), (1, 3), (3, 1)])]
    all_gather x1 -> x0, blocking collectives: 29.5 us -> none  [stationary_plan(): metas = lax.all_gather(meta.T, ('expert', 'dp'), axis=0).transpose(0, 2, 1)]
    ppermute x18 -> x24, waiting for transfers between devices: 81 us -> 95.5 us  [shift(): return lax.ppermute(v, 'dp', [(i, (i + k) % n_dp) for i in range(n_dp)])]
    ppermute x2 -> x3, waiting for transfers between devices: 0.51 us -> 13.3 us  [swap_x(): return lax.ppermute(v, 'tensor', [(0, 1), (1, 0)])]
    ppermute x2 -> x1, starting transfers between devices: 4.7 us -> 0.55 us  [swap_xy(): return lax.ppermute(v, ('expert', 'tensor'), pairs)]
    dynamic_slice x0 -> x1, local copies, waits for them, and re-layouts: none -> 3.03 us  [block(): lax.dynamic_slice_in_dim(w, start, unit, axis=2)]
    ppermute x4 -> x6, waiting for transfers between devices: 0.01 us -> 2.52 us  [swap_core(): return lax.ppermute(v, 'expert', [(0, 1), (1, 0), (2, 3), (3, 2)])]
    ppermute x18 -> x24, starting transfers between devices: 22.7 us -> 23.8 us  [shift(): return lax.ppermute(v, 'dp', [(i, (i + k) % n_dp) for i in range(n_dp)])]
  transfers between devices with their start and end apart: 30 -> 39, of which waited for: 17 -> 25; matrix products, arithmetic and copies ran while one was open for 1% -> 1% of each run, Pallas kernels for 9% -> 9%
where the time goes in v2:
time: 190 us
  waiting for transfers between devices  125 us (66%)
  starting transfers between devices  35.3 us (19%)
  Pallas kernels  20.6 us (11%)
  local copies, waits for them, and re-layouts  5.35 us (3%)
  other arithmetic  2.5 us (1%)
    ppermute x24, waiting for transfers between devices, shift(): return lax.ppermute(v, 'dp', [(i, (i + k) % n_dp) for i in range(n_dp)])  95.5 us
    ppermute x24, starting transfers between devices, shift(): return lax.ppermute(v, 'dp', [(i, (i + k) % n_dp) for i in range(n_dp)])  23.8 us
    ppermute x5, waiting for transfers between devices, swap_y(): return lax.ppermute(v, 'expert', [(0, 2), (2, 0), (1, 3), (3, 1)])  13.9 us
    ppermute x3, waiting for transfers between devices, swap_x(): return lax.ppermute(v, 'tensor', [(0, 1), (1, 0)])  13.3 us
    pallas_call x4, Pallas kernels, gate_up(): pl.pallas_call(functools.partial(gate_up_kernel, n_dp), grid=(1,), out_sh...  11 us
    ppermute x5, starting transfers between devices, swap_y(): return lax.ppermute(v, 'expert', [(0, 2), (2, 0), (1, 3), (3, 1)])  7.28 us
    pallas_call x2, Pallas kernels, down(): pl.pallas_call(functools.partial(down_kernel, n_dp), grid=(1,), out_shape...  7.2 us
  transfers between devices with their start and end apart: 39, of which 25 were waited for; matrix products, arithmetic and copies ran while one was open for 1% of the time, Pallas kernels for 9%

profile of v2, /device:TPU:0, one launch (start us, length us, event | category | flops | bytes accessed | tf_op | source)
XLA Modules:
  0.0 190.0 jit_solution(1449995570624232408)
XLA Ops:
  0.0 3.0 %constant_dynamic-slice_fusion.4 = (bf16[4,256,128]{2,1,0:T(8,128)(2,1)}, bf16[4,256,128]{2,1,0:T(8,128)(2,1)S(1)}, bf16[4,256,128]{2,1,0:T(8,128)(2,1)S(1)}, bf...) fusion(bf16[4,256,768]{2,1,0:T(8,128)(2,1)} %param.12, ...), kind=kLoop, calls=%fused_computation.26 | loop fusion | bytes 6291480 | tf_op jit(solution)/shard_map/dynamic_slice | solution.py:227
  7.6 3.0 %collective-permute-start.3 = (bf16[1,4,256,256]{3,2,1,0:T(8,128)(2,1)S(1)}, bf16[1,4,256,256]{3,2,1,0:T(8,128)(2,1)S(1)}, u32[]{:S(2)}, u32[]{:S(2)}) collective-permute-start(bf16[1,4,256,256]{3,2,1,0:T(8,128)(2,1)S(1)} %maximum_bitcast_fusion), channel_id=1, source_target_pairs={{0,16},{16,0},{8,24},{24,8},{1,17},{17,1},{9,25},{25,9},{2,18},{18... | collective-permute-start | bytes 1572872 | tf_op jit(solution)/shard_map/ppermute | solution.py:190
  10.6 3.6 %collective-permute-start.2 = (bf16[144,512]{1,0:T(8,128)(2,1)S(1)}, bf16[144,512]{1,0:T(8,128)(2,1)S(1)}, u32[]{:S(2)}, u32[]{:S(2)}) collective-permute-start(bf16[144,512]{1,0:T(8,128)(2,1)S(1)} %get-tuple-element.52), channel_id=1, source_target_pairs={{0,3},{1,0},{2,1},{3,2},{4,7},{5,4},{6,5},{7,6},{8,11},{9,8},{10,9... | collective-permute-start | bytes 442376 | tf_op jit(solution)/shard_map/ppermute | solution.py:203
  14.2 4.3 %collective-permute-done.2 = bf16[144,512]{1,0:T(8,128)(2,1)S(1)} collective-permute-done((bf16[144,512]{1,0:T(8,128)(2,1)S(1)}, bf16[144,512]{1,0:T(8,128)(2,1)S(1)}, u32[]{:S(2)}, u32[]{:S(2)}) %collective-permute-start.2) | collective-permute-done | bytes 147488 | tf_op jit(solution)/shard_map/ppermute | solution.py:203
  18.7 2.9 %collective-permute-done = bf16[144,512]{1,0:T(8,128)(2,1)S(1)} collective-permute-done((bf16[144,512]{1,0:T(8,128)(2,1)S(1)}, bf16[144,512]{1,0:T(8,128)(2,1)S(1)}, u32[]{:S(2)}, u32[]{:S(2)}) %collective-permute-start) | collective-permute-done | bytes 147488 | tf_op jit(solution)/shard_map/ppermute | solution.py:203
  21.7 6.0 %collective-permute-done.1 = bf16[144,512]{1,0:T(8,128)(2,1)S(1)} collective-permute-done((bf16[144,512]{1,0:T(8,128)(2,1)S(1)}, bf16[144,512]{1,0:T(8,128)(2,1)S(1)}, u32[]{:S(2)}, u32[]{:S(2)}) %collective-permute-start.1) | collective-permute-done | bytes 147488 | tf_op jit(solution)/shard_map/ppermute | solution.py:203
  31.7 11.3 %collective-permute-done.6.refs_4_.refs_5_.refs_6_.refs_7_ = bf16[4,144,512]{2,1,0:T(8,128)(2,1)S(1)} collective-permute-done((bf16[4,144,512]{2,1,0:T(8,128)(2,1)S(1)}, bf16[4,144,512]{2,1,0:T(8,128)(2,1)S(1)}, u32[]{:S(2)}, u32[]{:S(2)}) %collective-permute-start.6) | collective-permute-done | bytes 589856 | tf_op jit(solution)/shard_map/ppermute | solution.py:196
  47.3 5.6 %collective-permute-done.11 = bf16[2,128,256]{2,1,0:T(8,128)(2,1)S(1)} collective-permute-done((bf16[2,128,256]{2,1,0:T(8,128)(2,1)S(1)}, bf16[2,128,256]{2,1,0:T(8,128)(2,1)S(1)}, u32[]{:S(2)}, u32[]{:S(2)}) %collective-permute-start.11) | collective-permute-done | bytes 131104 | tf_op jit(solution)/shard_map/ppermute | solution.py:203
  53.1 6.8 %collective-permute-done.12 = bf16[2,128,256]{2,1,0:T(8,128)(2,1)S(1)} collective-permute-done((bf16[2,128,256]{2,1,0:T(8,128)(2,1)S(1)}, bf16[2,128,256]{2,1,0:T(8,128)(2,1)S(1)}, u32[]{:S(2)}, u32[]{:S(2)}) %collective-permute-start.12) | collective-permute-done | bytes 131104 | tf_op jit(solution)/shard_map/ppermute | solution.py:203
  63.6 5.7 %collective-permute-done.13 = bf16[2,128,256]{2,1,0:T(8,128)(2,1)S(1)} collective-permute-done((bf16[2,128,256]{2,1,0:T(8,128)(2,1)S(1)}, bf16[2,128,256]{2,1,0:T(8,128)(2,1)S(1)}, u32[]{:S(2)}, u32[]{:S(2)}) %collective-permute-start.13) | collective-permute-done | bytes 131104 | tf_op jit(solution)/shard_map/ppermute | solution.py:203
  74.4 3.6 %shard_map.78 = (bf16[2,128,512]{2,1,0:T(8,128)(2,1)S(1)}, bf16[2,128,512]{2,1,0:T(8,128)(2,1)S(1)}, bf16[2,128,512]{2,1,0:T(8,128)(2,1)S(1)}, bf16[2,128,512]{2,1,0:T(8,128)(2,1)S(1)}) custom-call(s32[4]{0:T(128)S(1)} %pad_add_fusion.where_ref, bf16[4,144,512]{2,1,0:T(8,128)(2,1)S(1)} %collective-permute-done.7.refs_0_.refs_1_.refs_2_.refs_3_, ...), custom_call_target="tpu_custom_call" | custom-call | flops 1 | bytes 1 | tf_op jit(solution)/shard_map/pallas_call | solution.py:251
  78.1 3.7 %shard_map.76 = (bf16[2,128,512]{2,1,0:T(8,128)(2,1)S(1)}, bf16[2,128,512]{2,1,0:T(8,128)(2,1)S(1)}, bf16[2,128,512]{2,1,0:T(8,128)(2,1)S(1)}, bf16[2,128,512]{2,1,0:T(8,128)(2,1)S(1)}) custom-call(s32[4]{0:T(128)S(1)} %pad_add_fusion.where_ref, bf16[4,144,512]{2,1,0:T(8,128)(2,1)S(1)} %pad_maximum_fusion.2.refs_0_.refs_1_.refs_2_.refs_3_, ...), custom_call_target="tpu_custom_call" | custom-call | flops 1 | bytes 1 | tf_op jit(solution)/shard_map/pallas_call | solution.py:251
  83.2 5.8 %collective-permute-done.21 = bf16[2,128,512]{2,1,0:T(8,128)(2,1)S(1)} collective-permute-done((bf16[2,128,512]{2,1,0:T(8,128)(2,1)S(1)}, bf16[2,128,512]{2,1,0:T(8,128)(2,1)S(1)}, u32[]{:S(2)}, u32[]{:S(2)}) %collective-permute-start.21) | collective-permute-done | bytes 262176 | tf_op jit(solution)/shard_map/ppermute | solution.py:203
  89.1 5.5 %collective-permute-done.16 = bf16[2,128,512]{2,1,0:T(8,128)(2,1)S(1)} collective-permute-done((bf16[2,128,512]{2,1,0:T(8,128)(2,1)S(1)}, bf16[2,128,512]{2,1,0:T(8,128)(2,1)S(1)}, u32[]{:S(2)}, u32[]{:S(2)}) %collective-permute-start.16) | collective-permute-done | bytes 262176 | tf_op jit(solution)/shard_map/ppermute | solution.py:203
  95.4 4.8 %collective-permute-done.22 = bf16[2,128,512]{2,1,0:T(8,128)(2,1)S(1)} collective-permute-done((bf16[2,128,512]{2,1,0:T(8,128)(2,1)S(1)}, bf16[2,128,512]{2,1,0:T(8,128)(2,1)S(1)}, u32[]{:S(2)}, u32[]{:S(2)}) %collective-permute-start.22) | collective-permute-done | bytes 262176 | tf_op jit(solution)/shard_map/ppermute | solution.py:203
  100.4 5.5 %collective-permute-done.17 = bf16[2,128,512]{2,1,0:T(8,128)(2,1)S(1)} collective-permute-done((bf16[2,128,512]{2,1,0:T(8,128)(2,1)S(1)}, bf16[2,128,512]{2,1,0:T(8,128)(2,1)S(1)}, u32[]{:S(2)}, u32[]{:S(2)}) %collective-permute-start.17) | collective-permute-done | bytes 262176 | tf_op jit(solution)/shard_map/ppermute | solution.py:203
  108.8 13.1 %collective-permute-done.20.refs_2_ = bf16[2,128,256]{2,1,0:T(8,128)(2,1)S(1)} collective-permute-done((bf16[2,128,256]{2,1,0:T(8,128)(2,1)S(1)}, bf16[2,128,256]{2,1,0:T(8,128)(2,1)S(1)}, u32[]{:S(2)}, u32[]{:S(2)}) %collective-permute-start.20) | collective-permute-done | bytes 131104 | tf_op jit(solution)/shard_map/ppermute | solution.py:203
  126.2 5.7 %collective-permute-done.24.refs_5_ = bf16[2,128,384]{2,1,0:T(8,128)(2,1)S(1)} collective-permute-done((bf16[2,128,384]{2,1,0:T(8,128)(2,1)S(1)}, bf16[2,128,384]{2,1,0:T(8,128)(2,1)S(1)}, u32[]{:S(2)}, u32[]{:S(2)}) %collective-permute-start.24) | collective-permute-done | bytes 196640 | tf_op jit(solution)/shard_map/ppermute | solution.py:203
  131.9 6.8 %collective-permute-done.25.refs_6_ = bf16[2,128,384]{2,1,0:T(8,128)(2,1)S(1)} collective-permute-done((bf16[2,128,384]{2,1,0:T(8,128)(2,1)S(1)}, bf16[2,128,384]{2,1,0:T(8,128)(2,1)S(1)}, u32[]{:S(2)}, u32[]{:S(2)}) %collective-permute-start.25) | collective-permute-done | bytes 196640 | tf_op jit(solution)/shard_map/ppermute | solution.py:203
  138.7 5.9 %collective-permute-start.27 = (bf16[2,128,384]{2,1,0:T(8,128)(2,1)S(1)}, bf16[2,128,384]{2,1,0:T(8,128)(2,1)S(1)}, u32[]{:S(2)}, u32[]{:S(2)}) collective-permute-start(bf16[2,128,384]{2,1,0:T(8,128)(2,1)S(1)} %shard_map.77.refs_4_), channel_id=1, source_target_pairs={{0,1},{1,2},{2,3},{3,0},{4,5},{5,6},{6,7},{7,4},{8,9},{9,10},{10,1... | collective-permute-start | bytes 589832 | tf_op jit(solution)/shard_map/ppermute | solution.py:203
  147.0 3.6 %shard_map.81 = (bf16[4,128,512]{2,1,0:T(8,128)(2,1)S(1)}, bf16[4,128,512]{2,1,0:T(8,128)(2,1)S(1)}) custom-call(s32[4]{0:T(128)S(1)} %pad_add_fusion.where_ref, bf16[4,144,512]{2,1,0:T(8,128)(2,1)S(1)} %collective-permute-done.7.refs_0_.refs_1_.refs_2_.refs_3_, bf16[4,144,512]{2,1,0:T(8,128)(2,1)S(1)} %collective-permute-done.7.refs_0_.refs_1_.refs_2_.refs_3_, ...), custom_call_target="tpu_custom_call" | custom-call | flops 1 | bytes 1 | tf_op jit(solution)/shard_map/pallas_call | solution.py:304
  155.2 3.6 %shard_map.80 = (bf16[4,128,512]{2,1,0:T(8,128)(2,1)S(1)}, bf16[4,128,512]{2,1,0:T(8,128)(2,1)S(1)}) custom-call(s32[4]{0:T(128)S(1)} %pad_add_fusion.where_ref, bf16[4,144,512]{2,1,0:T(8,128)(2,1)S(1)} %pad_maximum_fusion.2.refs_0_.refs_1_.refs_2_.refs_3_, bf16[4,144,512]{2,1,0:T(8,128)(2,1)S(1)} %pad_maximum_fusion.2.refs_0_.refs_1_.refs_2_.refs_3_, ...), custom_call_target="tpu_custom_call" | custom-call | flops 1 | bytes 1 | tf_op jit(solution)/shard_map/pallas_call | solution.py:304
  159.5 12.7 %collective-permute-done.33 = bf16[4,128,512]{2,1,0:T(8,128)(2,1)S(1)} collective-permute-done((bf16[4,128,512]{2,1,0:T(8,128)(2,1)S(1)}, bf16[4,128,512]{2,1,0:T(8,128)(2,1)S(1)}, u32[]{:S(2)}, u32[]{:S(2)}) %collective-permute-start.33) | collective-permute-done | bytes 524320 | tf_op jit(solution)/shard_map/ppermute | solution.py:190
  179.9 8.7 %collective-permute-done.37.refs_2_ = bf16[128,512]{1,0:T(8,128)(2,1)S(1)} collective-permute-done((bf16[128,512]{1,0:T(8,128)(2,1)S(1)}, bf16[128,512]{1,0:T(8,128)(2,1)S(1)}, u32[]{:S(2)}, u32[]{:S(2)}) %collective-permute-start.37) | collective-permute-done | bytes 131104 | tf_op jit(solution)/shard_map/ppermute | solution.py:203
  (104 shorter events, 47.6 us)
Async XLA Ops:
  3.3 24.4 %collective-permute-start.5 = (bf16[2,4,256,256]{3,2,1,0:T(8,128)(2,1)S(1)}, bf16[2,4,256,256]{3,2,1,0:T(8,128)(2,1)S(1)}, u32[]{:S(2)}, u32[]{:S(2)}) collective-permute-start(bf16[2,4,256,256]{3,2,1,0:T(8,128)(2,1)S(1)} %pad_maximum_fusion.refs_8_), channel_id=1, source_target_pairs={{0,8},{8,0},{16,24},{24,16},{1,9},{9,1},{17,25},{25,17},{2,10},{10... | collective-permute-start | bytes 3145736 | tf_op jit(solution)/shard_map/ppermute | solution.py:193
  3.9 23.8 %collective-permute-start.4 = (bf16[1,4,256,256]{3,2,1,0:T(8,128)(2,1)S(1)}, bf16[1,4,256,256]{3,2,1,0:T(8,128)(2,1)S(1)}, u32[]{:S(2)}, u32[]{:S(2)}) collective-permute-start(bf16[1,4,256,256]{3,2,1,0:T(8,128)(2,1)S(1)} %maximum_bitcast_fusion.1.refs_8_), channel_id=1, source_target_pairs={{0,8},{8,0},{16,24},{24,16},{1,9},{9,1},{17,25},{25,17},{2,10},{10... | collective-permute-start | bytes 1572872 | tf_op jit(solution)/shard_map/ppermute | solution.py:193
  7.6 20.1 %collective-permute-start.3 = (bf16[1,4,256,256]{3,2,1,0:T(8,128)(2,1)S(1)}, bf16[1,4,256,256]{3,2,1,0:T(8,128)(2,1)S(1)}, u32[]{:S(2)}, u32[]{:S(2)}) collective-permute-start(bf16[1,4,256,256]{3,2,1,0:T(8,128)(2,1)S(1)} %maximum_bitcast_fusion), channel_id=1, source_target_pairs={{0,16},{16,0},{8,24},{24,8},{1,17},{17,1},{9,25},{25,9},{2,18},{18... | collective-permute-start | bytes 1572872 | tf_op jit(solution)/shard_map/ppermute | solution.py:190
  27.7 15.3 %collective-permute-start.6 = (bf16[4,144,512]{2,1,0:T(8,128)(2,1)S(1)}, bf16[4,144,512]{2,1,0:T(8,128)(2,1)S(1)}, u32[]{:S(2)}, u32[]{:S(2)}) collective-permute-start(bf16[4,144,512]{2,1,0:T(8,128)(2,1)S(1)} %pad_maximum_fusion.2.refs_0_.refs_1_.refs_2_.refs_3_), channel_id=1, source_target_pairs={{0,4},{4,0},{1,5},{5,1},{2,6},{6,2},{3,7},{7,3},{8,12},{12,8},{9,1... | collective-permute-start | bytes 1769480 | tf_op jit(solution)/shard_map/ppermute | solution.py:196
  29.3 15.0 %collective-permute-start.7 = (bf16[4,144,512]{2,1,0:T(8,128)(2,1)S(1)}, bf16[4,144,512]{2,1,0:T(8,128)(2,1)S(1)}, u32[]{:S(2)}, u32[]{:S(2)}) collective-permute-start(bf16[4,144,512]{2,1,0:T(8,128)(2,1)S(1)} %pad_maximum_fusion.2.refs_0_.refs_1_.refs_2_.refs_3_), channel_id=1, source_target_pairs={{0,16},{16,0},{8,24},{24,8},{1,17},{17,1},{9,25},{25,9},{2,18},{18... | collective-permute-start | bytes 1769480 | tf_op jit(solution)/shard_map/ppermute | solution.py:190
  46.2 24.5 %collective-permute-start.9 = (bf16[2,4,256,256]{3,2,1,0:T(8,128)(2,1)S(1)}, bf16[2,4,256,256]{3,2,1,0:T(8,128)(2,1)S(1)}, u32[]{:S(2)}, u32[]{:S(2)}) collective-permute-start(bf16[2,4,256,256]{3,2,1,0:T(8,128)(2,1)S(1)} %pad_maximum_fusion.1), channel_id=1, source_target_pairs={{0,16},{16,0},{8,24},{24,8},{1,17},{17,1},{9,25},{25,9},{2,18},{18... | collective-permute-start | bytes 3145736 | tf_op jit(solution)/shard_map/ppermute | solution.py:190
  46.8 13.8 %collective-permute-start.10 = (bf16[4,144,512]{2,1,0:T(8,128)(2,1)S(1)}, bf16[4,144,512]{2,1,0:T(8,128)(2,1)S(1)}, u32[]{:S(2)}, u32[]{:S(2)}) collective-permute-start(bf16[4,144,512]{2,1,0:T(8,128)(2,1)S(1)} %collective-permute-done.7.refs_0_.refs_1_.refs_2_.refs_3_), channel_id=1, source_target_pairs={{0,4},{4,0},{1,5},{5,1},{2,6},{6,2},{3,7},{7,3},{8,12},{12,8},{9,1... | collective-permute-start | bytes 1769480 | tf_op jit(solution)/shard_map/ppermute | solution.py:196
  70.9 24.3 %collective-permute-start.31 = (bf16[4,256,384]{2,1,0:T(8,128)(2,1)S(1)}, bf16[4,256,384]{2,1,0:T(8,128)(2,1)S(1)}, u32[]{:S(2)}, u32[]{:S(2)}) collective-permute-start(bf16[4,256,384]{2,1,0:T(8,128)(2,1)S(1)} %get-tuple-element.84), channel_id=1, source_target_pairs={{0,16},{16,0},{8,24},{24,8},{1,17},{17,1},{9,25},{25,9},{2,18},{18... | collective-permute-start | bytes 2359304 | tf_op jit(solution)/shard_map/ppermute | solution.py:190
  81.7 12.9 %collective-permute-start.16 = (bf16[2,128,512]{2,1,0:T(8,128)(2,1)S(1)}, bf16[2,128,512]{2,1,0:T(8,128)(2,1)S(1)}, u32[]{:S(2)}, u32[]{:S(2)}) collective-permute-start(bf16[2,128,512]{2,1,0:T(8,128)(2,1)S(1)} %get-tuple-element.75), channel_id=1, source_target_pairs={{0,1},{1,2},{2,3},{3,0},{4,5},{5,6},{6,7},{7,4},{8,9},{9,10},{10,1... | collective-permute-start | bytes 786440 | tf_op jit(solution)/shard_map/ppermute | solution.py:203
  89.1 11.2 %collective-permute-start.22 = (bf16[2,128,512]{2,1,0:T(8,128)(2,1)S(1)}, bf16[2,128,512]{2,1,0:T(8,128)(2,1)S(1)}, u32[]{:S(2)}, u32[]{:S(2)}) collective-permute-start(bf16[2,128,512]{2,1,0:T(8,128)(2,1)S(1)} %add_convert_fusion.2), channel_id=1, source_target_pairs={{0,1},{1,2},{2,3},{3,0},{4,5},{5,6},{6,7},{7,4},{8,9},{9,10},{10,1... | collective-permute-start | bytes 786440 | tf_op jit(solution)/shard_map/ppermute | solution.py:203
  94.7 11.2 %collective-permute-start.17 = (bf16[2,128,512]{2,1,0:T(8,128)(2,1)S(1)}, bf16[2,128,512]{2,1,0:T(8,128)(2,1)S(1)}, u32[]{:S(2)}, u32[]{:S(2)}) collective-permute-start(bf16[2,128,512]{2,1,0:T(8,128)(2,1)S(1)} %add_convert_fusion.4), channel_id=1, source_target_pairs={{0,1},{1,2},{2,3},{3,0},{4,5},{5,6},{6,7},{7,4},{8,9},{9,10},{10,1... | collective-permute-start | bytes 786440 | tf_op jit(solution)/shard_map/ppermute | solution.py:203
  94.8 52.2 %collective-permute-start.30 = (bf16[4,256,384]{2,1,0:T(8,128)(2,1)S(1)}, bf16[4,256,384]{2,1,0:T(8,128)(2,1)S(1)}, u32[]{:S(2)}, u32[]{:S(2)}) collective-permute-start(bf16[4,256,384]{2,1,0:T(8,128)(2,1)S(1)} %get-tuple-element.94.refs_8_), channel_id=1, source_target_pairs={{0,8},{8,0},{16,24},{24,16},{1,9},{9,1},{17,25},{25,17},{2,10},{10... | collective-permute-start | bytes 2359304 | tf_op jit(solution)/shard_map/ppermute | solution.py:193
  94.8 13.8 %collective-permute-start.19 = (bf16[2,128,256]{2,1,0:T(8,128)(2,1)S(1)}, bf16[2,128,256]{2,1,0:T(8,128)(2,1)S(1)}, u32[]{:S(2)}, u32[]{:S(2)}) collective-permute-start(bf16[2,128,256]{2,1,0:T(8,128)(2,1)S(1)} %add_convert_fusion.6), channel_id=1, source_target_pairs={{0,1},{1,2},{2,3},{3,0},{4,5},{5,6},{6,7},{7,4},{8,9},{9,10},{10,1... | collective-permute-start | bytes 393224 | tf_op jit(solution)/shard_map/ppermute | solution.py:203
  95.2 51.8 %collective-permute-start.32 = (bf16[4,256,384]{2,1,0:T(8,128)(2,1)S(1)}, bf16[4,256,384]{2,1,0:T(8,128)(2,1)S(1)}, u32[]{:S(2)}, u32[]{:S(2)}) collective-permute-start(bf16[4,256,384]{2,1,0:T(8,128)(2,1)S(1)} %collective-permute-done.31.refs_10_), channel_id=1, source_target_pairs={{0,8},{8,0},{16,24},{24,16},{1,9},{9,1},{17,25},{25,17},{2,10},{10... | collective-permute-start | bytes 2359304 | tf_op jit(solution)/shard_map/ppermute | solution.py:193
  100.3 21.6 %collective-permute-start.23 = (bf16[2,128,512]{2,1,0:T(8,128)(2,1)S(1)}, bf16[2,128,512]{2,1,0:T(8,128)(2,1)S(1)}, u32[]{:S(2)}, u32[]{:S(2)}) collective-permute-start(bf16[2,128,512]{2,1,0:T(8,128)(2,1)S(1)} %add_convert_fusion.1), channel_id=1, source_target_pairs={{0,1},{1,2},{2,3},{3,0},{4,5},{5,6},{6,7},{7,4},{8,9},{9,10},{10,1... | collective-permute-start | bytes 786440 | tf_op jit(solution)/shard_map/ppermute | solution.py:203
  105.9 18.0 %collective-permute-start.18 = (bf16[2,128,512]{2,1,0:T(8,128)(2,1)S(1)}, bf16[2,128,512]{2,1,0:T(8,128)(2,1)S(1)}, u32[]{:S(2)}, u32[]{:S(2)}) collective-permute-start(bf16[2,128,512]{2,1,0:T(8,128)(2,1)S(1)} %add_convert_fusion.3), channel_id=1, source_target_pairs={{0,1},{1,2},{2,3},{3,0},{4,5},{5,6},{6,7},{7,4},{8,9},{9,10},{10,1... | collective-permute-start | bytes 786440 | tf_op jit(solution)/shard_map/ppermute | solution.py:203
  108.7 13.2 %collective-permute-start.20 = (bf16[2,128,256]{2,1,0:T(8,128)(2,1)S(1)}, bf16[2,128,256]{2,1,0:T(8,128)(2,1)S(1)}, u32[]{:S(2)}, u32[]{:S(2)}) collective-permute-start(bf16[2,128,256]{2,1,0:T(8,128)(2,1)S(1)} %add_convert_fusion.5), channel_id=1, source_target_pairs={{0,1},{1,2},{2,3},{3,0},{4,5},{5,6},{6,7},{7,4},{8,9},{9,10},{10,1... | collective-permute-start | bytes 393224 | tf_op jit(solution)/shard_map/ppermute | solution.py:203
  122.2 16.5 %collective-permute-start.25 = (bf16[2,128,384]{2,1,0:T(8,128)(2,1)S(1)}, bf16[2,128,384]{2,1,0:T(8,128)(2,1)S(1)}, u32[]{:S(2)}, u32[]{:S(2)}) collective-permute-start(bf16[2,128,384]{2,1,0:T(8,128)(2,1)S(1)} %shard_map.79.refs_4_), channel_id=1, source_target_pairs={{0,2},{1,3},{2,0},{3,1},{4,6},{5,7},{6,4},{7,5},{8,10},{9,11},{10,... | collective-permute-start | bytes 589832 | tf_op jit(solution)/shard_map/ppermute | solution.py:203
  123.9 14.8 %collective-permute-start.26 = (bf16[2,128,384]{2,1,0:T(8,128)(2,1)S(1)}, bf16[2,128,384]{2,1,0:T(8,128)(2,1)S(1)}, u32[]{:S(2)}, u32[]{:S(2)}) collective-permute-start(bf16[2,128,384]{2,1,0:T(8,128)(2,1)S(1)} %shard_map.79.refs_4_), channel_id=1, source_target_pairs={{0,3},{1,0},{2,1},{3,2},{4,7},{5,4},{6,5},{7,6},{8,11},{9,8},{10,9... | collective-permute-start | bytes 589832 | tf_op jit(solution)/shard_map/ppermute | solution.py:203
  138.7 14.0 %collective-permute-start.27 = (bf16[2,128,384]{2,1,0:T(8,128)(2,1)S(1)}, bf16[2,128,384]{2,1,0:T(8,128)(2,1)S(1)}, u32[]{:S(2)}, u32[]{:S(2)}) collective-permute-start(bf16[2,128,384]{2,1,0:T(8,128)(2,1)S(1)} %shard_map.77.refs_4_), channel_id=1, source_target_pairs={{0,1},{1,2},{2,3},{3,0},{4,5},{5,6},{6,7},{7,4},{8,9},{9,10},{10,1... | collective-permute-start | bytes 589832 | tf_op jit(solution)/shard_map/ppermute | solution.py:203
  150.6 21.6 %collective-permute-start.33 = (bf16[4,128,512]{2,1,0:T(8,128)(2,1)S(1)}, bf16[4,128,512]{2,1,0:T(8,128)(2,1)S(1)}, u32[]{:S(2)}, u32[]{:S(2)}) collective-permute-start(bf16[4,128,512]{2,1,0:T(8,128)(2,1)S(1)} %get-tuple-element.90), channel_id=1, source_target_pairs={{0,16},{16,0},{8,24},{24,8},{1,17},{17,1},{9,25},{25,9},{2,18},{18... | collective-permute-start | bytes 1572872 | tf_op jit(solution)/shard_map/ppermute | solution.py:190
  152.2 20.0 %collective-permute-start.34 = (bf16[4,128,512]{2,1,0:T(8,128)(2,1)S(1)}, bf16[4,128,512]{2,1,0:T(8,128)(2,1)S(1)}, u32[]{:S(2)}, u32[]{:S(2)}) collective-permute-start(bf16[4,128,512]{2,1,0:T(8,128)(2,1)S(1)} %get-tuple-element.91), channel_id=1, source_target_pairs={{0,20},{4,16},{8,28},{12,24},{16,4},{20,0},{24,12},{28,8},{1,21},{... | collective-permute-start | bytes 1572872 | tf_op jit(solution)/shard_map/ppermute | solution.py:200
  158.8 14.6 %collective-permute-start.35 = (bf16[4,128,512]{2,1,0:T(8,128)(2,1)S(1)}, bf16[4,128,512]{2,1,0:T(8,128)(2,1)S(1)}, u32[]{:S(2)}, u32[]{:S(2)}) collective-permute-start(bf16[4,128,512]{2,1,0:T(8,128)(2,1)S(1)} %get-tuple-element.92), channel_id=1, source_target_pairs={{0,4},{4,0},{1,5},{5,1},{2,6},{6,2},{3,7},{7,3},{8,12},{12,8},{9,1... | collective-permute-start | bytes 1572872 | tf_op jit(solution)/shard_map/ppermute | solution.py:196
  175.5 13.1 %collective-permute-start.37 = (bf16[128,512]{1,0:T(8,128)(2,1)S(1)}, bf16[128,512]{1,0:T(8,128)(2,1)S(1)}, u32[]{:S(2)}, u32[]{:S(2)}) collective-permute-start(bf16[128,512]{1,0:T(8,128)(2,1)S(1)} %get-tuple-element.108), channel_id=1, source_target_pairs={{0,2},{1,3},{2,0},{3,1},{4,6},{5,7},{6,4},{7,5},{8,10},{9,11},{10,... | collective-permute-start | bytes 393224 | tf_op jit(solution)/shard_map/ppermute | solution.py:203
  (23 other events, 203.6 us)

commit v3 on v2

--- a/solution.py
+++ b/solution.py
@@ -106,29 +106,33 @@
             out_ref[:, pl.ds(pl.multiple_of(slot, width), width)] = piece[:, j * width : (j + 1) * width]
 
 
-def gate_up_kernel(n_dp, where_ref, *refs):
-    own_refs, far_refs = refs[:n_dp], refs[n_dp : 2 * n_dp]
-    w_refs = refs[2 * n_dp : 2 * n_dp + 4]
-    out_refs = refs[2 * n_dp + 4 :]
+def gate_up_kernel(n, where_ref, *refs):
+    own_refs, far_refs, out_refs = refs[:n], refs[n : 2 * n], refs[-n:]
+    w_refs = refs[2 * n : -n]
     same = where_ref[3] == 1
     rows = own_refs[0].shape[0] - META_ROWS
-    blocks, experts, width, tile = w_refs[0].shape
     own = jnp.concatenate([r[:rows] for r in own_refs], axis=0)
     far = jnp.concatenate([r[:rows] for r in far_refs], axis=0)
     near_x = jnp.where(same, own, far)
     away_x = jnp.where(same, far, own)
-    pieces = (near_x[:, :width], near_x[:, width:], away_x[:, :width], away_x[:, width:])
     route = columns_of(own_refs, rows)[:2]
-    for b in range(blocks):
+    for b in range(len(w_refs) // 6):
+        gate, up, gate_core, up_core, far_w, far_core = w_refs[6 * b : 6 * b + 6]
+        experts, width, unit = gate.shape
         slots = [None, None]
         for e in range(experts):
-            part = sum(jnp.dot(p, w[b, e], preferred_element_type=F32) for p, w in zip(pieces, w_refs))
+            mine = jnp.concatenate([gate[e], up[e]], axis=1)
+            cores = jnp.concatenate([gate_core[e], up_core[e]], axis=1)
+            part = jnp.dot(near_x[:, :width], mine, preferred_element_type=F32)
+            part += jnp.dot(near_x[:, width:], cores, preferred_element_type=F32)
+            part += jnp.dot(away_x[:, :width], far_w[e], preferred_element_type=F32)
+            part += jnp.dot(away_x[:, width:], far_core[e], preferred_element_type=F32)
             for s in range(2):
                 held = jnp.zeros_like(part) if e == 0 else slots[s]
                 slots[s] = jnp.where(route[s] == float(e), part, held)
         for k, out in enumerate(out_refs):
             for s in range(2):
-                out[s, :, b * tile : (b + 1) * tile] = slots[s][k * rows : (k + 1) * rows].astype(BF)
+                out[s, :, 2 * b * unit : 2 * (b + 1) * unit] = slots[s][k * rows : (k + 1) * rows].astype(BF)
 
 
 def hidden_kernel(n_spans, *refs):
@@ -145,25 +149,38 @@
             at += unit
 
 
-def down_kernel(n_blocks, where_ref, *refs):
-    token_refs, h_refs = refs[:n_blocks], refs[n_blocks : 2 * n_blocks]
-    w_refs = refs[2 * n_blocks : 2 * n_blocks + 4]
-    near_out, away_out = refs[2 * n_blocks + 4 :]
+def down_kernel(n, n_parts, first, where_ref, *refs):
+    token_refs = refs[:n]
+    h_refs = refs[n : n * (1 + n_parts)]
+    w_refs = refs[n * (1 + n_parts) : n * (1 + n_parts) + 4]
+    rest = refs[n * (1 + n_parts) + 4 :]
     same = where_ref[3] == 1
     rows = h_refs[0].shape[1]
     experts, width = w_refs[0].shape[0], w_refs[0].shape[1]
     route0, route1, prob0, prob1 = columns_of(token_refs, rows)
-    h0 = jnp.concatenate([h[0] for h in h_refs], axis=0)
-    h1 = jnp.concatenate([h[1] for h in h_refs], axis=0)
+    hidden = [
+        jnp.concatenate(
+            [jnp.concatenate([h_refs[p * n + i][s] for p in range(n_parts)], axis=1) for i in range(n)], axis=0
+        )
+        for s in range(2)
+    ]
     total = [None] * 4
+    if not first:
+        total = [jnp.concatenate([rest[i][:, j * width : (j + 1) * width] for i in range(n)], axis=0) for j in range(4)]
     for e in range(experts):
-        first, second = route0 == float(e), route1 == float(e)
-        h_e = jnp.where(first, h0, jnp.where(second, h1, jnp.zeros_like(h1)))
-        scale = jnp.where(first, prob0, jnp.where(second, prob1, 0.0))
+        one, two = route0 == float(e), route1 == float(e)
+        h_e = jnp.where(one, hidden[0], jnp.where(two, hidden[1], jnp.zeros_like(hidden[1])))
+        scale = jnp.where(one, prob0, jnp.where(two, prob1, 0.0))
         for j in range(4):
             term = scale * lax.dot_general(h_e, w_refs[j][e], (((1,), (1,)), ((), ())), preferred_element_type=F32)
-            total[j] = term if e == 0 else total[j] + term
-    held = [t.astype(BF).reshape(n_blocks, rows, width) for t in total]
+            total[j] = term if total[j] is None else total[j] + term
+    if first:
+        for i in range(n):
+            for j in range(4):
+                rest[i][:, j * width : (j + 1) * width] = total[j][i * rows : (i + 1) * rows]
+        return
+    near_out, away_out = rest[n:]
+    held = [t.astype(BF).reshape(n, rows, width) for t in total]
     for j in range(2):
         cols = slice(j * width, (j + 1) * width)
         near_out[:, :, cols] = jnp.where(same, held[j], held[j + 2])
@@ -178,7 +195,6 @@
 
 def stationary_plan(tokens, routes, gate_prob, token_count, gate_weight, up_weight, down_weight):
     experts, width, share = gate_weight.shape
-    half = share // 2
     rows = tokens.shape[0]
     n_dp = lax.axis_size("dp")
     place = lax.axis_index("expert")
@@ -195,15 +211,8 @@
     def swap_x(v):
         return lax.ppermute(v, "tensor", [(0, 1), (1, 0)])
 
-    def swap_xy(v):
-        pairs = [(e * 2 + t, ((e + 2) % 4) * 2 + 1 - t) for e in range(4) for t in range(2)]
-        return lax.ppermute(v, ("expert", "tensor"), pairs)
-
     def shift(v, k):
         return lax.ppermute(v, "dp", [(i, (i + k) % n_dp) for i in range(n_dp)])
-
-    def cut(weight, which):
-        return lax.dynamic_slice_in_dim(weight, which * half, half, axis=2)
 
     live = jnp.arange(rows)[None, :] < token_count[0]
     slots = jnp.where(live, routes.T, -1).astype(F32)
@@ -216,112 +225,143 @@
         compiler_params=PARAMS,
         cost_estimate=LIGHT,
     )(where, tokens, slots, gate_prob.T)
-    own = jnp.stack([send[0]] + [shift(send[k], k) for k in range(1, n_dp)])
-
-    unit = UNIT
-
-    def gate_up_blocks(which, first, count):
-        def block(n):
-            start = which * half + n * unit
-            return jnp.concatenate(
-                [lax.dynamic_slice_in_dim(w, start, unit, axis=2) for w in (gate_weight, up_weight)], axis=2
-            )
-
-        return jnp.stack([block(n) for n in range(first, first + count)])
-
-    blocks = half // unit
-    spans = [(0, 1), (1, blocks - 1)]
-    gu_send = [gate_up_blocks(1 - y, *span) for span in spans]
-    gu_send[0], _ = lax.optimization_barrier((gu_send[0], send[0]))
-    gu_keep = [gate_up_blocks(y, *span) for span in spans]
-    gu_core = [swap_core(v) for v in gu_keep]
-    gu_y = [swap_y(gu_send[0])]
-    own, gu_y[0], *gu_core = lax.optimization_barrier((own, gu_y[0], *gu_core))
-
-    own_x, own_y = swap_x(own), swap_y(own)
-    gu_yc = [swap_core(gu_y[0])]
-    own_x, own_y, gu_yc[0], gu_send[1] = lax.optimization_barrier((own_x, own_y, gu_yc[0], gu_send[1]))
-    own_xy = swap_x(own_y)
-    gu_y.append(swap_y(gu_send[1]))
-
-    def gate_up(span, mine, other):
-        weights = (gu_keep[span], gu_core[span], gu_y[span], gu_yc[span])
-        columns = weights[0].shape[0] * 2 * unit
-        held = [pl.BlockSpec((None,) + mine.shape[1:], lambda n, k=k: (k, 0, 0)) for k in range(n_dp)]
-        outs = pl.pallas_call(
-            functools.partial(gate_up_kernel, n_dp),
-            grid=(1,),
-            out_shape=[jax.ShapeDtypeStruct((2, rows, columns), BF)] * n_dp,
-            in_specs=[SMEM] + held * 2 + [WHOLE] * 4,
-            out_specs=[WHOLE] * n_dp,
-            compiler_params=PARAMS,
-            cost_estimate=LIGHT,
-        )(where, *[mine] * n_dp, *[other] * n_dp, *weights)
-        return list(outs)
+    def cross_x(v, k):
+        pairs = [(t * n_dp + i, (1 - t) * n_dp + (i + k) % n_dp) for t in range(2) for i in range(n_dp)]
+        return lax.ppermute(v, ("tensor", "dp"), pairs)
+
+    gate_core, up_core = swap_core(gate_weight), swap_core(up_weight)
+    gate_core, up_core, *send = lax.optimization_barrier((gate_core, up_core, *send))
+    own = [send[0]] + [shift(send[k], k) for k in range(1, n_dp)]
+    stacked = swap_x(jnp.stack(own))
+    far = [stacked[k] for k in range(n_dp)]
+
+    blocks = share // UNIT
+
+    def block(weights, n):
+        return jnp.concatenate([w[:, :, n * UNIT : (n + 1) * UNIT] for w in weights], axis=2)
+
+    def gate_up(units, over_y, over_y_core):
+        def call(which):
+            n = len(which)
+            weights, w_specs = [], []
+            for i in units:
+                weights += [gate_weight, up_weight, gate_core, up_core]
+                w_specs += [pl.BlockSpec((experts, width, UNIT), lambda _, i=i: (0, 0, i))] * 4
+                for v in (over_y, over_y_core):
+                    weights.append(v)
+                    w_specs.append(pl.BlockSpec((None,) + v.shape[1:], lambda _, at=i - units[0]: (at, 0, 0, 0)))
+            return pl.pallas_call(
+                functools.partial(gate_up_kernel, n),
+                grid=(1,),
+                out_shape=[jax.ShapeDtypeStruct((2, rows, 2 * len(units) * UNIT), BF)] * n,
+                in_specs=[SMEM] + [WHOLE] * (2 * n) + w_specs,
+                out_specs=[WHOLE] * n,
+                compiler_params=PARAMS,
+                cost_estimate=LIGHT,
+            )(where, *[own[k] for k in which], *[far[k] for k in which], *weights)
+
+        (sent,) = call([1])
+        kept = call([0] + list(range(2, n_dp)))
+        return [kept[0], sent, *kept[1:]]
 
     def ring_step(parts, run, k):
         return (parts[k].astype(F32) + shift(run, 1).astype(F32)).astype(BF)
 
     def hidden_of(parts, gots):
+        columns = sum(p[0].shape[2] for p in parts) // 2
         return pl.pallas_call(
             functools.partial(hidden_kernel, len(parts)),
-            out_shape=jax.ShapeDtypeStruct((2, rows, half), BF),
+            out_shape=jax.ShapeDtypeStruct((2, rows, columns), BF),
             in_specs=[WHOLE] * (2 * len(parts)),
             out_specs=WHOLE,
             compiler_params=PARAMS,
             cost_estimate=LIGHT,
         )(*[p[0] for p in parts], *gots)
 
-    near0 = gate_up(0, own, own_x)
-    run_near0 = near0[1]
-    for k in range(2, n_dp):
-        run_near0 = ring_step(near0, run_near0, k)
-    own_xy, run_near0 = lax.optimization_barrier((own_xy, run_near0))
-    got_near0 = shift(run_near0, 1)
-    away0 = gate_up(0, own_y, own_xy)
-    run_away0 = ring_step(away0, away0[1], 2)
-    gu_y[1], run_away0, got_near0 = lax.optimization_barrier((gu_y[1], run_away0, got_near0))
-    gu_yc.append(swap_core(gu_y[1]))
-    for k in range(3, n_dp):
-        run_away0 = ring_step(away0, run_away0, k)
-    got_away0 = shift(run_away0, 1)
-    near1, away1 = gate_up(1, own, own_x), gate_up(1, own_y, own_xy)
-    run_near1, run_away1 = near1[1], away1[1]
-    for k in range(2, n_dp):
-        run_away1 = ring_step(away1, run_away1, k)
-        run_near1 = ring_step(near1, run_near1, k)
-    hidden_away = hidden_of([away0, away1], [got_away0, shift(run_away1, 1)])
-    hidden_near = hidden_of([near0, near1], [got_near0, shift(run_near1, 1)])
-
-    down_send, _ = lax.optimization_barrier((cut(down_weight, 1 - y), gu_y[1]))
-    down_y = swap_y(down_send)
-    down_keep = cut(down_weight, y)
-    down_core = swap_core(down_keep)
-    down_yc = swap_core(down_y)
-
-    def down(mine, hidden):
-        held = [pl.BlockSpec((None,) + mine.shape[1:], lambda n, k=k: (k, 0, 0)) for k in range(n_dp)]
+    def ring_dp(v):
+        held = [v]
+        for _ in range(1, n_dp):
+            held.append(shift(held[-1], 1))
+        return held
+
+    def gather_dp(v):
+        return [v] + [shift(v, k) for k in range(1, n_dp)]
+
+    bar = lax.optimization_barrier
+    given = (gate_weight, up_weight)
+
+    def pair(n):
+        return jnp.stack([block(given, n), block(given, n + 1)])
+
+    y01 = swap_y(pair(0))
+    own, far, y01, *given = bar((own, far, y01, *given))
+
+    yc01 = swap_core(y01)
+    y23 = swap_y(pair(2))
+    parts0 = gate_up([0, 1], y01, yc01)
+    run0 = ring_step(parts0, parts0[1], 2)
+    run0 = ring_step(parts0, run0, 3)
+    y23, run0, *given = bar((y23, run0, *given))
+
+    yc23 = swap_core(y23)
+    y45 = swap_y(pair(4))
+    got0 = shift(run0, 1)
+    parts1 = gate_up([2, 3], y23, yc23)
+    run1 = ring_step(parts1, parts1[1], 2)
+    hidden0 = gather_dp(hidden_of([parts0], [got0]))
+    run1 = ring_step(parts1, run1, 3)
+    y45, run1, down_from, *hidden0 = bar((y45, run1, down_weight, *hidden0))
+
+    yc45 = swap_core(y45)
+    down_y = swap_y(down_from)
+    got1 = shift(run1, 1)
+    parts2 = gate_up([4, 5], y45, yc45)
+    run2 = ring_step(parts2, parts2[1], 2)
+    hidden1 = ring_dp(hidden_of([parts1], [got1]))
+    run2 = ring_step(parts2, run2, 3)
+    got2 = shift(run2, 1)
+    got2, down_y, down_from, *hidden1 = bar((got2, down_y, down_from, *hidden1))
+    down_core, down_yc = swap_core(down_from), swap_core(down_y)
+    hidden2 = hidden_of([parts2], [got2])
+    hidden2 = gather_dp(hidden2)
+    hidden2[1], down_core, down_yc = bar((hidden2[1], down_core, down_yc))
+
+    down_weights = (down_weight, down_core, down_y, down_yc)
+    late = 2 * UNIT
+    sums = pl.pallas_call(
+        functools.partial(down_kernel, n_dp, 2, True),
+        grid=(1,),
+        out_shape=[jax.ShapeDtypeStruct((rows, 4 * width), F32)] * n_dp,
+        in_specs=[SMEM]
+        + [WHOLE] * (3 * n_dp)
+        + [pl.BlockSpec((experts, width, share - late), lambda _: (0, 0, 0))] * 4,
+        out_specs=[WHOLE] * n_dp,
+        compiler_params=PARAMS,
+        cost_estimate=pl.CostEstimate(flops=6_000_000_000, bytes_accessed=1, transcendentals=0),
+    )(where, *own, *hidden0, *hidden1, *down_weights)
+
+    hidden2[1], hidden2[2], hidden2[3], *sums = bar((hidden2[1], hidden2[2], hidden2[3], *sums))
+
+    def down(which):
+        n = len(which)
+        last = pl.BlockSpec((experts, width, late), lambda _: (0, 0, share // late - 1))
         return pl.pallas_call(
-            functools.partial(down_kernel, n_dp),
+            functools.partial(down_kernel, n, 1, False),
             grid=(1,),
-            out_shape=[jax.ShapeDtypeStruct((n_dp, rows, 2 * width), BF)] * 2,
-            in_specs=[SMEM] + held + [WHOLE] * (n_dp + 4),
+            out_shape=[jax.ShapeDtypeStruct((n, rows, 2 * width), BF)] * 2,
+            in_specs=[SMEM] + [WHOLE] * (2 * n) + [last] * 4 + [WHOLE] * n,
             out_specs=[WHOLE] * 2,
             compiler_params=PARAMS,
             cost_estimate=LIGHT,
-        )(where, *[mine] * n_dp, *hidden, down_keep, down_core, down_y, down_yc)
-
-    def gather_dp(v):
-        return [v] + [shift(v, k) for k in range(1, n_dp)]
-
-    hidden_away = gather_dp(hidden_away)
-    hidden_near, *hidden_away = lax.optimization_barrier((hidden_near, *hidden_away))
-    hidden_near = gather_dp(hidden_near)
-    away_y, away_xy = down(own_y, hidden_away)
-    near_mine, near_x = down(own, hidden_near)
-    total = near_mine.astype(F32) + swap_y(away_y).astype(F32) + swap_xy(away_xy).astype(F32)
-    total = (total + swap_x(near_x).astype(F32)).astype(BF)
-    back = [total[0]] + [shift(total[k], -k) for k in range(1, n_dp)]
+        )(where, *[own[k] for k in which], *[hidden2[k] for k in which], *down_weights, *[sums[k] for k in which])
+
+    back = [None] * n_dp
+    order = list(range(2, n_dp)) + [1, 0]
+    for which in (order[: n_dp // 2], order[n_dp // 2 :]):
+        mine, other = down(which)
+        total = (mine.astype(F32) + swap_x(other).astype(F32)).astype(BF)
+        for i, k in enumerate(which):
+            back[k] = total[i] if k == 0 else shift(total[i], -k)
     return pl.pallas_call(
         place_kernel,
         out_shape=jax.ShapeDtypeStruct(tokens.shape, BF),

time: 190 us -> 184 us (0.968)
  waiting for transfers between devices: 125 us -> 106 us
  Pallas kernels: 20.6 us -> 28.7 us
  starting transfers between devices: 35.3 us -> 39.4 us
    ppermute x24, waiting for transfers between devices: 95.5 us -> 82.8 us  [shift(): return lax.ppermute(v, 'dp', [(i, (i + k) % n_dp) for i in range(n_dp)])]
    ppermute x5 -> x4, waiting for transfers between devices: 13.9 us -> 1.68 us  [swap_y(): return lax.ppermute(v, 'expert', [(0, 2), (2, 0), (1, 3), (3, 1)])]
    pallas_call x6 -> x9, Pallas kernels: 18.2 us -> 26.2 us  [the longest x6 16.1 us: call(): pl.pallas_call(functools.partial(gate_up_kernel, n), grid=(1,), out_shape...]
    ppermute x3, waiting for transfers between devices: 13.3 us -> 18.4 us  [swap_x(): return lax.ppermute(v, 'tensor', [(0, 1), (1, 0)])]
    ppermute x24, starting transfers between devices: 23.8 us -> 28.2 us  [shift(): return lax.ppermute(v, 'dp', [(i, (i + k) % n_dp) for i in range(n_dp)])]
    unnamed x16 -> x24, local copies, waits for them, and re-layouts: 2.07 us -> 5.49 us
    dynamic_slice x2 -> x0, local copies, waits for them, and re-layouts: 3.24 us -> none  [the longest x1 3.03 us: block(): lax.dynamic_slice_in_dim(w, start, unit, axis=2)]
    ppermute x5 -> x4, starting transfers between devices: 7.28 us -> 6.34 us  [swap_y(): return lax.ppermute(v, 'expert', [(0, 2), (2, 0), (1, 3), (3, 1)])]
  transfers between devices with their start and end apart: 39 -> 38, of which waited for: 25 -> 26; matrix products, arithmetic and copies ran while one was open for 1% -> 2% of each run, Pallas kernels for 9% -> 13%
where the time goes in v3:
time: 184 us
  waiting for transfers between devices  106 us (58%)
  starting transfers between devices  39.4 us (21%)
  Pallas kernels  28.7 us (16%)
  local copies, waits for them, and re-layouts  7.1 us (4%)
  other arithmetic  2.06 us (1%)
    ppermute x24, waiting for transfers between devices, shift(): return lax.ppermute(v, 'dp', [(i, (i + k) % n_dp) for i in range(n_dp)])  82.8 us
    ppermute x24, starting transfers between devices, shift(): return lax.ppermute(v, 'dp', [(i, (i + k) % n_dp) for i in range(n_dp)])  28.2 us
    ppermute x3, waiting for transfers between devices, swap_x(): return lax.ppermute(v, 'tensor', [(0, 1), (1, 0)])  18.4 us
    pallas_call x6, Pallas kernels, call(): pl.pallas_call(functools.partial(gate_up_kernel, n), grid=(1,), out_shape...  16.1 us
    ppermute x4, starting transfers between devices, swap_y(): return lax.ppermute(v, 'expert', [(0, 2), (2, 0), (1, 3), (3, 1)])  6.34 us
    unnamed x24, local copies, waits for them, and re-layouts  5.49 us
    pallas_call x2, Pallas kernels, down(): pl.pallas_call(functools.partial(down_kernel, n, 1, False), grid=(1,), ou...  5.25 us
    pallas_call x1, Pallas kernels, stationary_plan(): pl.pallas_call(functools.partial(down_kernel, n_dp, 2, True), grid=(1,),...  4.9 us
  transfers between devices with their start and end apart: 38, of which 26 were waited for; matrix products, arithmetic and copies ran while one was open for 2% of the time, Pallas kernels for 13%

profile of v3, /device:TPU:0, one launch (start us, length us, event | category | flops | bytes accessed | tf_op | source)
XLA Modules:
  0.0 184.0 jit_solution(12100790609082672359)
XLA Ops:
  6.1 5.0 %collective-permute-start.4 = (bf16[144,512]{1,0:T(8,128)(2,1)S(1)}, bf16[144,512]{1,0:T(8,128)(2,1)S(1)}, u32[]{:S(2)}, u32[]{:S(2)}) collective-permute-start(bf16[144,512]{1,0:T(8,128)(2,1)S(1)} %get-tuple-element.78), channel_id=1, source_target_pairs={{0,3},{1,0},{2,1},{3,2},{4,7},{5,4},{6,5},{7,6},{8,11},{9,8},{10,9... | collective-permute-start | bytes 442376 | tf_op jit(solution)/shard_map/ppermute | solution.py:215
  15.3 4.3 %collective-permute-done.2.refs_0_.refs_1_ = bf16[144,512]{1,0:T(8,128)(2,1)S(1)} collective-permute-done((bf16[144,512]{1,0:T(8,128)(2,1)S(1)}, bf16[144,512]{1,0:T(8,128)(2,1)S(1)}, u32[]{:S(2)}, u32[]{:S(2)}) %collective-permute-start.2) | collective-permute-done | bytes 147488 | tf_op jit(solution)/shard_map/ppermute | solution.py:215
  19.6 4.2 %collective-permute-done.3.refs_1_.refs_2_.refs_0_ = bf16[144,512]{1,0:T(8,128)(2,1)S(1)} collective-permute-done((bf16[144,512]{1,0:T(8,128)(2,1)S(1)}, bf16[144,512]{1,0:T(8,128)(2,1)S(1)}, u32[]{:S(2)}, u32[]{:S(2)}) %collective-permute-start.3) | collective-permute-done | bytes 147488 | tf_op jit(solution)/shard_map/ppermute | solution.py:215
  25.5 12.8 %collective-permute-done.5 = bf16[4,144,512]{2,1,0:T(8,128)(2,1)S(1)} collective-permute-done((bf16[4,144,512]{2,1,0:T(8,128)(2,1)S(1)}, bf16[4,144,512]{2,1,0:T(8,128)(2,1)S(1)}, u32[]{:S(2)}, u32[]{:S(2)}) %collective-permute-start.5) | collective-permute-done | bytes 589856 | tf_op jit(solution)/shard_map/ppermute | solution.py:212
  44.7 3.3 %shard_map.74 = (bf16[2,128,512]{2,1,0:T(8,128)(2,1)S(1)}, bf16[2,128,512]{2,1,0:T(8,128)(2,1)S(1)}, bf16[2,128,512]{2,1,0:T(8,128)(2,1)S(1)}) custom-call(s32[4]{0:T(128)S(1)} %pad_add_fusion.where_ref, bf16[144,512]{1,0:T(8,128)(2,1)S(1)} %get-tuple-element.80.refs_0_.refs_1_, bf16[144,512]{1,0:T(8,128)(2,1)S(1)} %collective-permute-done.3.refs_1_.refs_2_.refs_0_, ...), custom_call_target="tpu_custom_call" | custom-call | flops 1 | bytes 1 | tf_op jit(solution)/shard_map/pallas_call | solution.py:253
  48.1 5.3 %collective-permute-done.9 = bf16[2,128,512]{2,1,0:T(8,128)(2,1)S(1)} collective-permute-done((bf16[2,128,512]{2,1,0:T(8,128)(2,1)S(1)}, bf16[2,128,512]{2,1,0:T(8,128)(2,1)S(1)}, u32[]{:S(2)}, u32[]{:S(2)}) %collective-permute-start.9) | collective-permute-done | bytes 262176 | tf_op jit(solution)/shard_map/ppermute | solution.py:215
  53.5 9.3 %collective-permute-done.10 = bf16[2,128,512]{2,1,0:T(8,128)(2,1)S(1)} collective-permute-done((bf16[2,128,512]{2,1,0:T(8,128)(2,1)S(1)}, bf16[2,128,512]{2,1,0:T(8,128)(2,1)S(1)}, u32[]{:S(2)}, u32[]{:S(2)}) %collective-permute-start.10) | collective-permute-done | bytes 262176 | tf_op jit(solution)/shard_map/ppermute | solution.py:215
  70.9 3.4 %shard_map.76 = (bf16[2,128,512]{2,1,0:T(8,128)(2,1)S(1)}, bf16[2,128,512]{2,1,0:T(8,128)(2,1)S(1)}, bf16[2,128,512]{2,1,0:T(8,128)(2,1)S(1)}) custom-call(s32[4]{0:T(128)S(1)} %pad_add_fusion.where_ref, bf16[144,512]{1,0:T(8,128)(2,1)S(1)} %get-tuple-element.80.refs_0_.refs_1_, bf16[144,512]{1,0:T(8,128)(2,1)S(1)} %collective-permute-done.3.refs_1_.refs_2_.refs_0_, ...), custom_call_target="tpu_custom_call" | custom-call | flops 1 | bytes 1 | tf_op jit(solution)/shard_map/pallas_call | solution.py:253
  74.3 5.9 %collective-permute-done.13 = bf16[2,128,512]{2,1,0:T(8,128)(2,1)S(1)} collective-permute-done((bf16[2,128,512]{2,1,0:T(8,128)(2,1)S(1)}, bf16[2,128,512]{2,1,0:T(8,128)(2,1)S(1)}, u32[]{:S(2)}, u32[]{:S(2)}) %collective-permute-start.13) | collective-permute-done | bytes 262176 | tf_op jit(solution)/shard_map/ppermute | solution.py:215
  80.4 5.5 %collective-permute-done.15.refs_1_ = bf16[2,128,512]{2,1,0:T(8,128)(2,1)S(1)} collective-permute-done((bf16[2,128,512]{2,1,0:T(8,128)(2,1)S(1)}, bf16[2,128,512]{2,1,0:T(8,128)(2,1)S(1)}, u32[]{:S(2)}, u32[]{:S(2)}) %collective-permute-start.15) | collective-permute-done | bytes 262176 | tf_op jit(solution)/shard_map/ppermute | solution.py:215
  91.7 2.7 %collective-permute-done.16.refs_5_ = bf16[2,128,256]{2,1,0:T(8,128)(2,1)S(1)} collective-permute-done((bf16[2,128,256]{2,1,0:T(8,128)(2,1)S(1)}, bf16[2,128,256]{2,1,0:T(8,128)(2,1)S(1)}, u32[]{:S(2)}, u32[]{:S(2)}) %collective-permute-start.16) | collective-permute-done | bytes 131104 | tf_op jit(solution)/shard_map/ppermute | solution.py:215
  94.4 4.8 %collective-permute-done.17.refs_6_ = bf16[2,128,256]{2,1,0:T(8,128)(2,1)S(1)} collective-permute-done((bf16[2,128,256]{2,1,0:T(8,128)(2,1)S(1)}, bf16[2,128,256]{2,1,0:T(8,128)(2,1)S(1)}, u32[]{:S(2)}, u32[]{:S(2)}) %collective-permute-start.17) | collective-permute-done | bytes 131104 | tf_op jit(solution)/shard_map/ppermute | solution.py:215
  104.0 3.3 %collective-permute-start.20 = (bf16[2,128,512]{2,1,0:T(8,128)(2,1)S(1)}, bf16[2,128,512]{2,1,0:T(8,128)(2,1)S(1)}, u32[]{:S(2)}, u32[]{:S(2)}) collective-permute-start(bf16[2,128,512]{2,1,0:T(8,128)(2,1)S(1)} %shard_map.80), channel_id=1, source_target_pairs={{0,1},{1,2},{2,3},{3,0},{4,5},{5,6},{6,7},{7,4},{8,9},{9,10},{10,1... | collective-permute-start | bytes 786440 | tf_op jit(solution)/shard_map/ppermute | solution.py:215
  107.3 3.3 %shard_map.79 = (bf16[2,128,512]{2,1,0:T(8,128)(2,1)S(1)}, bf16[2,128,512]{2,1,0:T(8,128)(2,1)S(1)}, bf16[2,128,512]{2,1,0:T(8,128)(2,1)S(1)}) custom-call(s32[4]{0:T(128)S(1)} %pad_add_fusion.where_ref, bf16[144,512]{1,0:T(8,128)(2,1)S(1)} %get-tuple-element.80.refs_0_.refs_1_, bf16[144,512]{1,0:T(8,128)(2,1)S(1)} %collective-permute-done.3.refs_1_.refs_2_.refs_0_, ...), custom_call_target="tpu_custom_call" | custom-call | flops 1 | bytes 1 | tf_op jit(solution)/shard_map/pallas_call | solution.py:253
  110.6 4.3 %collective-permute-done.20 = bf16[2,128,512]{2,1,0:T(8,128)(2,1)S(1)} collective-permute-done((bf16[2,128,512]{2,1,0:T(8,128)(2,1)S(1)}, bf16[2,128,512]{2,1,0:T(8,128)(2,1)S(1)}, u32[]{:S(2)}, u32[]{:S(2)}) %collective-permute-start.20) | collective-permute-done | bytes 262176 | tf_op jit(solution)/shard_map/ppermute | solution.py:215
  116.6 4.0 %collective-permute-done.24.refs_1_ = bf16[2,128,512]{2,1,0:T(8,128)(2,1)S(1)} collective-permute-done((bf16[2,128,512]{2,1,0:T(8,128)(2,1)S(1)}, bf16[2,128,512]{2,1,0:T(8,128)(2,1)S(1)}, u32[]{:S(2)}, u32[]{:S(2)}) %collective-permute-start.24) | collective-permute-done | bytes 262176 | tf_op jit(solution)/shard_map/ppermute | solution.py:215
  122.2 6.0 %collective-permute-done.25.refs_9_ = bf16[2,128,256]{2,1,0:T(8,128)(2,1)S(1)} collective-permute-done((bf16[2,128,256]{2,1,0:T(8,128)(2,1)S(1)}, bf16[2,128,256]{2,1,0:T(8,128)(2,1)S(1)}, u32[]{:S(2)}, u32[]{:S(2)}) %collective-permute-start.25) | collective-permute-done | bytes 131104 | tf_op jit(solution)/shard_map/ppermute | solution.py:215
  130.1 6.3 %collective-permute-done.26.refs_10_ = bf16[2,128,256]{2,1,0:T(8,128)(2,1)S(1)} collective-permute-done((bf16[2,128,256]{2,1,0:T(8,128)(2,1)S(1)}, bf16[2,128,256]{2,1,0:T(8,128)(2,1)S(1)}, u32[]{:S(2)}, u32[]{:S(2)}) %collective-permute-start.26) | collective-permute-done | bytes 131104 | tf_op jit(solution)/shard_map/ppermute | solution.py:215
  136.4 6.8 %collective-permute-done.27.refs_11_ = bf16[2,128,256]{2,1,0:T(8,128)(2,1)S(1)} collective-permute-done((bf16[2,128,256]{2,1,0:T(8,128)(2,1)S(1)}, bf16[2,128,256]{2,1,0:T(8,128)(2,1)S(1)}, u32[]{:S(2)}, u32[]{:S(2)}) %collective-permute-start.27) | collective-permute-done | bytes 131104 | tf_op jit(solution)/shard_map/ppermute | solution.py:215
  144.2 3.6 %collective-permute-start.32 = (bf16[2,128,256]{2,1,0:T(8,128)(2,1)S(1)}, bf16[2,128,256]{2,1,0:T(8,128)(2,1)S(1)}, u32[]{:S(2)}, u32[]{:S(2)}) collective-permute-start(bf16[2,128,256]{2,1,0:T(8,128)(2,1)S(1)} %shard_map.82.refs_3_), channel_id=1, source_target_pairs={{0,3},{1,0},{2,1},{3,2},{4,7},{5,4},{6,5},{7,6},{8,11},{9,8},{10,9... | collective-permute-start | bytes 393224 | tf_op jit(solution)/shard_map/ppermute | solution.py:215
  147.8 4.5 %collective-permute-done.28.refs_2_ = bf16[2,128,256]{2,1,0:T(8,128)(2,1)S(1)} collective-permute-done((bf16[2,128,256]{2,1,0:T(8,128)(2,1)S(1)}, bf16[2,128,256]{2,1,0:T(8,128)(2,1)S(1)}, u32[]{:S(2)}, u32[]{:S(2)}) %collective-permute-start.28) | collective-permute-done | bytes 131104 | tf_op jit(solution)/shard_map/ppermute | solution.py:215
  154.6 4.9 %shard_map.83 = (f32[128,1024]{1,0:T(8,128)S(1)}, f32[128,1024]{1,0:T(8,128)S(1)}, f32[128,1024]{1,0:T(8,128)S(1)}, f32[128,1024]{1,0:T(8,128)S(1)}) custom-call(s32[4]{0:T(128)S(1)} %pad_add_fusion.where_ref, bf16[144,512]{1,0:T(8,128)(2,1)S(1)} %get-tuple-element.80.refs_0_.refs_1_, bf16[144,512]{1,0:T(8,128)(2,1)S(1)} %collective-permute-done.2.refs_0_.refs_1_, ...), custom_call_target="tpu_custom_call" | custom-call | flops 6000000000 | bytes 1 | tf_op jit(solution)/shard_map/pallas_call | solution.py:331
  168.4 3.5 %collective-permute-done.35 = bf16[2,128,512]{2,1,0:T(8,128)(2,1)S(1)} collective-permute-done((bf16[2,128,512]{2,1,0:T(8,128)(2,1)S(1)}, bf16[2,128,512]{2,1,0:T(8,128)(2,1)S(1)}, u32[]{:S(2)}, u32[]{:S(2)}) %collective-permute-start.35) | collective-permute-done | bytes 262176 | tf_op jit(solution)/shard_map/ppermute | solution.py:212
  177.0 4.5 %collective-permute-done.36.refs_2_ = bf16[128,512]{1,0:T(8,128)(2,1)S(1)} collective-permute-done((bf16[128,512]{1,0:T(8,128)(2,1)S(1)}, bf16[128,512]{1,0:T(8,128)(2,1)S(1)}, u32[]{:S(2)}, u32[]{:S(2)}) %collective-permute-start.36) | collective-permute-done | bytes 131104 | tf_op jit(solution)/shard_map/ppermute | solution.py:215
  (119 shorter events, 61.4 us)
Async XLA Ops:
  6.1 9.2 %collective-permute-start.4 = (bf16[144,512]{1,0:T(8,128)(2,1)S(1)}, bf16[144,512]{1,0:T(8,128)(2,1)S(1)}, u32[]{:S(2)}, u32[]{:S(2)}) collective-permute-start(bf16[144,512]{1,0:T(8,128)(2,1)S(1)} %get-tuple-element.78), channel_id=1, source_target_pairs={{0,3},{1,0},{2,1},{3,2},{4,7},{5,4},{6,5},{7,6},{8,11},{9,8},{10,9... | collective-permute-start | bytes 442376 | tf_op jit(solution)/shard_map/ppermute | solution.py:215
  11.1 12.8 %collective-permute-start.3 = (bf16[144,512]{1,0:T(8,128)(2,1)S(1)}, bf16[144,512]{1,0:T(8,128)(2,1)S(1)}, u32[]{:S(2)}, u32[]{:S(2)}) collective-permute-start(bf16[144,512]{1,0:T(8,128)(2,1)S(1)} %get-tuple-element.77), channel_id=1, source_target_pairs={{0,2},{1,3},{2,0},{3,1},{4,6},{5,7},{6,4},{7,5},{8,10},{9,11},{10,... | collective-permute-start | bytes 442376 | tf_op jit(solution)/shard_map/ppermute | solution.py:215
  12.2 26.2 %collective-permute-start.6 = (bf16[2,4,256,256]{3,2,1,0:T(8,128)(2,1)S(1)}, bf16[2,4,256,256]{3,2,1,0:T(8,128)(2,1)S(1)}, u32[]{:S(2)}, u32[]{:S(2)}) collective-permute-start(bf16[2,4,256,256]{3,2,1,0:T(8,128)(2,1)S(1)} %pad_maximum_fusion), channel_id=1, source_target_pairs={{0,16},{16,0},{8,24},{24,8},{1,17},{17,1},{9,25},{25,9},{2,18},{18... | collective-permute-start | bytes 3145736 | tf_op jit(solution)/shard_map/ppermute | solution.py:206
  24.0 14.3 %collective-permute-start.5 = (bf16[4,144,512]{2,1,0:T(8,128)(2,1)S(1)}, bf16[4,144,512]{2,1,0:T(8,128)(2,1)S(1)}, u32[]{:S(2)}, u32[]{:S(2)}) collective-permute-start(bf16[4,144,512]{2,1,0:T(8,128)(2,1)S(1)} %pad_maximum_fusion.3), channel_id=1, source_target_pairs={{0,4},{4,0},{1,5},{5,1},{2,6},{6,2},{3,7},{7,3},{8,12},{12,8},{9,1... | collective-permute-start | bytes 1769480 | tf_op jit(solution)/shard_map/ppermute | solution.py:212
  38.9 25.6 %collective-permute-start.7 = (bf16[2,4,256,256]{3,2,1,0:T(8,128)(2,1)S(1)}, bf16[2,4,256,256]{3,2,1,0:T(8,128)(2,1)S(1)}, u32[]{:S(2)}, u32[]{:S(2)}) collective-permute-start(bf16[2,4,256,256]{3,2,1,0:T(8,128)(2,1)S(1)} %pad_maximum_fusion.1), channel_id=1, source_target_pairs={{0,16},{16,0},{8,24},{24,8},{1,17},{17,1},{9,25},{25,9},{2,18},{18... | collective-permute-start | bytes 3145736 | tf_op jit(solution)/shard_map/ppermute | solution.py:206
  43.1 10.2 %collective-permute-start.9 = (bf16[2,128,512]{2,1,0:T(8,128)(2,1)S(1)}, bf16[2,128,512]{2,1,0:T(8,128)(2,1)S(1)}, u32[]{:S(2)}, u32[]{:S(2)}) collective-permute-start(bf16[2,128,512]{2,1,0:T(8,128)(2,1)S(1)} %shard_map.75), channel_id=1, source_target_pairs={{0,1},{1,2},{2,3},{3,0},{4,5},{5,6},{6,7},{7,4},{8,9},{9,10},{10,1... | collective-permute-start | bytes 786440 | tf_op jit(solution)/shard_map/ppermute | solution.py:215
  53.4 9.4 %collective-permute-start.10 = (bf16[2,128,512]{2,1,0:T(8,128)(2,1)S(1)}, bf16[2,128,512]{2,1,0:T(8,128)(2,1)S(1)}, u32[]{:S(2)}, u32[]{:S(2)}) collective-permute-start(bf16[2,128,512]{2,1,0:T(8,128)(2,1)S(1)} %add_convert_fusion.7), channel_id=1, source_target_pairs={{0,1},{1,2},{2,3},{3,0},{4,5},{5,6},{6,7},{7,4},{8,9},{9,10},{10,1... | collective-permute-start | bytes 786440 | tf_op jit(solution)/shard_map/ppermute | solution.py:215
  65.0 34.3 %collective-permute-start.11 = (bf16[2,4,256,256]{3,2,1,0:T(8,128)(2,1)S(1)}, bf16[2,4,256,256]{3,2,1,0:T(8,128)(2,1)S(1)}, u32[]{:S(2)}, u32[]{:S(2)}) collective-permute-start(bf16[2,4,256,256]{3,2,1,0:T(8,128)(2,1)S(1)} %pad_maximum_fusion.2), channel_id=1, source_target_pairs={{0,16},{16,0},{8,24},{24,8},{1,17},{17,1},{9,25},{25,9},{2,18},{18... | collective-permute-start | bytes 3145736 | tf_op jit(solution)/shard_map/ppermute | solution.py:206
  69.2 11.0 %collective-permute-start.13 = (bf16[2,128,512]{2,1,0:T(8,128)(2,1)S(1)}, bf16[2,128,512]{2,1,0:T(8,128)(2,1)S(1)}, u32[]{:S(2)}, u32[]{:S(2)}) collective-permute-start(bf16[2,128,512]{2,1,0:T(8,128)(2,1)S(1)} %shard_map.77), channel_id=1, source_target_pairs={{0,1},{1,2},{2,3},{3,0},{4,5},{5,6},{6,7},{7,4},{8,9},{9,10},{10,1... | collective-permute-start | bytes 786440 | tf_op jit(solution)/shard_map/ppermute | solution.py:215
  70.8 15.0 %collective-permute-start.15 = (bf16[2,128,512]{2,1,0:T(8,128)(2,1)S(1)}, bf16[2,128,512]{2,1,0:T(8,128)(2,1)S(1)}, u32[]{:S(2)}, u32[]{:S(2)}) collective-permute-start(bf16[2,128,512]{2,1,0:T(8,128)(2,1)S(1)} %add_convert_fusion.6), channel_id=1, source_target_pairs={{0,1},{1,2},{2,3},{3,0},{4,5},{5,6},{6,7},{7,4},{8,9},{9,10},{10,1... | collective-permute-start | bytes 786440 | tf_op jit(solution)/shard_map/ppermute | solution.py:215
  80.3 11.4 %collective-permute-start.14 = (bf16[2,128,512]{2,1,0:T(8,128)(2,1)S(1)}, bf16[2,128,512]{2,1,0:T(8,128)(2,1)S(1)}, u32[]{:S(2)}, u32[]{:S(2)}) collective-permute-start(bf16[2,128,512]{2,1,0:T(8,128)(2,1)S(1)} %add_convert_fusion.5), channel_id=1, source_target_pairs={{0,1},{1,2},{2,3},{3,0},{4,5},{5,6},{6,7},{7,4},{8,9},{9,10},{10,1... | collective-permute-start | bytes 786440 | tf_op jit(solution)/shard_map/ppermute | solution.py:215
  86.1 13.2 %collective-permute-start.17 = (bf16[2,128,256]{2,1,0:T(8,128)(2,1)S(1)}, bf16[2,128,256]{2,1,0:T(8,128)(2,1)S(1)}, u32[]{:S(2)}, u32[]{:S(2)}) collective-permute-start(bf16[2,128,256]{2,1,0:T(8,128)(2,1)S(1)} %shard_map.78.refs_4_), channel_id=1, source_target_pairs={{0,2},{1,3},{2,0},{3,1},{4,6},{5,7},{6,4},{7,5},{8,10},{9,11},{10,... | collective-permute-start | bytes 393224 | tf_op jit(solution)/shard_map/ppermute | solution.py:215
  87.4 11.9 %collective-permute-start.18 = (bf16[2,128,256]{2,1,0:T(8,128)(2,1)S(1)}, bf16[2,128,256]{2,1,0:T(8,128)(2,1)S(1)}, u32[]{:S(2)}, u32[]{:S(2)}) collective-permute-start(bf16[2,128,256]{2,1,0:T(8,128)(2,1)S(1)} %shard_map.78.refs_4_), channel_id=1, source_target_pairs={{0,3},{1,0},{2,1},{3,2},{4,7},{5,4},{6,5},{7,6},{8,11},{9,8},{10,9... | collective-permute-start | bytes 393224 | tf_op jit(solution)/shard_map/ppermute | solution.py:215
  99.3 43.9 %collective-permute-start.23 = (bf16[4,256,768]{2,1,0:T(8,128)(2,1)S(1)}, bf16[4,256,768]{2,1,0:T(8,128)(2,1)S(1)}, u32[]{:S(2)}, u32[]{:S(2)}) collective-permute-start(bf16[4,256,768]{2,1,0:T(8,128)(2,1)S(1)} %copy-done.4), channel_id=1, source_target_pairs={{0,16},{16,0},{8,24},{24,8},{1,17},{17,1},{9,25},{25,9},{2,18},{18... | collective-permute-start | bytes 4718600 | tf_op jit(solution)/shard_map/ppermute | solution.py:206
  104.0 11.0 %collective-permute-start.20 = (bf16[2,128,512]{2,1,0:T(8,128)(2,1)S(1)}, bf16[2,128,512]{2,1,0:T(8,128)(2,1)S(1)}, u32[]{:S(2)}, u32[]{:S(2)}) collective-permute-start(bf16[2,128,512]{2,1,0:T(8,128)(2,1)S(1)} %shard_map.80), channel_id=1, source_target_pairs={{0,1},{1,2},{2,3},{3,0},{4,5},{5,6},{6,7},{7,4},{8,9},{9,10},{10,1... | collective-permute-start | bytes 786440 | tf_op jit(solution)/shard_map/ppermute | solution.py:215
  107.3 13.3 %collective-permute-start.24 = (bf16[2,128,512]{2,1,0:T(8,128)(2,1)S(1)}, bf16[2,128,512]{2,1,0:T(8,128)(2,1)S(1)}, u32[]{:S(2)}, u32[]{:S(2)}) collective-permute-start(bf16[2,128,512]{2,1,0:T(8,128)(2,1)S(1)} %add_convert_fusion.4), channel_id=1, source_target_pairs={{0,1},{1,2},{2,3},{3,0},{4,5},{5,6},{6,7},{7,4},{8,9},{9,10},{10,1... | collective-permute-start | bytes 786440 | tf_op jit(solution)/shard_map/ppermute | solution.py:215
  115.0 14.6 %collective-permute-start.21 = (bf16[2,128,512]{2,1,0:T(8,128)(2,1)S(1)}, bf16[2,128,512]{2,1,0:T(8,128)(2,1)S(1)}, u32[]{:S(2)}, u32[]{:S(2)}) collective-permute-start(bf16[2,128,512]{2,1,0:T(8,128)(2,1)S(1)} %add_convert_fusion.3), channel_id=1, source_target_pairs={{0,1},{1,2},{2,3},{3,0},{4,5},{5,6},{6,7},{7,4},{8,9},{9,10},{10,1... | collective-permute-start | bytes 786440 | tf_op jit(solution)/shard_map/ppermute | solution.py:215
  129.8 13.5 %collective-permute-start.22 = (bf16[2,128,512]{2,1,0:T(8,128)(2,1)S(1)}, bf16[2,128,512]{2,1,0:T(8,128)(2,1)S(1)}, u32[]{:S(2)}, u32[]{:S(2)}) collective-permute-start(bf16[2,128,512]{2,1,0:T(8,128)(2,1)S(1)} %add_convert_fusion.2), channel_id=1, source_target_pairs={{0,1},{1,2},{2,3},{3,0},{4,5},{5,6},{6,7},{7,4},{8,9},{9,10},{10,1... | collective-permute-start | bytes 786440 | tf_op jit(solution)/shard_map/ppermute | solution.py:215
  143.2 9.0 %collective-permute-start.29 = (bf16[4,256,768]{2,1,0:T(8,128)(2,1)S(1)}, bf16[4,256,768]{2,1,0:T(8,128)(2,1)S(1)}, u32[]{:S(2)}, u32[]{:S(2)}) collective-permute-start(bf16[4,256,768]{2,1,0:T(8,128)(2,1)S(1)} %copy-done.4), channel_id=1, source_target_pairs={{0,8},{8,0},{16,24},{24,16},{1,9},{9,1},{17,25},{25,17},{2,10},{10... | collective-permute-start | bytes 4718600 | tf_op jit(solution)/shard_map/ppermute | solution.py:209
  143.3 9.0 %collective-permute-start.30 = (bf16[4,256,768]{2,1,0:T(8,128)(2,1)S(1)}, bf16[4,256,768]{2,1,0:T(8,128)(2,1)S(1)}, u32[]{:S(2)}, u32[]{:S(2)}) collective-permute-start(bf16[4,256,768]{2,1,0:T(8,128)(2,1)S(1)} %collective-permute-done.23.refs_14_.refs_6_), channel_id=1, source_target_pairs={{0,8},{8,0},{16,24},{24,16},{1,9},{9,1},{17,25},{25,17},{2,10},{10... | collective-permute-start | bytes 4718600 | tf_op jit(solution)/shard_map/ppermute | solution.py:209
  144.0 15.5 %collective-permute-start.31 = (bf16[2,128,256]{2,1,0:T(8,128)(2,1)S(1)}, bf16[2,128,256]{2,1,0:T(8,128)(2,1)S(1)}, u32[]{:S(2)}, u32[]{:S(2)}) collective-permute-start(bf16[2,128,256]{2,1,0:T(8,128)(2,1)S(1)} %shard_map.82.refs_3_), channel_id=1, source_target_pairs={{0,2},{1,3},{2,0},{3,1},{4,6},{5,7},{6,4},{7,5},{8,10},{9,11},{10,... | collective-permute-start | bytes 393224 | tf_op jit(solution)/shard_map/ppermute | solution.py:215
  144.2 15.3 %collective-permute-start.32 = (bf16[2,128,256]{2,1,0:T(8,128)(2,1)S(1)}, bf16[2,128,256]{2,1,0:T(8,128)(2,1)S(1)}, u32[]{:S(2)}, u32[]{:S(2)}) collective-permute-start(bf16[2,128,256]{2,1,0:T(8,128)(2,1)S(1)} %shard_map.82.refs_3_), channel_id=1, source_target_pairs={{0,3},{1,0},{2,1},{3,2},{4,7},{5,4},{6,5},{7,6},{8,11},{9,8},{10,9... | collective-permute-start | bytes 393224 | tf_op jit(solution)/shard_map/ppermute | solution.py:215
  171.9 9.6 %collective-permute-start.36 = (bf16[128,512]{1,0:T(8,128)(2,1)S(1)}, bf16[128,512]{1,0:T(8,128)(2,1)S(1)}, u32[]{:S(2)}, u32[]{:S(2)}) collective-permute-start(bf16[128,512]{1,0:T(8,128)(2,1)S(1)} %get-tuple-element.154), channel_id=1, source_target_pairs={{0,2},{1,3},{2,0},{3,1},{4,6},{5,7},{6,4},{7,5},{8,10},{9,11},{10,... | collective-permute-start | bytes 393224 | tf_op jit(solution)/shard_map/ppermute | solution.py:215
  172.0 9.5 %collective-permute-start.37 = (bf16[128,512]{1,0:T(8,128)(2,1)S(1)}, bf16[128,512]{1,0:T(8,128)(2,1)S(1)}, u32[]{:S(2)}, u32[]{:S(2)}) collective-permute-start(bf16[128,512]{1,0:T(8,128)(2,1)S(1)} %get-tuple-element.153), channel_id=1, source_target_pairs={{0,1},{1,2},{2,3},{3,0},{4,5},{5,6},{6,7},{7,4},{8,9},{9,10},{10,1... | collective-permute-start | bytes 393224 | tf_op jit(solution)/shard_map/ppermute | solution.py:215
  (26 other events, 227.2 us)

commit v4 on v3

--- a/solution.py
+++ b/solution.py
@@ -301,7 +301,8 @@
     parts0 = gate_up([0, 1], y01, yc01)
     run0 = ring_step(parts0, parts0[1], 2)
     run0 = ring_step(parts0, run0, 3)
-    y23, run0, *given = bar((y23, run0, *given))
+    down_core = swap_core(down_weight)
+    y23, run0, down_core, *given = bar((y23, run0, down_core, *given))
 
     yc23 = swap_core(y23)
     y45 = swap_y(pair(4))
@@ -320,8 +321,8 @@
     hidden1 = ring_dp(hidden_of([parts1], [got1]))
     run2 = ring_step(parts2, run2, 3)
     got2 = shift(run2, 1)
-    got2, down_y, down_from, *hidden1 = bar((got2, down_y, down_from, *hidden1))
-    down_core, down_yc = swap_core(down_from), swap_core(down_y)
+    got2, down_y, down_from, hidden1[2] = bar((got2, down_y, down_from, hidden1[2]))
+    down_yc = swap_core(down_y)
     hidden2 = hidden_of([parts2], [got2])
     hidden2 = gather_dp(hidden2)
     hidden2[1], down_core, down_yc = bar((hidden2[1], down_core, down_yc))
@@ -340,7 +341,7 @@
         cost_estimate=pl.CostEstimate(flops=6_000_000_000, bytes_accessed=1, transcendentals=0),
     )(where, *own, *hidden0, *hidden1, *down_weights)
 
-    hidden2[1], hidden2[2], hidden2[3], *sums = bar((hidden2[1], hidden2[2], hidden2[3], *sums))
+    hidden2[1], *sums = bar((hidden2[1], *sums))
 
     def down(which):
         n = len(which)

time: 184 us -> 182 us (0.989)
  starting transfers between devices: 39.4 us -> 47.3 us
  waiting for transfers between devices: 106 us -> 98.8 us
  local copies, waits for them, and re-layouts: 7.1 us -> 4.12 us
    ppermute x24, starting transfers between devices: 28.2 us -> 36.1 us  [shift(): return lax.ppermute(v, 'dp', [(i, (i + k) % n_dp) for i in range(n_dp)])]
    ppermute x24, waiting for transfers between devices: 82.8 us -> 76.9 us  [shift(): return lax.ppermute(v, 'dp', [(i, (i + k) % n_dp) for i in range(n_dp)])]
    unnamed x24, local copies, waits for them, and re-layouts: 5.49 us -> 2.51 us
  transfers between devices with their start and end apart: 38 -> 38, of which waited for: 26 -> 28; matrix products, arithmetic and copies ran while one was open for 2% -> 2% of each run, Pallas kernels for 13% -> 13%
where the time goes in v4:
time: 182 us
  waiting for transfers between devices  98.8 us (54%)
  starting transfers between devices  47.3 us (26%)
  Pallas kernels  28.5 us (16%)
  local copies, waits for them, and re-layouts  4.12 us (2%)
  other arithmetic  2.07 us (1%)
    ppermute x24, waiting for transfers between devices, shift(): return lax.ppermute(v, 'dp', [(i, (i + k) % n_dp) for i in range(n_dp)])  76.9 us
    ppermute x24, starting transfers between devices, shift(): return lax.ppermute(v, 'dp', [(i, (i + k) % n_dp) for i in range(n_dp)])  36.1 us
    ppermute x3, waiting for transfers between devices, swap_x(): return lax.ppermute(v, 'tensor', [(0, 1), (1, 0)])  18 us
    pallas_call x6, Pallas kernels, call(): pl.pallas_call(functools.partial(gate_up_kernel, n), grid=(1,), out_shape...  16 us
    ppermute x4, starting transfers between devices, swap_y(): return lax.ppermute(v, 'expert', [(0, 2), (2, 0), (1, 3), (3, 1)])  6.34 us
    pallas_call x2, Pallas kernels, down(): pl.pallas_call(functools.partial(down_kernel, n, 1, False), grid=(1,), ou...  5.24 us
    pallas_call x1, Pallas kernels, stationary_plan(): pl.pallas_call(functools.partial(down_kernel, n_dp, 2, True), grid=(1,),...  4.91 us
    ppermute x3, starting transfers between devices, swap_x(): return lax.ppermute(v, 'tensor', [(0, 1), (1, 0)])  3.71 us
  transfers between devices with their start and end apart: 38, of which 28 were waited for; matrix products, arithmetic and copies ran while one was open for 2% of the time, Pallas kernels for 13%

profile of v4, /device:TPU:0, one launch (start us, length us, event | category | flops | bytes accessed | tf_op | source)
XLA Modules:
  0.0 181.9 jit_solution(4094388810880167386)
XLA Ops:
  6.8 5.0 %collective-permute-start.4 = (bf16[144,512]{1,0:T(8,128)(2,1)S(1)}, bf16[144,512]{1,0:T(8,128)(2,1)S(1)}, u32[]{:S(2)}, u32[]{:S(2)}) collective-permute-start(bf16[144,512]{1,0:T(8,128)(2,1)S(1)} %get-tuple-element.73), channel_id=1, source_target_pairs={{0,3},{1,0},{2,1},{3,2},{4,7},{5,4},{6,5},{7,6},{8,11},{9,8},{10,9... | collective-permute-start | bytes 442376 | tf_op jit(solution)/shard_map/ppermute | solution.py:215
  16.1 4.3 %collective-permute-done.2.refs_0_.refs_1_ = bf16[144,512]{1,0:T(8,128)(2,1)S(1)} collective-permute-done((bf16[144,512]{1,0:T(8,128)(2,1)S(1)}, bf16[144,512]{1,0:T(8,128)(2,1)S(1)}, u32[]{:S(2)}, u32[]{:S(2)}) %collective-permute-start.2) | collective-permute-done | bytes 147488 | tf_op jit(solution)/shard_map/ppermute | solution.py:215
  20.5 4.2 %collective-permute-done.3.refs_1_.refs_2_.refs_0_ = bf16[144,512]{1,0:T(8,128)(2,1)S(1)} collective-permute-done((bf16[144,512]{1,0:T(8,128)(2,1)S(1)}, bf16[144,512]{1,0:T(8,128)(2,1)S(1)}, u32[]{:S(2)}, u32[]{:S(2)}) %collective-permute-start.3) | collective-permute-done | bytes 147488 | tf_op jit(solution)/shard_map/ppermute | solution.py:215
  26.3 12.8 %collective-permute-done.5 = bf16[4,144,512]{2,1,0:T(8,128)(2,1)S(1)} collective-permute-done((bf16[4,144,512]{2,1,0:T(8,128)(2,1)S(1)}, bf16[4,144,512]{2,1,0:T(8,128)(2,1)S(1)}, u32[]{:S(2)}, u32[]{:S(2)}) %collective-permute-start.5) | collective-permute-done | bytes 589856 | tf_op jit(solution)/shard_map/ppermute | solution.py:212
  45.5 3.3 %shard_map.74 = (bf16[2,128,512]{2,1,0:T(8,128)(2,1)S(1)}, bf16[2,128,512]{2,1,0:T(8,128)(2,1)S(1)}, bf16[2,128,512]{2,1,0:T(8,128)(2,1)S(1)}) custom-call(s32[4]{0:T(128)S(1)} %pad_add_fusion.where_ref, bf16[144,512]{1,0:T(8,128)(2,1)S(1)} %get-tuple-element.75.refs_0_.refs_1_, bf16[144,512]{1,0:T(8,128)(2,1)S(1)} %collective-permute-done.3.refs_1_.refs_2_.refs_0_, ...), custom_call_target="tpu_custom_call" | custom-call | flops 1 | bytes 1 | tf_op jit(solution)/shard_map/pallas_call | solution.py:253
  48.8 5.3 %collective-permute-done.9 = bf16[2,128,512]{2,1,0:T(8,128)(2,1)S(1)} collective-permute-done((bf16[2,128,512]{2,1,0:T(8,128)(2,1)S(1)}, bf16[2,128,512]{2,1,0:T(8,128)(2,1)S(1)}, u32[]{:S(2)}, u32[]{:S(2)}) %collective-permute-start.9) | collective-permute-done | bytes 262176 | tf_op jit(solution)/shard_map/ppermute | solution.py:215
  54.2 9.3 %collective-permute-done.10 = bf16[2,128,512]{2,1,0:T(8,128)(2,1)S(1)} collective-permute-done((bf16[2,128,512]{2,1,0:T(8,128)(2,1)S(1)}, bf16[2,128,512]{2,1,0:T(8,128)(2,1)S(1)}, u32[]{:S(2)}, u32[]{:S(2)}) %collective-permute-start.10) | collective-permute-done | bytes 262176 | tf_op jit(solution)/shard_map/ppermute | solution.py:215
  71.7 3.3 %shard_map.76 = (bf16[2,128,512]{2,1,0:T(8,128)(2,1)S(1)}, bf16[2,128,512]{2,1,0:T(8,128)(2,1)S(1)}, bf16[2,128,512]{2,1,0:T(8,128)(2,1)S(1)}) custom-call(s32[4]{0:T(128)S(1)} %pad_add_fusion.where_ref, bf16[144,512]{1,0:T(8,128)(2,1)S(1)} %get-tuple-element.75.refs_0_.refs_1_, bf16[144,512]{1,0:T(8,128)(2,1)S(1)} %collective-permute-done.3.refs_1_.refs_2_.refs_0_, ...), custom_call_target="tpu_custom_call" | custom-call | flops 1 | bytes 1 | tf_op jit(solution)/shard_map/pallas_call | solution.py:253
  75.0 6.1 %collective-permute-done.14 = bf16[2,128,512]{2,1,0:T(8,128)(2,1)S(1)} collective-permute-done((bf16[2,128,512]{2,1,0:T(8,128)(2,1)S(1)}, bf16[2,128,512]{2,1,0:T(8,128)(2,1)S(1)}, u32[]{:S(2)}, u32[]{:S(2)}) %collective-permute-start.14) | collective-permute-done | bytes 262176 | tf_op jit(solution)/shard_map/ppermute | solution.py:215
  81.2 5.5 %collective-permute-done.16.refs_1_ = bf16[2,128,512]{2,1,0:T(8,128)(2,1)S(1)} collective-permute-done((bf16[2,128,512]{2,1,0:T(8,128)(2,1)S(1)}, bf16[2,128,512]{2,1,0:T(8,128)(2,1)S(1)}, u32[]{:S(2)}, u32[]{:S(2)}) %collective-permute-start.16) | collective-permute-done | bytes 262176 | tf_op jit(solution)/shard_map/ppermute | solution.py:215
  95.2 4.8 %collective-permute-done.18.refs_6_ = bf16[2,128,256]{2,1,0:T(8,128)(2,1)S(1)} collective-permute-done((bf16[2,128,256]{2,1,0:T(8,128)(2,1)S(1)}, bf16[2,128,256]{2,1,0:T(8,128)(2,1)S(1)}, u32[]{:S(2)}, u32[]{:S(2)}) %collective-permute-start.18) | collective-permute-done | bytes 131104 | tf_op jit(solution)/shard_map/ppermute | solution.py:215
  104.8 3.3 %collective-permute-start.21 = (bf16[2,128,512]{2,1,0:T(8,128)(2,1)S(1)}, bf16[2,128,512]{2,1,0:T(8,128)(2,1)S(1)}, u32[]{:S(2)}, u32[]{:S(2)}) collective-permute-start(bf16[2,128,512]{2,1,0:T(8,128)(2,1)S(1)} %shard_map.80), channel_id=1, source_target_pairs={{0,1},{1,2},{2,3},{3,0},{4,5},{5,6},{6,7},{7,4},{8,9},{9,10},{10,1... | collective-permute-start | bytes 786440 | tf_op jit(solution)/shard_map/ppermute | solution.py:215
  108.2 3.3 %shard_map.79 = (bf16[2,128,512]{2,1,0:T(8,128)(2,1)S(1)}, bf16[2,128,512]{2,1,0:T(8,128)(2,1)S(1)}, bf16[2,128,512]{2,1,0:T(8,128)(2,1)S(1)}) custom-call(s32[4]{0:T(128)S(1)} %pad_add_fusion.where_ref, bf16[144,512]{1,0:T(8,128)(2,1)S(1)} %get-tuple-element.75.refs_0_.refs_1_, bf16[144,512]{1,0:T(8,128)(2,1)S(1)} %collective-permute-done.3.refs_1_.refs_2_.refs_0_, ...), custom_call_target="tpu_custom_call" | custom-call | flops 1 | bytes 1 | tf_op jit(solution)/shard_map/pallas_call | solution.py:253
  111.5 4.3 %collective-permute-done.21 = bf16[2,128,512]{2,1,0:T(8,128)(2,1)S(1)} collective-permute-done((bf16[2,128,512]{2,1,0:T(8,128)(2,1)S(1)}, bf16[2,128,512]{2,1,0:T(8,128)(2,1)S(1)}, u32[]{:S(2)}, u32[]{:S(2)}) %collective-permute-start.21) | collective-permute-done | bytes 262176 | tf_op jit(solution)/shard_map/ppermute | solution.py:215
  117.4 4.0 %collective-permute-done.25.refs_1_ = bf16[2,128,512]{2,1,0:T(8,128)(2,1)S(1)} collective-permute-done((bf16[2,128,512]{2,1,0:T(8,128)(2,1)S(1)}, bf16[2,128,512]{2,1,0:T(8,128)(2,1)S(1)}, u32[]{:S(2)}, u32[]{:S(2)}) %collective-permute-start.25) | collective-permute-done | bytes 262176 | tf_op jit(solution)/shard_map/ppermute | solution.py:215
  123.2 3.8 %collective-permute-done.22 = bf16[2,128,512]{2,1,0:T(8,128)(2,1)S(1)} collective-permute-done((bf16[2,128,512]{2,1,0:T(8,128)(2,1)S(1)}, bf16[2,128,512]{2,1,0:T(8,128)(2,1)S(1)}, u32[]{:S(2)}, u32[]{:S(2)}) %collective-permute-start.22) | collective-permute-done | bytes 262176 | tf_op jit(solution)/shard_map/ppermute | solution.py:215
  131.2 7.2 %collective-permute-done.27.refs_10_ = bf16[2,128,256]{2,1,0:T(8,128)(2,1)S(1)} collective-permute-done((bf16[2,128,256]{2,1,0:T(8,128)(2,1)S(1)}, bf16[2,128,256]{2,1,0:T(8,128)(2,1)S(1)}, u32[]{:S(2)}, u32[]{:S(2)}) %collective-permute-start.27) | collective-permute-done | bytes 131104 | tf_op jit(solution)/shard_map/ppermute | solution.py:215
  140.4 2.7 %collective-permute-start.33 = (bf16[2,128,256]{2,1,0:T(8,128)(2,1)S(1)}, bf16[2,128,256]{2,1,0:T(8,128)(2,1)S(1)}, u32[]{:S(2)}, u32[]{:S(2)}) collective-permute-start(bf16[2,128,256]{2,1,0:T(8,128)(2,1)S(1)} %shard_map.82.refs_3_), channel_id=1, source_target_pairs={{0,2},{1,3},{2,0},{3,1},{4,6},{5,7},{6,4},{7,5},{8,10},{9,11},{10,... | collective-permute-start | bytes 393224 | tf_op jit(solution)/shard_map/ppermute | solution.py:215
  144.2 2.8 %collective-permute-done.28.refs_2_ = bf16[2,128,256]{2,1,0:T(8,128)(2,1)S(1)} collective-permute-done((bf16[2,128,256]{2,1,0:T(8,128)(2,1)S(1)}, bf16[2,128,256]{2,1,0:T(8,128)(2,1)S(1)}, u32[]{:S(2)}, u32[]{:S(2)}) %collective-permute-start.28) | collective-permute-done | bytes 131104 | tf_op jit(solution)/shard_map/ppermute | solution.py:215
  147.0 2.7 %collective-permute-done.30.refs_11_ = bf16[2,128,256]{2,1,0:T(8,128)(2,1)S(1)} collective-permute-done((bf16[2,128,256]{2,1,0:T(8,128)(2,1)S(1)}, bf16[2,128,256]{2,1,0:T(8,128)(2,1)S(1)}, u32[]{:S(2)}, u32[]{:S(2)}) %collective-permute-start.30) | collective-permute-done | bytes 131104 | tf_op jit(solution)/shard_map/ppermute | solution.py:215
  149.8 4.9 %shard_map.83 = (f32[128,1024]{1,0:T(8,128)S(1)}, f32[128,1024]{1,0:T(8,128)S(1)}, f32[128,1024]{1,0:T(8,128)S(1)}, f32[128,1024]{1,0:T(8,128)S(1)}) custom-call(s32[4]{0:T(128)S(1)} %pad_add_fusion.where_ref, bf16[144,512]{1,0:T(8,128)(2,1)S(1)} %get-tuple-element.75.refs_0_.refs_1_, bf16[144,512]{1,0:T(8,128)(2,1)S(1)} %collective-permute-done.2.refs_0_.refs_1_, ...), custom_call_target="tpu_custom_call" | custom-call | flops 6000000000 | bytes 1 | tf_op jit(solution)/shard_map/pallas_call | solution.py:332
  162.4 4.5 %collective-permute-done.35 = bf16[2,128,512]{2,1,0:T(8,128)(2,1)S(1)} collective-permute-done((bf16[2,128,512]{2,1,0:T(8,128)(2,1)S(1)}, bf16[2,128,512]{2,1,0:T(8,128)(2,1)S(1)}, u32[]{:S(2)}, u32[]{:S(2)}) %collective-permute-start.35) | collective-permute-done | bytes 262176 | tf_op jit(solution)/shard_map/ppermute | solution.py:212
  171.6 3.2 %collective-permute-start.32 = (bf16[128,512]{1,0:T(8,128)(2,1)S(1)}, bf16[128,512]{1,0:T(8,128)(2,1)S(1)}, u32[]{:S(2)}, u32[]{:S(2)}) collective-permute-start(bf16[128,512]{1,0:T(8,128)(2,1)S(1)} %get-tuple-element.145), channel_id=1, source_target_pairs={{0,3},{1,0},{2,1},{3,2},{4,7},{5,4},{6,5},{7,6},{8,11},{9,8},{10,9... | collective-permute-start | bytes 393224 | tf_op jit(solution)/shard_map/ppermute | solution.py:215
  174.7 4.5 %collective-permute-done.36.refs_2_ = bf16[128,512]{1,0:T(8,128)(2,1)S(1)} collective-permute-done((bf16[128,512]{1,0:T(8,128)(2,1)S(1)}, bf16[128,512]{1,0:T(8,128)(2,1)S(1)}, u32[]{:S(2)}, u32[]{:S(2)}) %collective-permute-start.36) | collective-permute-done | bytes 131104 | tf_op jit(solution)/shard_map/ppermute | solution.py:215
  (119 shorter events, 65.7 us)
Async XLA Ops:
  11.9 12.8 %collective-permute-start.3 = (bf16[144,512]{1,0:T(8,128)(2,1)S(1)}, bf16[144,512]{1,0:T(8,128)(2,1)S(1)}, u32[]{:S(2)}, u32[]{:S(2)}) collective-permute-start(bf16[144,512]{1,0:T(8,128)(2,1)S(1)} %get-tuple-element.72), channel_id=1, source_target_pairs={{0,2},{1,3},{2,0},{3,1},{4,6},{5,7},{6,4},{7,5},{8,10},{9,11},{10,... | collective-permute-start | bytes 442376 | tf_op jit(solution)/shard_map/ppermute | solution.py:215
  13.0 26.1 %collective-permute-start.6 = (bf16[2,4,256,256]{3,2,1,0:T(8,128)(2,1)S(1)}, bf16[2,4,256,256]{3,2,1,0:T(8,128)(2,1)S(1)}, u32[]{:S(2)}, u32[]{:S(2)}) collective-permute-start(bf16[2,4,256,256]{3,2,1,0:T(8,128)(2,1)S(1)} %pad_maximum_fusion), channel_id=1, source_target_pairs={{0,16},{16,0},{8,24},{24,8},{1,17},{17,1},{9,25},{25,9},{2,18},{18... | collective-permute-start | bytes 3145736 | tf_op jit(solution)/shard_map/ppermute | solution.py:206
  24.7 14.3 %collective-permute-start.5 = (bf16[4,144,512]{2,1,0:T(8,128)(2,1)S(1)}, bf16[4,144,512]{2,1,0:T(8,128)(2,1)S(1)}, u32[]{:S(2)}, u32[]{:S(2)}) collective-permute-start(bf16[4,144,512]{2,1,0:T(8,128)(2,1)S(1)} %pad_maximum_fusion.3), channel_id=1, source_target_pairs={{0,4},{4,0},{1,5},{5,1},{2,6},{6,2},{3,7},{7,3},{8,12},{12,8},{9,1... | collective-permute-start | bytes 1769480 | tf_op jit(solution)/shard_map/ppermute | solution.py:212
  39.2 24.4 %collective-permute-start.11 = (bf16[4,256,768]{2,1,0:T(8,128)(2,1)S(1)}, bf16[4,256,768]{2,1,0:T(8,128)(2,1)S(1)}, u32[]{:S(2)}, u32[]{:S(2)}) collective-permute-start(bf16[4,256,768]{2,1,0:T(8,128)(2,1)S(1)} %copy-done.4), channel_id=1, source_target_pairs={{0,8},{8,0},{16,24},{24,16},{1,9},{9,1},{17,25},{25,17},{2,10},{10... | collective-permute-start | bytes 4718600 | tf_op jit(solution)/shard_map/ppermute | solution.py:209
  40.1 25.2 %collective-permute-start.7 = (bf16[2,4,256,256]{3,2,1,0:T(8,128)(2,1)S(1)}, bf16[2,4,256,256]{3,2,1,0:T(8,128)(2,1)S(1)}, u32[]{:S(2)}, u32[]{:S(2)}) collective-permute-start(bf16[2,4,256,256]{3,2,1,0:T(8,128)(2,1)S(1)} %pad_maximum_fusion.1), channel_id=1, source_target_pairs={{0,16},{16,0},{8,24},{24,8},{1,17},{17,1},{9,25},{25,9},{2,18},{18... | collective-permute-start | bytes 3145736 | tf_op jit(solution)/shard_map/ppermute | solution.py:206
  43.9 10.2 %collective-permute-start.9 = (bf16[2,128,512]{2,1,0:T(8,128)(2,1)S(1)}, bf16[2,128,512]{2,1,0:T(8,128)(2,1)S(1)}, u32[]{:S(2)}, u32[]{:S(2)}) collective-permute-start(bf16[2,128,512]{2,1,0:T(8,128)(2,1)S(1)} %shard_map.75), channel_id=1, source_target_pairs={{0,1},{1,2},{2,3},{3,0},{4,5},{5,6},{6,7},{7,4},{8,9},{9,10},{10,1... | collective-permute-start | bytes 786440 | tf_op jit(solution)/shard_map/ppermute | solution.py:215
  65.8 34.3 %collective-permute-start.12 = (bf16[2,4,256,256]{3,2,1,0:T(8,128)(2,1)S(1)}, bf16[2,4,256,256]{3,2,1,0:T(8,128)(2,1)S(1)}, u32[]{:S(2)}, u32[]{:S(2)}) collective-permute-start(bf16[2,4,256,256]{3,2,1,0:T(8,128)(2,1)S(1)} %pad_maximum_fusion.2), channel_id=1, source_target_pairs={{0,16},{16,0},{8,24},{24,8},{1,17},{17,1},{9,25},{25,9},{2,18},{18... | collective-permute-start | bytes 3145736 | tf_op jit(solution)/shard_map/ppermute | solution.py:206
  70.0 11.0 %collective-permute-start.14 = (bf16[2,128,512]{2,1,0:T(8,128)(2,1)S(1)}, bf16[2,128,512]{2,1,0:T(8,128)(2,1)S(1)}, u32[]{:S(2)}, u32[]{:S(2)}) collective-permute-start(bf16[2,128,512]{2,1,0:T(8,128)(2,1)S(1)} %shard_map.77), channel_id=1, source_target_pairs={{0,1},{1,2},{2,3},{3,0},{4,5},{5,6},{6,7},{7,4},{8,9},{9,10},{10,1... | collective-permute-start | bytes 786440 | tf_op jit(solution)/shard_map/ppermute | solution.py:215
  71.6 15.1 %collective-permute-start.16 = (bf16[2,128,512]{2,1,0:T(8,128)(2,1)S(1)}, bf16[2,128,512]{2,1,0:T(8,128)(2,1)S(1)}, u32[]{:S(2)}, u32[]{:S(2)}) collective-permute-start(bf16[2,128,512]{2,1,0:T(8,128)(2,1)S(1)} %add_convert_fusion.6), channel_id=1, source_target_pairs={{0,1},{1,2},{2,3},{3,0},{4,5},{5,6},{6,7},{7,4},{8,9},{9,10},{10,1... | collective-permute-start | bytes 786440 | tf_op jit(solution)/shard_map/ppermute | solution.py:215
  81.1 11.4 %collective-permute-start.15 = (bf16[2,128,512]{2,1,0:T(8,128)(2,1)S(1)}, bf16[2,128,512]{2,1,0:T(8,128)(2,1)S(1)}, u32[]{:S(2)}, u32[]{:S(2)}) collective-permute-start(bf16[2,128,512]{2,1,0:T(8,128)(2,1)S(1)} %add_convert_fusion.5), channel_id=1, source_target_pairs={{0,1},{1,2},{2,3},{3,0},{4,5},{5,6},{6,7},{7,4},{8,9},{9,10},{10,1... | collective-permute-start | bytes 786440 | tf_op jit(solution)/shard_map/ppermute | solution.py:215
  86.9 13.2 %collective-permute-start.18 = (bf16[2,128,256]{2,1,0:T(8,128)(2,1)S(1)}, bf16[2,128,256]{2,1,0:T(8,128)(2,1)S(1)}, u32[]{:S(2)}, u32[]{:S(2)}) collective-permute-start(bf16[2,128,256]{2,1,0:T(8,128)(2,1)S(1)} %shard_map.78.refs_4_), channel_id=1, source_target_pairs={{0,2},{1,3},{2,0},{3,1},{4,6},{5,7},{6,4},{7,5},{8,10},{9,11},{10,... | collective-permute-start | bytes 393224 | tf_op jit(solution)/shard_map/ppermute | solution.py:215
  88.1 12.0 %collective-permute-start.19 = (bf16[2,128,256]{2,1,0:T(8,128)(2,1)S(1)}, bf16[2,128,256]{2,1,0:T(8,128)(2,1)S(1)}, u32[]{:S(2)}, u32[]{:S(2)}) collective-permute-start(bf16[2,128,256]{2,1,0:T(8,128)(2,1)S(1)} %shard_map.78.refs_4_), channel_id=1, source_target_pairs={{0,3},{1,0},{2,1},{3,2},{4,7},{5,4},{6,5},{7,6},{8,11},{9,8},{10,9... | collective-permute-start | bytes 393224 | tf_op jit(solution)/shard_map/ppermute | solution.py:215
  100.1 38.4 %collective-permute-start.24 = (bf16[4,256,768]{2,1,0:T(8,128)(2,1)S(1)}, bf16[4,256,768]{2,1,0:T(8,128)(2,1)S(1)}, u32[]{:S(2)}, u32[]{:S(2)}) collective-permute-start(bf16[4,256,768]{2,1,0:T(8,128)(2,1)S(1)} %copy-done.4), channel_id=1, source_target_pairs={{0,16},{16,0},{8,24},{24,8},{1,17},{17,1},{9,25},{25,9},{2,18},{18... | collective-permute-start | bytes 4718600 | tf_op jit(solution)/shard_map/ppermute | solution.py:206
  104.8 11.0 %collective-permute-start.21 = (bf16[2,128,512]{2,1,0:T(8,128)(2,1)S(1)}, bf16[2,128,512]{2,1,0:T(8,128)(2,1)S(1)}, u32[]{:S(2)}, u32[]{:S(2)}) collective-permute-start(bf16[2,128,512]{2,1,0:T(8,128)(2,1)S(1)} %shard_map.80), channel_id=1, source_target_pairs={{0,1},{1,2},{2,3},{3,0},{4,5},{5,6},{6,7},{7,4},{8,9},{9,10},{10,1... | collective-permute-start | bytes 786440 | tf_op jit(solution)/shard_map/ppermute | solution.py:215
  108.1 13.3 %collective-permute-start.25 = (bf16[2,128,512]{2,1,0:T(8,128)(2,1)S(1)}, bf16[2,128,512]{2,1,0:T(8,128)(2,1)S(1)}, u32[]{:S(2)}, u32[]{:S(2)}) collective-permute-start(bf16[2,128,512]{2,1,0:T(8,128)(2,1)S(1)} %add_convert_fusion.4), channel_id=1, source_target_pairs={{0,1},{1,2},{2,3},{3,0},{4,5},{5,6},{6,7},{7,4},{8,9},{9,10},{10,1... | collective-permute-start | bytes 786440 | tf_op jit(solution)/shard_map/ppermute | solution.py:215
  115.9 11.2 %collective-permute-start.22 = (bf16[2,128,512]{2,1,0:T(8,128)(2,1)S(1)}, bf16[2,128,512]{2,1,0:T(8,128)(2,1)S(1)}, u32[]{:S(2)}, u32[]{:S(2)}) collective-permute-start(bf16[2,128,512]{2,1,0:T(8,128)(2,1)S(1)} %add_convert_fusion.3), channel_id=1, source_target_pairs={{0,1},{1,2},{2,3},{3,0},{4,5},{5,6},{6,7},{7,4},{8,9},{9,10},{10,1... | collective-permute-start | bytes 786440 | tf_op jit(solution)/shard_map/ppermute | solution.py:215
  127.1 11.4 %collective-permute-start.23 = (bf16[2,128,512]{2,1,0:T(8,128)(2,1)S(1)}, bf16[2,128,512]{2,1,0:T(8,128)(2,1)S(1)}, u32[]{:S(2)}, u32[]{:S(2)}) collective-permute-start(bf16[2,128,512]{2,1,0:T(8,128)(2,1)S(1)} %add_convert_fusion.2), channel_id=1, source_target_pairs={{0,1},{1,2},{2,3},{3,0},{4,5},{5,6},{6,7},{7,4},{8,9},{9,10},{10,1... | collective-permute-start | bytes 786440 | tf_op jit(solution)/shard_map/ppermute | solution.py:215
  129.0 9.4 %collective-permute-start.27 = (bf16[2,128,256]{2,1,0:T(8,128)(2,1)S(1)}, bf16[2,128,256]{2,1,0:T(8,128)(2,1)S(1)}, u32[]{:S(2)}, u32[]{:S(2)}) collective-permute-start(bf16[2,128,256]{2,1,0:T(8,128)(2,1)S(1)} %collective-permute-done.26.refs_9_), channel_id=1, source_target_pairs={{0,1},{1,2},{2,3},{3,0},{4,5},{5,6},{6,7},{7,4},{8,9},{9,10},{10,1... | collective-permute-start | bytes 393224 | tf_op jit(solution)/shard_map/ppermute | solution.py:215
  140.4 9.4 %collective-permute-start.30 = (bf16[2,128,256]{2,1,0:T(8,128)(2,1)S(1)}, bf16[2,128,256]{2,1,0:T(8,128)(2,1)S(1)}, u32[]{:S(2)}, u32[]{:S(2)}) collective-permute-start(bf16[2,128,256]{2,1,0:T(8,128)(2,1)S(1)} %collective-permute-done.27.refs_10_), channel_id=1, source_target_pairs={{0,1},{1,2},{2,3},{3,0},{4,5},{5,6},{6,7},{7,4},{8,9},{9,10},{10,1... | collective-permute-start | bytes 393224 | tf_op jit(solution)/shard_map/ppermute | solution.py:215
  140.4 14.5 %collective-permute-start.33 = (bf16[2,128,256]{2,1,0:T(8,128)(2,1)S(1)}, bf16[2,128,256]{2,1,0:T(8,128)(2,1)S(1)}, u32[]{:S(2)}, u32[]{:S(2)}) collective-permute-start(bf16[2,128,256]{2,1,0:T(8,128)(2,1)S(1)} %shard_map.82.refs_3_), channel_id=1, source_target_pairs={{0,2},{1,3},{2,0},{3,1},{4,6},{5,7},{6,4},{7,5},{8,10},{9,11},{10,... | collective-permute-start | bytes 393224 | tf_op jit(solution)/shard_map/ppermute | solution.py:215
  143.1 11.8 %collective-permute-start.34 = (bf16[2,128,256]{2,1,0:T(8,128)(2,1)S(1)}, bf16[2,128,256]{2,1,0:T(8,128)(2,1)S(1)}, u32[]{:S(2)}, u32[]{:S(2)}) collective-permute-start(bf16[2,128,256]{2,1,0:T(8,128)(2,1)S(1)} %shard_map.82.refs_3_), channel_id=1, source_target_pairs={{0,3},{1,0},{2,1},{3,2},{4,7},{5,4},{6,5},{7,6},{8,11},{9,8},{10,9... | collective-permute-start | bytes 393224 | tf_op jit(solution)/shard_map/ppermute | solution.py:215
  161.8 9.7 %collective-permute-start.31 = (bf16[2,128,512]{2,1,0:T(8,128)(2,1)S(1)}, bf16[2,128,512]{2,1,0:T(8,128)(2,1)S(1)}, u32[]{:S(2)}, u32[]{:S(2)}) collective-permute-start(bf16[2,128,512]{2,1,0:T(8,128)(2,1)S(1)} %get-tuple-element.122), channel_id=1, source_target_pairs={{0,4},{4,0},{1,5},{5,1},{2,6},{6,2},{3,7},{7,3},{8,12},{12,8},{9,1... | collective-permute-start | bytes 786440 | tf_op jit(solution)/shard_map/ppermute | solution.py:212
  166.9 12.3 %collective-permute-start.36 = (bf16[128,512]{1,0:T(8,128)(2,1)S(1)}, bf16[128,512]{1,0:T(8,128)(2,1)S(1)}, u32[]{:S(2)}, u32[]{:S(2)}) collective-permute-start(bf16[128,512]{1,0:T(8,128)(2,1)S(1)} %get-tuple-element.144), channel_id=1, source_target_pairs={{0,2},{1,3},{2,0},{3,1},{4,6},{5,7},{6,4},{7,5},{8,10},{9,11},{10,... | collective-permute-start | bytes 393224 | tf_op jit(solution)/shard_map/ppermute | solution.py:215
  169.3 9.9 %collective-permute-start.37 = (bf16[128,512]{1,0:T(8,128)(2,1)S(1)}, bf16[128,512]{1,0:T(8,128)(2,1)S(1)}, u32[]{:S(2)}, u32[]{:S(2)}) collective-permute-start(bf16[128,512]{1,0:T(8,128)(2,1)S(1)} %get-tuple-element.143), channel_id=1, source_target_pairs={{0,1},{1,2},{2,3},{3,0},{4,5},{5,6},{6,7},{7,4},{8,9},{9,10},{10,1... | collective-permute-start | bytes 393224 | tf_op jit(solution)/shard_map/ppermute | solution.py:215
  (26 other events, 235.7 us)

commit v5 on v4

--- a/solution.py
+++ b/solution.py
@@ -225,14 +225,10 @@
         compiler_params=PARAMS,
         cost_estimate=LIGHT,
     )(where, tokens, slots, gate_prob.T)
-    def cross_x(v, k):
-        pairs = [(t * n_dp + i, (1 - t) * n_dp + (i + k) % n_dp) for t in range(2) for i in range(n_dp)]
-        return lax.ppermute(v, ("tensor", "dp"), pairs)
-
     gate_core, up_core = swap_core(gate_weight), swap_core(up_weight)
     gate_core, up_core, *send = lax.optimization_barrier((gate_core, up_core, *send))
     own = [send[0]] + [shift(send[k], k) for k in range(1, n_dp)]
-    stacked = swap_x(jnp.stack(own))
+    stacked = swap_x(jnp.stack([v[:rows] for v in own]))
     far = [stacked[k] for k in range(n_dp)]
 
     blocks = share // UNIT
@@ -325,7 +321,7 @@
     down_yc = swap_core(down_y)
     hidden2 = hidden_of([parts2], [got2])
     hidden2 = gather_dp(hidden2)
-    hidden2[1], down_core, down_yc = bar((hidden2[1], down_core, down_yc))
+    hidden2[1], down_yc = bar((hidden2[1], down_yc))
 
     down_weights = (down_weight, down_core, down_y, down_yc)
     late = 2 * UNIT

time: 182 us -> 183 us (level)
  waiting for transfers between devices: 98.8 us -> 105 us
  starting transfers between devices: 47.3 us -> 42.6 us
    ppermute x24, waiting for transfers between devices: 76.9 us -> 82 us  [shift(): return lax.ppermute(v, 'dp', [(i, (i + k) % n_dp) for i in range(n_dp)])]
    ppermute x24, starting transfers between devices: 36.1 us -> 31.6 us  [shift(): return lax.ppermute(v, 'dp', [(i, (i + k) % n_dp) for i in range(n_dp)])]
    unnamed x24 -> x26, local copies, waits for them, and re-layouts: 2.51 us -> 0.07 us
  transfers between devices with their start and end apart: 38 -> 38, of which waited for: 28 -> 27; matrix products, arithmetic and copies ran while one was open for 2% -> 3% of each run, Pallas kernels for 13% -> 13%
where the time goes in v5:
time: 183 us; the launch traced here: 182 us
  waiting for transfers between devices  105 us (57%)
  starting transfers between devices  42.6 us (23%)
  Pallas kernels  28.5 us (16%)
  local copies, waits for them, and re-layouts  2.7 us (1%)
  other arithmetic  2.36 us (1%)
    ppermute x24, waiting for transfers between devices, shift(): return lax.ppermute(v, 'dp', [(i, (i + k) % n_dp) for i in range(n_dp)])  82 us
    ppermute x24, starting transfers between devices, shift(): return lax.ppermute(v, 'dp', [(i, (i + k) % n_dp) for i in range(n_dp)])  31.6 us
    ppermute x3, waiting for transfers between devices, swap_x(): return lax.ppermute(v, 'tensor', [(0, 1), (1, 0)])  17.5 us
    pallas_call x6, Pallas kernels, call(): pl.pallas_call(functools.partial(gate_up_kernel, n), grid=(1,), out_shape...  16 us
    ppermute x4, starting transfers between devices, swap_y(): return lax.ppermute(v, 'expert', [(0, 2), (2, 0), (1, 3), (3, 1)])  6.11 us
    pallas_call x2, Pallas kernels, down(): pl.pallas_call(functools.partial(down_kernel, n, 1, False), grid=(1,), ou...  5.25 us
    pallas_call x1, Pallas kernels, stationary_plan(): pl.pallas_call(functools.partial(down_kernel, n_dp, 2, True), grid=(1,),...  4.91 us
    ppermute x3, starting transfers between devices, swap_x(): return lax.ppermute(v, 'tensor', [(0, 1), (1, 0)])  3.71 us
  transfers between devices with their start and end apart: 38, of which 27 were waited for; matrix products, arithmetic and copies ran while one was open for 3% of the time, Pallas kernels for 13%

profile of v5, /device:TPU:0, one launch (start us, length us, event | category | flops | bytes accessed | tf_op | source)
XLA Modules:
  0.0 182.1 jit_solution(15601362745441884715)
XLA Ops:
  3.9 3.0 %collective-permute-start.6 = (bf16[2,4,256,256]{3,2,1,0:T(8,128)(2,1)}, bf16[2,4,256,256]{3,2,1,0:T(8,128)(2,1)S(1)}, u32[]{:S(2)}, u32[]{:S(2)}) collective-permute-start(bf16[2,4,256,256]{3,2,1,0:T(8,128)(2,1)} %pad_maximum_fusion), channel_id=1, source_target_pairs={{0,16},{16,0},{8,24},{24,8},{1,17},{17,1},{9,25},{25,9},{2,18},{18... | collective-permute-start | bytes 3145736 | tf_op jit(solution)/shard_map/ppermute | solution.py:206
  13.0 3.9 %collective-permute-done.2.refs_0_.refs_1_ = bf16[144,512]{1,0:T(8,128)(2,1)S(1)} collective-permute-done((bf16[144,512]{1,0:T(8,128)(2,1)S(1)}, bf16[144,512]{1,0:T(8,128)(2,1)S(1)}, u32[]{:S(2)}, u32[]{:S(2)}) %collective-permute-start.2) | collective-permute-done | bytes 147488 | tf_op jit(solution)/shard_map/ppermute | solution.py:215
  18.3 6.9 %collective-permute-done.3.refs_1_.refs_2_.refs_0_ = bf16[144,512]{1,0:T(8,128)(2,1)S(1)} collective-permute-done((bf16[144,512]{1,0:T(8,128)(2,1)S(1)}, bf16[144,512]{1,0:T(8,128)(2,1)S(1)}, u32[]{:S(2)}, u32[]{:S(2)}) %collective-permute-start.3) | collective-permute-done | bytes 147488 | tf_op jit(solution)/shard_map/ppermute | solution.py:215
  26.9 12.4 %collective-permute-done.5 = bf16[4,128,512]{2,1,0:T(8,128)(2,1)S(1)} collective-permute-done((bf16[4,128,512]{2,1,0:T(8,128)(2,1)S(1)}, bf16[4,128,512]{2,1,0:T(8,128)(2,1)S(1)}, u32[]{:S(2)}, u32[]{:S(2)}) %collective-permute-start.5) | collective-permute-done | bytes 524320 | tf_op jit(solution)/shard_map/ppermute | solution.py:212
  44.1 3.3 %shard_map.74 = (bf16[2,128,512]{2,1,0:T(8,128)(2,1)S(1)}, bf16[2,128,512]{2,1,0:T(8,128)(2,1)S(1)}, bf16[2,128,512]{2,1,0:T(8,128)(2,1)S(1)}) custom-call(s32[4]{0:T(128)S(1)} %pad_add_fusion.where_ref, bf16[144,512]{1,0:T(8,128)(2,1)S(1)} %get-tuple-element.74.refs_0_.refs_1_, bf16[144,512]{1,0:T(8,128)(2,1)S(1)} %collective-permute-done.3.refs_1_.refs_2_.refs_0_, ...), custom_call_target="tpu_custom_call" | custom-call | flops 1 | bytes 1 | tf_op jit(solution)/shard_map/pallas_call | solution.py:249
  47.4 6.8 %collective-permute-done.9 = bf16[2,128,512]{2,1,0:T(8,128)(2,1)S(1)} collective-permute-done((bf16[2,128,512]{2,1,0:T(8,128)(2,1)S(1)}, bf16[2,128,512]{2,1,0:T(8,128)(2,1)S(1)}, u32[]{:S(2)}, u32[]{:S(2)}) %collective-permute-start.9) | collective-permute-done | bytes 262176 | tf_op jit(solution)/shard_map/ppermute | solution.py:215
  54.4 9.3 %collective-permute-done.10 = bf16[2,128,512]{2,1,0:T(8,128)(2,1)S(1)} collective-permute-done((bf16[2,128,512]{2,1,0:T(8,128)(2,1)S(1)}, bf16[2,128,512]{2,1,0:T(8,128)(2,1)S(1)}, u32[]{:S(2)}, u32[]{:S(2)}) %collective-permute-start.10) | collective-permute-done | bytes 262176 | tf_op jit(solution)/shard_map/ppermute | solution.py:215
  70.4 3.3 %shard_map.76 = (bf16[2,128,512]{2,1,0:T(8,128)(2,1)S(1)}, bf16[2,128,512]{2,1,0:T(8,128)(2,1)S(1)}, bf16[2,128,512]{2,1,0:T(8,128)(2,1)S(1)}) custom-call(s32[4]{0:T(128)S(1)} %pad_add_fusion.where_ref, bf16[144,512]{1,0:T(8,128)(2,1)S(1)} %get-tuple-element.74.refs_0_.refs_1_, bf16[144,512]{1,0:T(8,128)(2,1)S(1)} %collective-permute-done.3.refs_1_.refs_2_.refs_0_, ...), custom_call_target="tpu_custom_call" | custom-call | flops 1 | bytes 1 | tf_op jit(solution)/shard_map/pallas_call | solution.py:249
  73.7 7.6 %collective-permute-done.14 = bf16[2,128,512]{2,1,0:T(8,128)(2,1)S(1)} collective-permute-done((bf16[2,128,512]{2,1,0:T(8,128)(2,1)S(1)}, bf16[2,128,512]{2,1,0:T(8,128)(2,1)S(1)}, u32[]{:S(2)}, u32[]{:S(2)}) %collective-permute-start.14) | collective-permute-done | bytes 262176 | tf_op jit(solution)/shard_map/ppermute | solution.py:215
  81.4 5.5 %collective-permute-done.16.refs_1_ = bf16[2,128,512]{2,1,0:T(8,128)(2,1)S(1)} collective-permute-done((bf16[2,128,512]{2,1,0:T(8,128)(2,1)S(1)}, bf16[2,128,512]{2,1,0:T(8,128)(2,1)S(1)}, u32[]{:S(2)}, u32[]{:S(2)}) %collective-permute-start.16) | collective-permute-done | bytes 262176 | tf_op jit(solution)/shard_map/ppermute | solution.py:215
  87.2 3.7 %collective-permute-start.19 = (bf16[2,128,256]{2,1,0:T(8,128)(2,1)S(1)}, bf16[2,128,256]{2,1,0:T(8,128)(2,1)S(1)}, u32[]{:S(2)}, u32[]{:S(2)}) collective-permute-start(bf16[2,128,256]{2,1,0:T(8,128)(2,1)S(1)} %shard_map.78.refs_4_), channel_id=1, source_target_pairs={{0,3},{1,0},{2,1},{3,2},{4,7},{5,4},{6,5},{7,6},{8,11},{9,8},{10,9... | collective-permute-start | bytes 393224 | tf_op jit(solution)/shard_map/ppermute | solution.py:215
  95.5 4.8 %collective-permute-done.18.refs_6_ = bf16[2,128,256]{2,1,0:T(8,128)(2,1)S(1)} collective-permute-done((bf16[2,128,256]{2,1,0:T(8,128)(2,1)S(1)}, bf16[2,128,256]{2,1,0:T(8,128)(2,1)S(1)}, u32[]{:S(2)}, u32[]{:S(2)}) %collective-permute-start.18) | collective-permute-done | bytes 131104 | tf_op jit(solution)/shard_map/ppermute | solution.py:215
  105.0 3.3 %collective-permute-start.21 = (bf16[2,128,512]{2,1,0:T(8,128)(2,1)S(1)}, bf16[2,128,512]{2,1,0:T(8,128)(2,1)S(1)}, u32[]{:S(2)}, u32[]{:S(2)}) collective-permute-start(bf16[2,128,512]{2,1,0:T(8,128)(2,1)S(1)} %shard_map.80), channel_id=1, source_target_pairs={{0,1},{1,2},{2,3},{3,0},{4,5},{5,6},{6,7},{7,4},{8,9},{9,10},{10,1... | collective-permute-start | bytes 786440 | tf_op jit(solution)/shard_map/ppermute | solution.py:215
  108.4 3.3 %shard_map.79 = (bf16[2,128,512]{2,1,0:T(8,128)(2,1)S(1)}, bf16[2,128,512]{2,1,0:T(8,128)(2,1)S(1)}, bf16[2,128,512]{2,1,0:T(8,128)(2,1)S(1)}) custom-call(s32[4]{0:T(128)S(1)} %pad_add_fusion.where_ref, bf16[144,512]{1,0:T(8,128)(2,1)S(1)} %get-tuple-element.74.refs_0_.refs_1_, bf16[144,512]{1,0:T(8,128)(2,1)S(1)} %collective-permute-done.3.refs_1_.refs_2_.refs_0_, ...), custom_call_target="tpu_custom_call" | custom-call | flops 1 | bytes 1 | tf_op jit(solution)/shard_map/pallas_call | solution.py:249
  111.7 4.3 %collective-permute-done.21 = bf16[2,128,512]{2,1,0:T(8,128)(2,1)S(1)} collective-permute-done((bf16[2,128,512]{2,1,0:T(8,128)(2,1)S(1)}, bf16[2,128,512]{2,1,0:T(8,128)(2,1)S(1)}, u32[]{:S(2)}, u32[]{:S(2)}) %collective-permute-start.21) | collective-permute-done | bytes 262176 | tf_op jit(solution)/shard_map/ppermute | solution.py:215
  117.6 4.0 %collective-permute-done.25.refs_1_ = bf16[2,128,512]{2,1,0:T(8,128)(2,1)S(1)} collective-permute-done((bf16[2,128,512]{2,1,0:T(8,128)(2,1)S(1)}, bf16[2,128,512]{2,1,0:T(8,128)(2,1)S(1)}, u32[]{:S(2)}, u32[]{:S(2)}) %collective-permute-start.25) | collective-permute-done | bytes 262176 | tf_op jit(solution)/shard_map/ppermute | solution.py:215
  123.5 3.8 %collective-permute-done.22 = bf16[2,128,512]{2,1,0:T(8,128)(2,1)S(1)} collective-permute-done((bf16[2,128,512]{2,1,0:T(8,128)(2,1)S(1)}, bf16[2,128,512]{2,1,0:T(8,128)(2,1)S(1)}, u32[]{:S(2)}, u32[]{:S(2)}) %collective-permute-start.22) | collective-permute-done | bytes 262176 | tf_op jit(solution)/shard_map/ppermute | solution.py:215
  131.4 7.2 %collective-permute-done.27.refs_10_ = bf16[2,128,256]{2,1,0:T(8,128)(2,1)S(1)} collective-permute-done((bf16[2,128,256]{2,1,0:T(8,128)(2,1)S(1)}, bf16[2,128,256]{2,1,0:T(8,128)(2,1)S(1)}, u32[]{:S(2)}, u32[]{:S(2)}) %collective-permute-start.27) | collective-permute-done | bytes 131104 | tf_op jit(solution)/shard_map/ppermute | solution.py:215
  144.4 2.8 %collective-permute-done.28.refs_2_ = bf16[2,128,256]{2,1,0:T(8,128)(2,1)S(1)} collective-permute-done((bf16[2,128,256]{2,1,0:T(8,128)(2,1)S(1)}, bf16[2,128,256]{2,1,0:T(8,128)(2,1)S(1)}, u32[]{:S(2)}, u32[]{:S(2)}) %collective-permute-start.28) | collective-permute-done | bytes 131104 | tf_op jit(solution)/shard_map/ppermute | solution.py:215
  147.3 2.7 %collective-permute-done.30.refs_11_ = bf16[2,128,256]{2,1,0:T(8,128)(2,1)S(1)} collective-permute-done((bf16[2,128,256]{2,1,0:T(8,128)(2,1)S(1)}, bf16[2,128,256]{2,1,0:T(8,128)(2,1)S(1)}, u32[]{:S(2)}, u32[]{:S(2)}) %collective-permute-start.30) | collective-permute-done | bytes 131104 | tf_op jit(solution)/shard_map/ppermute | solution.py:215
  150.0 4.9 %shard_map.83 = (f32[128,1024]{1,0:T(8,128)S(1)}, f32[128,1024]{1,0:T(8,128)S(1)}, f32[128,1024]{1,0:T(8,128)S(1)}, f32[128,1024]{1,0:T(8,128)S(1)}) custom-call(s32[4]{0:T(128)S(1)} %pad_add_fusion.where_ref, bf16[144,512]{1,0:T(8,128)(2,1)S(1)} %get-tuple-element.74.refs_0_.refs_1_, bf16[144,512]{1,0:T(8,128)(2,1)S(1)} %collective-permute-done.2.refs_0_.refs_1_, ...), custom_call_target="tpu_custom_call" | custom-call | flops 6000000000 | bytes 1 | tf_op jit(solution)/shard_map/pallas_call | solution.py:328
  162.6 4.5 %collective-permute-done.35 = bf16[2,128,512]{2,1,0:T(8,128)(2,1)S(1)} collective-permute-done((bf16[2,128,512]{2,1,0:T(8,128)(2,1)S(1)}, bf16[2,128,512]{2,1,0:T(8,128)(2,1)S(1)}, u32[]{:S(2)}, u32[]{:S(2)}) %collective-permute-start.35) | collective-permute-done | bytes 262176 | tf_op jit(solution)/shard_map/ppermute | solution.py:212
  171.8 3.1 %collective-permute-start.32 = (bf16[128,512]{1,0:T(8,128)(2,1)S(1)}, bf16[128,512]{1,0:T(8,128)(2,1)S(1)}, u32[]{:S(2)}, u32[]{:S(2)}) collective-permute-start(bf16[128,512]{1,0:T(8,128)(2,1)S(1)} %get-tuple-element.143), channel_id=1, source_target_pairs={{0,3},{1,0},{2,1},{3,2},{4,7},{5,4},{6,5},{7,6},{8,11},{9,8},{10,9... | collective-permute-start | bytes 393224 | tf_op jit(solution)/shard_map/ppermute | solution.py:215
  174.9 4.5 %collective-permute-done.36.refs_2_ = bf16[128,512]{1,0:T(8,128)(2,1)S(1)} collective-permute-done((bf16[128,512]{1,0:T(8,128)(2,1)S(1)}, bf16[128,512]{1,0:T(8,128)(2,1)S(1)}, u32[]{:S(2)}, u32[]{:S(2)}) %collective-permute-start.36) | collective-permute-done | bytes 131104 | tf_op jit(solution)/shard_map/ppermute | solution.py:215
  (125 shorter events, 62.0 us)
Async XLA Ops:
  3.9 35.4 %collective-permute-start.6 = (bf16[2,4,256,256]{3,2,1,0:T(8,128)(2,1)}, bf16[2,4,256,256]{3,2,1,0:T(8,128)(2,1)S(1)}, u32[]{:S(2)}, u32[]{:S(2)}) collective-permute-start(bf16[2,4,256,256]{3,2,1,0:T(8,128)(2,1)} %pad_maximum_fusion), channel_id=1, source_target_pairs={{0,16},{16,0},{8,24},{24,8},{1,17},{17,1},{9,25},{25,9},{2,18},{18... | collective-permute-start | bytes 3145736 | tf_op jit(solution)/shard_map/ppermute | solution.py:206
  12.2 13.0 %collective-permute-start.3 = (bf16[144,512]{1,0:T(8,128)(2,1)S(1)}, bf16[144,512]{1,0:T(8,128)(2,1)S(1)}, u32[]{:S(2)}, u32[]{:S(2)}) collective-permute-start(bf16[144,512]{1,0:T(8,128)(2,1)S(1)} %get-tuple-element.71), channel_id=1, source_target_pairs={{0,2},{1,3},{2,0},{3,1},{4,6},{5,7},{6,4},{7,5},{8,10},{9,11},{10,... | collective-permute-start | bytes 442376 | tf_op jit(solution)/shard_map/ppermute | solution.py:215
  25.3 13.9 %collective-permute-start.5 = (bf16[4,128,512]{2,1,0:T(8,128)(2,1)S(1)}, bf16[4,128,512]{2,1,0:T(8,128)(2,1)S(1)}, u32[]{:S(2)}, u32[]{:S(2)}) collective-permute-start(bf16[4,128,512]{2,1,0:T(8,128)(2,1)S(1)} %pad_maximum_fusion.3), channel_id=1, source_target_pairs={{0,4},{4,0},{1,5},{5,1},{2,6},{6,2},{3,7},{7,3},{8,12},{12,8},{9,1... | collective-permute-start | bytes 1572872 | tf_op jit(solution)/shard_map/ppermute | solution.py:212
  39.4 24.4 %collective-permute-start.11 = (bf16[4,256,768]{2,1,0:T(8,128)(2,1)S(1)}, bf16[4,256,768]{2,1,0:T(8,128)(2,1)S(1)}, u32[]{:S(2)}, u32[]{:S(2)}) collective-permute-start(bf16[4,256,768]{2,1,0:T(8,128)(2,1)S(1)} %copy-done.4), channel_id=1, source_target_pairs={{0,8},{8,0},{16,24},{24,16},{1,9},{9,1},{17,25},{25,17},{2,10},{10... | collective-permute-start | bytes 4718600 | tf_op jit(solution)/shard_map/ppermute | solution.py:209
  40.3 25.2 %collective-permute-start.7 = (bf16[2,4,256,256]{3,2,1,0:T(8,128)(2,1)S(1)}, bf16[2,4,256,256]{3,2,1,0:T(8,128)(2,1)S(1)}, u32[]{:S(2)}, u32[]{:S(2)}) collective-permute-start(bf16[2,4,256,256]{3,2,1,0:T(8,128)(2,1)S(1)} %pad_maximum_fusion.1), channel_id=1, source_target_pairs={{0,16},{16,0},{8,24},{24,8},{1,17},{17,1},{9,25},{25,9},{2,18},{18... | collective-permute-start | bytes 3145736 | tf_op jit(solution)/shard_map/ppermute | solution.py:206
  44.1 10.2 %collective-permute-start.9 = (bf16[2,128,512]{2,1,0:T(8,128)(2,1)S(1)}, bf16[2,128,512]{2,1,0:T(8,128)(2,1)S(1)}, u32[]{:S(2)}, u32[]{:S(2)}) collective-permute-start(bf16[2,128,512]{2,1,0:T(8,128)(2,1)S(1)} %shard_map.75), channel_id=1, source_target_pairs={{0,1},{1,2},{2,3},{3,0},{4,5},{5,6},{6,7},{7,4},{8,9},{9,10},{10,1... | collective-permute-start | bytes 786440 | tf_op jit(solution)/shard_map/ppermute | solution.py:215
  66.0 34.3 %collective-permute-start.12 = (bf16[2,4,256,256]{3,2,1,0:T(8,128)(2,1)S(1)}, bf16[2,4,256,256]{3,2,1,0:T(8,128)(2,1)S(1)}, u32[]{:S(2)}, u32[]{:S(2)}) collective-permute-start(bf16[2,4,256,256]{3,2,1,0:T(8,128)(2,1)S(1)} %pad_maximum_fusion.2), channel_id=1, source_target_pairs={{0,16},{16,0},{8,24},{24,8},{1,17},{17,1},{9,25},{25,9},{2,18},{18... | collective-permute-start | bytes 3145736 | tf_op jit(solution)/shard_map/ppermute | solution.py:206
  70.3 11.0 %collective-permute-start.14 = (bf16[2,128,512]{2,1,0:T(8,128)(2,1)S(1)}, bf16[2,128,512]{2,1,0:T(8,128)(2,1)S(1)}, u32[]{:S(2)}, u32[]{:S(2)}) collective-permute-start(bf16[2,128,512]{2,1,0:T(8,128)(2,1)S(1)} %shard_map.77), channel_id=1, source_target_pairs={{0,1},{1,2},{2,3},{3,0},{4,5},{5,6},{6,7},{7,4},{8,9},{9,10},{10,1... | collective-permute-start | bytes 786440 | tf_op jit(solution)/shard_map/ppermute | solution.py:215
  70.3 16.6 %collective-permute-start.16 = (bf16[2,128,512]{2,1,0:T(8,128)(2,1)S(1)}, bf16[2,128,512]{2,1,0:T(8,128)(2,1)S(1)}, u32[]{:S(2)}, u32[]{:S(2)}) collective-permute-start(bf16[2,128,512]{2,1,0:T(8,128)(2,1)S(1)} %add_convert_fusion.6), channel_id=1, source_target_pairs={{0,1},{1,2},{2,3},{3,0},{4,5},{5,6},{6,7},{7,4},{8,9},{9,10},{10,1... | collective-permute-start | bytes 786440 | tf_op jit(solution)/shard_map/ppermute | solution.py:215
  81.3 11.4 %collective-permute-start.15 = (bf16[2,128,512]{2,1,0:T(8,128)(2,1)S(1)}, bf16[2,128,512]{2,1,0:T(8,128)(2,1)S(1)}, u32[]{:S(2)}, u32[]{:S(2)}) collective-permute-start(bf16[2,128,512]{2,1,0:T(8,128)(2,1)S(1)} %add_convert_fusion.5), channel_id=1, source_target_pairs={{0,1},{1,2},{2,3},{3,0},{4,5},{5,6},{6,7},{7,4},{8,9},{9,10},{10,1... | collective-permute-start | bytes 786440 | tf_op jit(solution)/shard_map/ppermute | solution.py:215
  87.1 13.2 %collective-permute-start.18 = (bf16[2,128,256]{2,1,0:T(8,128)(2,1)S(1)}, bf16[2,128,256]{2,1,0:T(8,128)(2,1)S(1)}, u32[]{:S(2)}, u32[]{:S(2)}) collective-permute-start(bf16[2,128,256]{2,1,0:T(8,128)(2,1)S(1)} %shard_map.78.refs_4_), channel_id=1, source_target_pairs={{0,2},{1,3},{2,0},{3,1},{4,6},{5,7},{6,4},{7,5},{8,10},{9,11},{10,... | collective-permute-start | bytes 393224 | tf_op jit(solution)/shard_map/ppermute | solution.py:215
  87.2 13.1 %collective-permute-start.19 = (bf16[2,128,256]{2,1,0:T(8,128)(2,1)S(1)}, bf16[2,128,256]{2,1,0:T(8,128)(2,1)S(1)}, u32[]{:S(2)}, u32[]{:S(2)}) collective-permute-start(bf16[2,128,256]{2,1,0:T(8,128)(2,1)S(1)} %shard_map.78.refs_4_), channel_id=1, source_target_pairs={{0,3},{1,0},{2,1},{3,2},{4,7},{5,4},{6,5},{7,6},{8,11},{9,8},{10,9... | collective-permute-start | bytes 393224 | tf_op jit(solution)/shard_map/ppermute | solution.py:215
  100.3 38.4 %collective-permute-start.24 = (bf16[4,256,768]{2,1,0:T(8,128)(2,1)S(1)}, bf16[4,256,768]{2,1,0:T(8,128)(2,1)S(1)}, u32[]{:S(2)}, u32[]{:S(2)}) collective-permute-start(bf16[4,256,768]{2,1,0:T(8,128)(2,1)S(1)} %copy-done.4), channel_id=1, source_target_pairs={{0,16},{16,0},{8,24},{24,8},{1,17},{17,1},{9,25},{25,9},{2,18},{18... | collective-permute-start | bytes 4718600 | tf_op jit(solution)/shard_map/ppermute | solution.py:206
  105.0 11.0 %collective-permute-start.21 = (bf16[2,128,512]{2,1,0:T(8,128)(2,1)S(1)}, bf16[2,128,512]{2,1,0:T(8,128)(2,1)S(1)}, u32[]{:S(2)}, u32[]{:S(2)}) collective-permute-start(bf16[2,128,512]{2,1,0:T(8,128)(2,1)S(1)} %shard_map.80), channel_id=1, source_target_pairs={{0,1},{1,2},{2,3},{3,0},{4,5},{5,6},{6,7},{7,4},{8,9},{9,10},{10,1... | collective-permute-start | bytes 786440 | tf_op jit(solution)/shard_map/ppermute | solution.py:215
  108.3 13.3 %collective-permute-start.25 = (bf16[2,128,512]{2,1,0:T(8,128)(2,1)S(1)}, bf16[2,128,512]{2,1,0:T(8,128)(2,1)S(1)}, u32[]{:S(2)}, u32[]{:S(2)}) collective-permute-start(bf16[2,128,512]{2,1,0:T(8,128)(2,1)S(1)} %add_convert_fusion.4), channel_id=1, source_target_pairs={{0,1},{1,2},{2,3},{3,0},{4,5},{5,6},{6,7},{7,4},{8,9},{9,10},{10,1... | collective-permute-start | bytes 786440 | tf_op jit(solution)/shard_map/ppermute | solution.py:215
  116.1 11.2 %collective-permute-start.22 = (bf16[2,128,512]{2,1,0:T(8,128)(2,1)S(1)}, bf16[2,128,512]{2,1,0:T(8,128)(2,1)S(1)}, u32[]{:S(2)}, u32[]{:S(2)}) collective-permute-start(bf16[2,128,512]{2,1,0:T(8,128)(2,1)S(1)} %add_convert_fusion.3), channel_id=1, source_target_pairs={{0,1},{1,2},{2,3},{3,0},{4,5},{5,6},{6,7},{7,4},{8,9},{9,10},{10,1... | collective-permute-start | bytes 786440 | tf_op jit(solution)/shard_map/ppermute | solution.py:215
  127.3 11.4 %collective-permute-start.23 = (bf16[2,128,512]{2,1,0:T(8,128)(2,1)S(1)}, bf16[2,128,512]{2,1,0:T(8,128)(2,1)S(1)}, u32[]{:S(2)}, u32[]{:S(2)}) collective-permute-start(bf16[2,128,512]{2,1,0:T(8,128)(2,1)S(1)} %add_convert_fusion.2), channel_id=1, source_target_pairs={{0,1},{1,2},{2,3},{3,0},{4,5},{5,6},{6,7},{7,4},{8,9},{9,10},{10,1... | collective-permute-start | bytes 786440 | tf_op jit(solution)/shard_map/ppermute | solution.py:215
  129.2 9.4 %collective-permute-start.27 = (bf16[2,128,256]{2,1,0:T(8,128)(2,1)S(1)}, bf16[2,128,256]{2,1,0:T(8,128)(2,1)S(1)}, u32[]{:S(2)}, u32[]{:S(2)}) collective-permute-start(bf16[2,128,256]{2,1,0:T(8,128)(2,1)S(1)} %collective-permute-done.26.refs_9_), channel_id=1, source_target_pairs={{0,1},{1,2},{2,3},{3,0},{4,5},{5,6},{6,7},{7,4},{8,9},{9,10},{10,1... | collective-permute-start | bytes 393224 | tf_op jit(solution)/shard_map/ppermute | solution.py:215
  140.6 9.4 %collective-permute-start.30 = (bf16[2,128,256]{2,1,0:T(8,128)(2,1)S(1)}, bf16[2,128,256]{2,1,0:T(8,128)(2,1)S(1)}, u32[]{:S(2)}, u32[]{:S(2)}) collective-permute-start(bf16[2,128,256]{2,1,0:T(8,128)(2,1)S(1)} %collective-permute-done.27.refs_10_), channel_id=1, source_target_pairs={{0,1},{1,2},{2,3},{3,0},{4,5},{5,6},{6,7},{7,4},{8,9},{9,10},{10,1... | collective-permute-start | bytes 393224 | tf_op jit(solution)/shard_map/ppermute | solution.py:215
  140.6 14.5 %collective-permute-start.33 = (bf16[2,128,256]{2,1,0:T(8,128)(2,1)S(1)}, bf16[2,128,256]{2,1,0:T(8,128)(2,1)S(1)}, u32[]{:S(2)}, u32[]{:S(2)}) collective-permute-start(bf16[2,128,256]{2,1,0:T(8,128)(2,1)S(1)} %shard_map.82.refs_3_), channel_id=1, source_target_pairs={{0,2},{1,3},{2,0},{3,1},{4,6},{5,7},{6,4},{7,5},{8,10},{9,11},{10,... | collective-permute-start | bytes 393224 | tf_op jit(solution)/shard_map/ppermute | solution.py:215
  143.4 11.8 %collective-permute-start.34 = (bf16[2,128,256]{2,1,0:T(8,128)(2,1)S(1)}, bf16[2,128,256]{2,1,0:T(8,128)(2,1)S(1)}, u32[]{:S(2)}, u32[]{:S(2)}) collective-permute-start(bf16[2,128,256]{2,1,0:T(8,128)(2,1)S(1)} %shard_map.82.refs_3_), channel_id=1, source_target_pairs={{0,3},{1,0},{2,1},{3,2},{4,7},{5,4},{6,5},{7,6},{8,11},{9,8},{10,9... | collective-permute-start | bytes 393224 | tf_op jit(solution)/shard_map/ppermute | solution.py:215
  162.0 9.7 %collective-permute-start.31 = (bf16[2,128,512]{2,1,0:T(8,128)(2,1)S(1)}, bf16[2,128,512]{2,1,0:T(8,128)(2,1)S(1)}, u32[]{:S(2)}, u32[]{:S(2)}) collective-permute-start(bf16[2,128,512]{2,1,0:T(8,128)(2,1)S(1)} %get-tuple-element.120), channel_id=1, source_target_pairs={{0,4},{4,0},{1,5},{5,1},{2,6},{6,2},{3,7},{7,3},{8,12},{12,8},{9,1... | collective-permute-start | bytes 786440 | tf_op jit(solution)/shard_map/ppermute | solution.py:212
  167.2 12.3 %collective-permute-start.36 = (bf16[128,512]{1,0:T(8,128)(2,1)S(1)}, bf16[128,512]{1,0:T(8,128)(2,1)S(1)}, u32[]{:S(2)}, u32[]{:S(2)}) collective-permute-start(bf16[128,512]{1,0:T(8,128)(2,1)S(1)} %get-tuple-element.142), channel_id=1, source_target_pairs={{0,2},{1,3},{2,0},{3,1},{4,6},{5,7},{6,4},{7,5},{8,10},{9,11},{10,... | collective-permute-start | bytes 393224 | tf_op jit(solution)/shard_map/ppermute | solution.py:215
  169.5 9.9 %collective-permute-start.37 = (bf16[128,512]{1,0:T(8,128)(2,1)S(1)}, bf16[128,512]{1,0:T(8,128)(2,1)S(1)}, u32[]{:S(2)}, u32[]{:S(2)}) collective-permute-start(bf16[128,512]{1,0:T(8,128)(2,1)S(1)} %get-tuple-element.141), channel_id=1, source_target_pairs={{0,1},{1,2},{2,3},{3,0},{4,5},{5,6},{6,7},{7,4},{8,9},{9,10},{10,1... | collective-permute-start | bytes 393224 | tf_op jit(solution)/shard_map/ppermute | solution.py:215
  (27 other events, 304.9 us)
